TPU v7x, 32 devices: a whole 2x2x4 slice. The times are simulated.
32 devices in a mesh: tok: 8 (over y, x, core), rep: 4 (over z).
Axes of the slice: x: 2, y: 2, z: 4, core: 2. Of those that a mesh axis runs over, the one named last changes fastest.
Arguments:
- tokens: bfloat16 [2, 4, 4096, 1024], P(None, 'rep', 'tok'), may hold values from -6 to 6
- cotangent: bfloat16 [2, 4, 4096, 1024], P(None, 'rep', 'tok'), may hold values from -6 to 6
- init_num: float32 [2, 4, 2, 1024], P(None, 'rep', None, 'tok'), may hold values from -34 to 34, as said below
- init_den: float32 [2, 4, 2, 1024], P(None, 'rep', None, 'tok'), may hold values from 0.5 to 20
- prev_att: bfloat16 [2, 4, 2, 1024], P(None, 'rep'), may hold values from -5 to 5
- seg_doc: int32 [2, 4, 2], P(None, 'rep'), may hold values from 0 to 1, as said below
- w_kvr: float32 [1024, 3072], P(('tok', 'rep')), may hold values from -0.1875 to 0.1875
- w_out: float32 [1024, 1024], P(('tok', 'rep')), may hold values from -0.75 to 0.75
- f_kr: float32 [1024, 5120], P(('tok', 'rep')), may hold values from -0.1875 to 0.1875
- f_value: float32 [4096, 1024], P(('tok', 'rep')), may hold values from -0.09375 to 0.09375
- vectors: float32 [11, 1024], replicated, may hold values from -16 to 2
- m_kvr: float32 [1024, 3072], P(('tok', 'rep')), may hold values from -36.20387 to 36.20387
- v_kvr: float32 [1024, 3072], P(('tok', 'rep')), may hold values from 211.02592 to 845.4144
- m_out: float32 [1024, 1024], P(('tok', 'rep')), may hold values from -16.29174 to 16.29174
- v_out: float32 [1024, 1024], P(('tok', 'rep')), may hold values from 38.66624 to 154.99265
- m_fkr: float32 [1024, 5120], P(('tok', 'rep')), may hold values from -36.20387 to 36.20387
- v_fkr: float32 [1024, 5120], P(('tok', 'rep')), may hold values from 187.76064 to 750.3872
- m_fvalue: float32 [4096, 1024], P(('tok', 'rep')), may hold values from -72.40774 to 72.40774
- v_fvalue: float32 [4096, 1024], P(('tok', 'rep')), may hold values from 773.3248 to 3093.2993
- vec_m: float32 [11, 1024], P(None, ('tok', 'rep')), may hold values from -54.3058 to 54.3058
- vec_v: float32 [11, 1024], P(None, ('tok', 'rep')), may hold values from 429.2608 to 1723.5968
Outputs:
- mixed: bfloat16 [2, 4, 4096, 1024], P(None, 'rep', 'tok')
- token_grad: bfloat16 [2, 4, 4096, 1024], P(None, 'rep', 'tok')
- new_kvr: float32 [1024, 3072], P(('tok', 'rep'))
- mom_kvr: float32 [1024, 3072], P(('tok', 'rep'))
- sq_kvr: float32 [1024, 3072], P(('tok', 'rep'))
- new_out: float32 [1024, 1024], P(('tok', 'rep'))
- mom_out: float32 [1024, 1024], P(('tok', 'rep'))
- sq_out: float32 [1024, 1024], P(('tok', 'rep'))
- new_fkr: float32 [1024, 5120], P(('tok', 'rep'))
- mom_fkr: float32 [1024, 5120], P(('tok', 'rep'))
- sq_fkr: float32 [1024, 5120], P(('tok', 'rep'))
- new_fvalue: float32 [4096, 1024], P(('tok', 'rep'))
- mom_fvalue: float32 [4096, 1024], P(('tok', 'rep'))
- sq_fvalue: float32 [4096, 1024], P(('tok', 'rep'))
- new_vectors: float32 [11, 1024], P(None, ('tok', 'rep'))
- mom_vectors: float32 [11, 1024], P(None, ('tok', 'rep'))
- sq_vectors: float32 [11, 1024], P(None, ('tok', 'rep'))
Inputs may be any that keep to these rules, and one draw needn't show every extreme that they name: `seg_doc`: in each group, along the segments, document numbers start at 0, never fall and rise by one where a new document begins; a segment continues the document of the segment before it where its number is equal. init_num divided by init_den lies within -1.7 to 1.7.
All inputs are finite; a program needn't handle non-finite values.
Results may differ from a plain program's by a relative error of at most 0.023.
Values may be sent and summed in bfloat16 or wider, within the bound.
No kernel may reach another device: no remote copies, remote signals or barrier semaphores. Data moves between devices by JAX's collectives and lax.ppermute only.
A program may use at most 320 MiB of HBM per device.

v0:
```python
import math

import jax
import jax.numpy as jnp
from jax import lax
from jax.sharding import PartitionSpec as P

EMBED_SIZE = 1024
FF = 4096
SEG_LEN = 2048
WBLOCK = 128
STEP = 10


def from_behind(block, axis, distance):
    devices = range(lax.axis_size(axis))
    route = [(i - distance, i) for i in devices if i - distance in devices]
    return lax.ppermute(block, axis, route)


def layer_norm(payload_entries, gain, offset):
    center = payload_entries - jnp.mean(payload_entries, axis=-1, keepdims=True)
    spread = jnp.mean(center * center, axis=-1, keepdims=True)
    return center * lax.rsqrt(spread + 1e-05) * gain + offset


def weight_grad(inputs, grads):
    return jnp.einsum("mti,mto->io", inputs, grads, preferred_element_type=jnp.float32)


def apply_right(inputs, weights):
    return jnp.einsum("mti,io->mto", inputs, weights, preferred_element_type=jnp.float32)


def apply_left(grads, weights):
    return jnp.einsum("mto,io->mti", grads, weights, preferred_element_type=jnp.float32)


def mix_inputs(normed, incoming, previous, is_new, factors):
    before = jnp.concatenate([incoming, normed[:, :-1]], axis=1)
    before = jnp.where(is_new[:, :, None], previous, before)
    return tuple((normed * factor + before * (1.0 - factor) for factor in factors))


def from_left(last_rows):
    return from_behind(last_rows, "tok", 1)


def to_left(grad_rows):
    return from_behind(grad_rows, "tok", -1)


def wkv_by_block(
    lookup_entries,
    payload_entries,
    fading_speeds,
    ongoing_reward,
    supplied_numerator,
    supplied_denominator,
    fresh_block_flags,
):
    exact = lax.Precision.HIGHEST
    micro_count, length, channel_width = lookup_entries.shape
    blocks = length // WBLOCK
    rate = -jnp.exp(fading_speeds)
    displacement_amounts = jnp.arange(WBLOCK)
    lag_steps = displacement_amounts[:, None] - 1 - displacement_amounts[None, :]
    inner = jnp.where(
        (lag_steps >= 0)[:, :, None],
        jnp.exp(jnp.maximum(lag_steps, 0)[:, :, None].astype(jnp.float32) * rate),
        0.0,
    )
    tiled_lookup_vectors = lookup_entries.reshape(micro_count, blocks, WBLOCK, channel_width)
    value_blocks = payload_entries.reshape(micro_count, blocks, WBLOCK, channel_width)
    weight_rows = jnp.exp(tiled_lookup_vectors)
    weighted = weight_rows * value_blocks
    local_num = jnp.einsum("tic,mbic->mbtc", inner, weighted, precision=exact)
    local_den = jnp.einsum("tic,mbic->mbtc", inner, weight_rows, precision=exact)
    tail = jnp.exp((WBLOCK - 1 - displacement_amounts)[:, None].astype(jnp.float32) * rate)
    add_num = jnp.sum(tail * weighted, axis=2)
    add_den = jnp.sum(tail * weight_rows, axis=2)
    step_decay = jnp.exp(WBLOCK * rate)

    def block_step(state, inputs):
        numer, denom = state
        is_new, starting_dividend, starting_divisor, plus_num, plus_den = inputs
        numer = jnp.where(is_new[:, None], starting_dividend, numer)
        denom = jnp.where(is_new[:, None], starting_divisor, denom)
        return ((step_decay * numer + plus_num, step_decay * denom + plus_den), (numer, denom))

    zero_state = jnp.zeros((micro_count, channel_width), jnp.float32)
    scan_inputs = (
        jnp.moveaxis(fresh_block_flags, 1, 0),
        jnp.moveaxis(supplied_numerator, 1, 0),
        jnp.moveaxis(supplied_denominator, 1, 0),
        jnp.moveaxis(add_num, 1, 0),
        jnp.moveaxis(add_den, 1, 0),
    )
    final_state, (begin_num, begin_den) = lax.scan(
        block_step, (zero_state, zero_state), scan_inputs
    )
    begin_num = jnp.moveaxis(begin_num, 0, 1)
    begin_den = jnp.moveaxis(begin_den, 0, 1)
    within = jnp.exp(displacement_amounts[:, None].astype(jnp.float32) * rate)
    diagonal_term = jnp.exp(ongoing_reward + tiled_lookup_vectors)
    numer_all = within * begin_num[:, :, None, :] + local_num + diagonal_term * value_blocks
    denom_all = within * begin_den[:, :, None, :] + local_den + diagonal_term
    return (numer_all / denom_all).reshape(micro_count, length, channel_width)


def adam_step(master, moment, second, gradient, rate, shrink):
    moment_new = 0.9 * moment + 0.1 * gradient
    second_new = 0.95 * second + 0.05 * gradient * gradient
    scaled = moment_new / (1.0 - 0.9**STEP) / (jnp.sqrt(second_new / (1.0 - 0.95**STEP)) + 1e-08)
    return (master - rate * (scaled + shrink * master), moment_new, second_new)


def on_device(
    tokens,
    cotangent,
    init_num,
    init_den,
    prev_att,
    seg_doc,
    w_kvr,
    w_out,
    f_kr,
    f_value,
    vectors,
    m_kvr,
    v_kvr,
    m_out,
    v_out,
    m_fkr,
    v_fkr,
    m_fvalue,
    v_fvalue,
    vec_m,
    vec_v,
):
    exact = lax.Precision.HIGHEST
    tok_count = lax.axis_size("tok")
    rep_count = lax.axis_size("rep")
    token_position = lax.axis_index("tok")
    flat_index = token_position * rep_count + lax.axis_index("rep")
    channel_width = EMBED_SIZE // tok_count
    local_len = tokens.shape[2]
    seg_count = seg_doc.shape[2]
    per_seg = SEG_LEN // WBLOCK
    low_kvr = w_kvr.astype(jnp.bfloat16)
    low_out = w_out.astype(jnp.bfloat16)
    low_fkr = f_kr.astype(jnp.bfloat16)
    low_fvalue = f_value.astype(jnp.bfloat16)
    part_kvr, part_out, part_fkr, part_fvalue = (
        lax.all_gather(low_kvr, "rep", axis=0, tiled=True),
        lax.all_gather(low_out, "rep", axis=0, tiled=True),
        lax.all_gather(low_fkr, "rep", axis=0, tiled=True),
        lax.all_gather(low_fvalue, "rep", axis=0, tiled=True),
    )
    kvr_full, out_full, fkr_full, fvalue_full = (
        lax.all_gather(part_kvr, "tok", axis=0, tiled=True),
        lax.all_gather(part_out, "tok", axis=0, tiled=True),
        lax.all_gather(part_fkr, "tok", axis=0, tiled=True),
        lax.all_gather(part_fvalue, "tok", axis=0, tiled=True),
    )
    position = token_position * local_len + jnp.arange(local_len)
    row_seg = position // SEG_LEN
    row_start = position % SEG_LEN == 0
    seg_match = row_seg[:, None] == jnp.arange(seg_count)[None, :]
    onehot_rows = seg_match.astype(jnp.float32)
    documents = seg_doc[:, 0, :]
    document_start_marker = jnp.concatenate(
        [jnp.ones((documents.shape[0], 1), jnp.bool_), documents[:, 1:] != documents[:, :-1]],
        axis=1,
    )
    row_new = jnp.logical_and(
        row_start[None, :],
        jnp.any(jnp.logical_and(document_start_marker[:, None, :], seg_match[None, :, :]), axis=-1),
    )
    block_index = jnp.arange(seg_count * per_seg)
    fresh_block_flags = jnp.logical_and(
        (block_index % per_seg == 0)[None, :], jnp.repeat(document_start_marker, per_seg, axis=1)
    )
    decay_local = lax.dynamic_slice_in_dim(
        vectors[9], token_position * channel_width, channel_width
    )
    reward_portion = lax.dynamic_slice_in_dim(
        vectors[10], token_position * channel_width, channel_width
    )

    def run(first_micro, last_micro):
        tokens_in = tokens[first_micro:last_micro, 0].astype(jnp.float32)
        cot_in = cotangent[first_micro:last_micro, 0].astype(jnp.float32)
        new_rows = row_new[first_micro:last_micro]
        fresh_blocks = fresh_block_flags[first_micro:last_micro]
        att_rows = jnp.einsum(
            "ts,msd->mtd",
            onehot_rows,
            prev_att[first_micro:last_micro, 0].astype(jnp.float32),
            precision=exact,
        )
        supplied_numerator = jnp.repeat(init_num[first_micro:last_micro, 0], per_seg, axis=1)
        supplied_denominator = jnp.repeat(init_den[first_micro:last_micro, 0], per_seg, axis=1)
        normed, norm_back = jax.vjp(layer_norm, tokens_in, vectors[0], vectors[1])
        incoming = from_left(normed[:, -1:])

        def first_mix(normed_in, incoming_in, factor_key, factor_value, factor_recept):
            return mix_inputs(
                normed_in,
                incoming_in,
                att_rows,
                new_rows,
                (factor_key, factor_value, factor_recept),
            )

        (mix_key, mix_value, mix_recept), mix_back = jax.vjp(
            first_mix, normed, incoming, vectors[4], vectors[5], vectors[6]
        )
        key_low = mix_key.astype(jnp.bfloat16)
        value_low = mix_value.astype(jnp.bfloat16)
        recept_low = mix_recept.astype(jnp.bfloat16)
        lookup_entries = apply_right(key_low, kvr_full[:, :EMBED_SIZE]).astype(jnp.bfloat16)
        payload_entries = apply_right(value_low, kvr_full[:, EMBED_SIZE : 2 * EMBED_SIZE]).astype(
            jnp.bfloat16
        )
        recept = apply_right(recept_low, kvr_full[:, 2 * EMBED_SIZE :])
        key_chan, value_chan = (
            lax.all_to_all(lookup_entries, "tok", split_axis=2, concat_axis=1, tiled=True),
            lax.all_to_all(payload_entries, "tok", split_axis=2, concat_axis=1, tiled=True),
        )

        def weighted_average_feature(
            lookup_argument, payload_argument, fading_argument, reward_argument
        ):
            return wkv_by_block(
                lookup_argument,
                payload_argument,
                fading_argument,
                reward_argument,
                supplied_numerator,
                supplied_denominator,
                fresh_blocks,
            )

        wkv_chan, wkv_backward_pass = jax.vjp(
            weighted_average_feature,
            key_chan.astype(jnp.float32),
            value_chan.astype(jnp.float32),
            decay_local,
            reward_portion,
        )
        wkv_rows = lax.all_to_all(
            wkv_chan.astype(jnp.bfloat16), "tok", split_axis=1, concat_axis=2, tiled=True
        ).astype(jnp.float32)
        gate_att = jax.nn.sigmoid(recept)
        gated = (gate_att * wkv_rows).astype(jnp.bfloat16)
        middle = tokens_in + apply_right(gated, out_full)
        normed_two, norm_back_two = jax.vjp(layer_norm, middle, vectors[2], vectors[3])
        incoming_two = from_left(normed_two[:, -1:])

        def second_mix(normed_in, incoming_in, factor_key, factor_recept):
            return mix_inputs(
                normed_in,
                incoming_in,
                jnp.zeros_like(normed_in),
                new_rows,
                (factor_key, factor_recept),
            )

        (mix_key_two, mix_recept_two), mix_back_two = jax.vjp(
            second_mix, normed_two, incoming_two, vectors[7], vectors[8]
        )
        key_two_low = mix_key_two.astype(jnp.bfloat16)
        recept_two_low = mix_recept_two.astype(jnp.bfloat16)
        hidden = apply_right(key_two_low, fkr_full[:, :FF])
        gate_pre = apply_right(recept_two_low, fkr_full[:, FF:])
        active = jnp.maximum(hidden, 0.0)
        squared = jnp.square(active).astype(jnp.bfloat16)
        channel = apply_right(squared, fvalue_full)
        gate_ffn = jax.nn.sigmoid(gate_pre)
        result = (middle + gate_ffn * channel).astype(jnp.bfloat16)
        d_channel = (cot_in * gate_ffn).astype(jnp.bfloat16)
        d_gate = (cot_in * channel * gate_ffn * (1.0 - gate_ffn)).astype(jnp.bfloat16)
        grad_fvalue = weight_grad(squared, d_channel)
        d_hidden = (apply_left(d_channel, fvalue_full) * 2.0 * active).astype(jnp.bfloat16)
        grad_fkr = jnp.concatenate(
            [weight_grad(key_two_low, d_hidden), weight_grad(recept_two_low, d_gate)], axis=1
        )
        d_mix_key_two = apply_left(d_hidden, fkr_full[:, :FF])
        d_mix_recept_two = apply_left(d_gate, fkr_full[:, FF:])
        d_normed_two, d_incoming_two, d_fmix_key, d_fmix_recept = mix_back_two(
            (d_mix_key_two, d_mix_recept_two)
        )
        d_normed_two = d_normed_two.at[:, -1:].add(to_left(d_incoming_two))
        d_middle_norm, d_gain_two, d_offset_two = norm_back_two(d_normed_two)
        d_middle = cot_in + d_middle_norm
        d_att = d_middle.astype(jnp.bfloat16)
        grad_out = weight_grad(gated, d_att)
        d_gated = apply_left(d_att, out_full)
        d_wkv = (d_gated * gate_att).astype(jnp.bfloat16)
        d_recept = (d_gated * wkv_rows * gate_att * (1.0 - gate_att)).astype(jnp.bfloat16)
        wkv_channel_gradient = lax.all_to_all(d_wkv, "tok", split_axis=2, concat_axis=1, tiled=True)
        (
            lookup_feature_derivative,
            payload_feature_derivative,
            fading_derivative,
            reward_derivative,
        ) = wkv_backward_pass(wkv_channel_gradient.astype(jnp.float32))
        d_keys, d_values = (
            lax.all_to_all(
                lookup_feature_derivative.astype(jnp.bfloat16),
                "tok",
                split_axis=1,
                concat_axis=2,
                tiled=True,
            ),
            lax.all_to_all(
                payload_feature_derivative.astype(jnp.bfloat16),
                "tok",
                split_axis=1,
                concat_axis=2,
                tiled=True,
            ),
        )
        grad_kvr = jnp.concatenate(
            [
                weight_grad(key_low, d_keys),
                weight_grad(value_low, d_values),
                weight_grad(recept_low, d_recept),
            ],
            axis=1,
        )
        d_mix_key = apply_left(d_keys, kvr_full[:, :EMBED_SIZE])
        d_mix_value = apply_left(d_values, kvr_full[:, EMBED_SIZE : 2 * EMBED_SIZE])
        d_mix_recept = apply_left(d_recept, kvr_full[:, 2 * EMBED_SIZE :])
        d_normed, d_incoming, d_share_key, d_share_value, d_share_recept = mix_back(
            (d_mix_key, d_mix_value, d_mix_recept)
        )
        d_normed = d_normed.at[:, -1:].add(to_left(d_incoming))
        d_tokens_norm, d_gain_one, d_offset_one = norm_back(d_normed)
        grad_rows = (d_middle + d_tokens_norm).astype(jnp.bfloat16)
        decay_full = lax.dynamic_update_slice_in_dim(
            jnp.zeros((EMBED_SIZE,), jnp.float32),
            fading_derivative,
            token_position * channel_width,
            0,
        )
        reward_assembled = lax.dynamic_update_slice_in_dim(
            jnp.zeros((EMBED_SIZE,), jnp.float32),
            reward_derivative,
            token_position * channel_width,
            0,
        )
        grad_vec = jnp.stack(
            [
                d_gain_one,
                d_offset_one,
                d_gain_two,
                d_offset_two,
                d_share_key,
                d_share_value,
                d_share_recept,
                d_fmix_key,
                d_fmix_recept,
                decay_full,
                reward_assembled,
            ]
        )
        return (result, grad_rows, (grad_kvr, grad_out, grad_fkr, grad_fvalue, grad_vec))

    pieces = [run(micro_index, micro_index + 1) for micro_index in range(tokens.shape[0])]
    mixed_rows = jnp.concatenate([piece[0] for piece in pieces], axis=0)
    grad_rows_all = jnp.concatenate([piece[1] for piece in pieces], axis=0)
    totals = pieces[0][2]
    for piece in pieces[1:]:
        totals = tuple((total + extra for total, extra in zip(totals, piece[2])))
    grad_kvr, grad_out, grad_fkr, grad_fvalue, grad_vec = totals
    tok_kvr, tok_out, tok_fkr, tok_fvalue, tok_vec = (
        lax.psum_scatter(
            grad_kvr.astype(jnp.bfloat16), "tok", scatter_dimension=0, tiled=True
        ).astype(jnp.float32),
        lax.psum_scatter(
            grad_out.astype(jnp.bfloat16), "tok", scatter_dimension=0, tiled=True
        ).astype(jnp.float32),
        lax.psum_scatter(
            grad_fkr.astype(jnp.bfloat16), "tok", scatter_dimension=0, tiled=True
        ).astype(jnp.float32),
        lax.psum_scatter(
            grad_fvalue.astype(jnp.bfloat16), "tok", scatter_dimension=0, tiled=True
        ).astype(jnp.float32),
        lax.psum_scatter(
            grad_vec.astype(jnp.bfloat16), "tok", scatter_dimension=1, tiled=True
        ).astype(jnp.float32),
    )
    sum_kvr, sum_out, sum_fkr, sum_fvalue, sum_vec = (
        lax.psum_scatter(
            tok_kvr.astype(jnp.bfloat16), "rep", scatter_dimension=0, tiled=True
        ).astype(jnp.float32),
        lax.psum_scatter(
            tok_out.astype(jnp.bfloat16), "rep", scatter_dimension=0, tiled=True
        ).astype(jnp.float32),
        lax.psum_scatter(
            tok_fkr.astype(jnp.bfloat16), "rep", scatter_dimension=0, tiled=True
        ).astype(jnp.float32),
        lax.psum_scatter(
            tok_fvalue.astype(jnp.bfloat16), "rep", scatter_dimension=0, tiled=True
        ).astype(jnp.float32),
        lax.psum_scatter(
            tok_vec.astype(jnp.bfloat16), "rep", scatter_dimension=1, tiled=True
        ).astype(jnp.float32),
    )
    base_rate = 2.5 / math.sqrt(EMBED_SIZE)
    new_kvr, mom_kvr, sq_kvr = adam_step(w_kvr, m_kvr, v_kvr, sum_kvr, base_rate, 0.01)
    new_out, mom_out, sq_out = adam_step(w_out, m_out, v_out, sum_out, 4.0 * base_rate, 0.01)
    new_fkr, mom_fkr, sq_fkr = adam_step(f_kr, m_fkr, v_fkr, sum_fkr, base_rate, 0.01)
    new_fvalue, mom_fvalue, sq_fvalue = adam_step(
        f_value, m_fvalue, v_fvalue, sum_fvalue, 2.5 / math.sqrt(FF), 0.01
    )
    columns = vec_m.shape[1]
    vec_master = lax.dynamic_slice_in_dim(vectors, flat_index * columns, columns, 1)
    vec_rates = jnp.array([0.6, 0.3, 0.6, 0.3, 0.3, 0.3, 0.3, 0.3, 0.3, 3.0, 0.5], jnp.float32)[
        :, None
    ]
    new_vectors, mom_vectors, sq_vectors = adam_step(
        vec_master, vec_m, vec_v, sum_vec, vec_rates, 0.0
    )
    out_shape = tokens.shape
    return (
        mixed_rows.reshape(out_shape),
        grad_rows_all.reshape(out_shape),
        new_kvr,
        mom_kvr,
        sq_kvr,
        new_out,
        mom_out,
        sq_out,
        new_fkr,
        mom_fkr,
        sq_fkr,
        new_fvalue,
        mom_fvalue,
        sq_fvalue,
        new_vectors,
        mom_vectors,
        sq_vectors,
    )


def solution(mesh):
    placed = (
        P(None, "rep", "tok", None),
        P(None, "rep", "tok", None),
        P(None, "rep", None, "tok"),
        P(None, "rep", None, "tok"),
        P(None, "rep", None, None),
        P(None, "rep", None),
        P(("tok", "rep"), None),
        P(("tok", "rep"), None),
        P(("tok", "rep"), None),
        P(("tok", "rep"), None),
        P(),
        P(("tok", "rep"), None),
        P(("tok", "rep"), None),
        P(("tok", "rep"), None),
        P(("tok", "rep"), None),
        P(("tok", "rep"), None),
        P(("tok", "rep"), None),
        P(("tok", "rep"), None),
        P(("tok", "rep"), None),
        P(None, ("tok", "rep")),
        P(None, ("tok", "rep")),
    )
    return jax.shard_map(
        on_device,
        mesh=mesh,
        in_specs=placed,
        out_specs=(
            P(None, "rep", "tok", None),
            P(None, "rep", "tok", None),
            P(("tok", "rep"), None),
            P(("tok", "rep"), None),
            P(("tok", "rep"), None),
            P(("tok", "rep"), None),
            P(("tok", "rep"), None),
            P(("tok", "rep"), None),
            P(("tok", "rep"), None),
            P(("tok", "rep"), None),
            P(("tok", "rep"), None),
            P(("tok", "rep"), None),
            P(("tok", "rep"), None),
            P(("tok", "rep"), None),
            P(None, ("tok", "rep")),
            P(None, ("tok", "rep")),
            P(None, ("tok", "rep")),
        ),
        check_vma=False,
    )
```

profile of v0, /device:TPU:0, one launch (start us, length us, event | category | flops | bytes accessed | tf_op | source)
XLA Modules:
  0.0 2038.9 jit_solution(1832853886922606940)
XLA Ops:
  8.4 21.7 %all_gather.24 = bf16[128,3072]{1,0:T(8,128)(2,1)} all-gather(bf16[32,3072]{1,0:T(8,128)(2,1)S(1)} %convert_element_type.773), channel_id=1, replica_groups=mesh['tok'=8,'rep'=4] {'rep'}, dimensions={0}, use_global_device_ids=true | all-gather | bytes 983040 | tf_op jit(solution)/shard_map/all_gather | solution.py:155
  253.1 161.3 %while.99 = (s32[]{:T(128)}, f32[1,128]{1,0:T(1,128)}, f32[1,128]{1,0:T(1,128)}, f32[32,1,128]{2,1,0:T(1,128)S(1)}, f32[32,1,128]{2,1,0:T(1,128)S(1)}, /*index=5...) while((s32[]{:T(128)}, f32[1,128]{1,0:T(1,128)}, ...), condition=%wide.region_14.15_spmd.clone, body=%wide.region_13.14_spmd.clone.sunk | while | flops 1539 | bytes 8357 | solution.py:99
  462.5 24.6 %reduce.99 = bf16[4096,128]{1,0:T(8,128)(2,1)} reduce(bf16[4096,1,128]{2,1,0:T(2,128)(2,1)} %bitcast.960, bf16[]{:T(256)} %broadcast.1936), dimensions={1}, to_apply=%bitcast.791.reduce_sub_computation | reduce | bytes 2097154
  493.8 103.8 %while.98 = (s32[]{:T(128)}, f32[1,128]{1,0:T(1,128)S(1)}, f32[1,128]{1,0:T(1,128)S(1)}, f32[32,1,128]{2,1,0:T(1,128)S(1)}, f32[32,1,128]{2,1,0:T(1,128)S(1)}, /...) while((s32[]{:T(128)}, f32[1,128]{1,0:T(1,128)S(1)}, ...), condition=%wide.region_6.7_spmd.clone, body=%wide.region_5.6_spmd.clone.sunk | while | flops 1539 | bytes 8357 | solution.py:99
  654.1 24.4 %reduce.98 = bf16[4096,128]{1,0:T(8,128)(2,1)} reduce(bf16[4096,1,128]{2,1,0:T(2,128)(2,1)} %bitcast.963, bf16[]{:T(256)} %broadcast.1936), dimensions={1}, to_apply=%bitcast.793.reduce_sub_computation | reduce | bytes 2097154
  772.9 16.7 add_convert_fusion
  789.7 72.7 %reduce-scatter.27.cloned.1.call-done = bf16[512,1024]{1,0:T(8,128)(2,1)} async-done(((bf16[4096,1024]{1,0:T(8,128)(2,1)}), bf16[512,1024]{1,0:T(8,128)(2,1)}) %reduce-scatter.27.cloned.1.call-update) | async-done | bytes 1048592 | tf_op jit(solution)/shard_map/reduce_scatter | solution.py:388
  862.4 29.3 %reduce-scatter.29.cloned.1.call-done = bf16[128,1024]{1,0:T(8,128)(2,1)} async-done(((bf16[512,1024]{1,0:T(8,128)(2,1)}), bf16[128,1024]{1,0:T(8,128)(2,1)}) %reduce-scatter.29.cloned.1.call-update) | async-done | bytes 262160 | tf_op jit(solution)/shard_map/reduce_scatter | solution.py:405
  894.6 26.5 %all-gather.15.cloned.1.call-done = bf16[512,1024]{1,0:T(8,128)(2,1)} async-done(((bf16[128,1024]{1,0:T(8,128)(2,1)}), bf16[512,1024]{1,0:T(8,128)(2,1)}) %all-gather.15.cloned.1.call-update) | async-done | bytes 1048592 | tf_op jit(solution)/shard_map/all_gather | solution.py:158
  921.9 55.1 %all-gather.17.cloned.1.call-done = bf16[4096,1024]{1,0:T(8,128)(2,1)} async-done(((bf16[512,1024]{1,0:T(8,128)(2,1)}), bf16[4096,1024]{1,0:T(8,128)(2,1)}) %all-gather.17.cloned.1.call-update) | async-done | bytes 8388624 | tf_op jit(solution)/shard_map/all_gather | solution.py:164
  1182.8 93.9 %while.100 = (s32[]{:T(128)}, f32[128]{0:T(128)}, f32[1,128]{1,0:T(1,128)S(1)}, f32[1,128]{1,0:T(1,128)}, f32[32,1,128]{2,1,0:T(1,128)S(1)}, /*index=5*/f32[32,1...) while((s32[]{:T(128)}, f32[128]{0:T(128)}, ...), condition=%wide.region_22.23_spmd.clone, body=%wide.region_21.22_spmd.clone.sunk | while | flops 2180 | bytes 10540 | solution.py:99
  1278.4 58.4 %while.101 = (s32[]{:T(128)}, f32[128]{0:T(128)}, f32[1,128]{1,0:T(1,128)S(1)}, f32[1,128]{1,0:T(1,128)S(1)}, f32[32,1,128]{2,1,0:T(1,128)S(1)}, /*index=5*/f32[...) while((s32[]{:T(128)}, f32[128]{0:T(128)}, ...), condition=%wide.region_30.31_spmd.clone, body=%wide.region_29.30_spmd.clone.sunk | while | flops 2180 | bytes 10540 | solution.py:99
  1365.5 23.3 %reduce.105 = bf16[4096,128]{1,0:T(8,128)(2,1)} reduce(bf16[4096,1,128]{2,1,0:T(2,128)(2,1)S(1)} %bitcast.970, bf16[]{:T(256)} %broadcast.1936), dimensions={1}, to_apply=%bitcast.803.reduce_sub_computation | reduce | bytes 2097154
  1395.8 16.1 fusion.258
  1452.4 23.5 %reduce.104 = bf16[4096,128]{1,0:T(8,128)(2,1)} reduce(bf16[4096,1,128]{2,1,0:T(2,128)(2,1)S(1)} %bitcast.971, bf16[]{:T(256)} %broadcast.1936), dimensions={1}, to_apply=%bitcast.805.reduce_sub_computation | reduce | bytes 2097154
  1523.5 23.3 %reduce.103 = bf16[4096,128]{1,0:T(8,128)(2,1)} reduce(bf16[4096,1,128]{2,1,0:T(2,128)(2,1)S(1)} %bitcast.972, bf16[]{:T(256)} %broadcast.1936), dimensions={1}, to_apply=%bitcast.799.reduce_sub_computation | reduce | bytes 2097154
  1565.4 23.4 %reduce.102 = bf16[4096,128]{1,0:T(8,128)(2,1)} reduce(bf16[4096,1,128]{2,1,0:T(2,128)(2,1)S(1)} %bitcast.953, bf16[]{:T(256)} %broadcast.1936), dimensions={1}, to_apply=%bitcast.801.reduce_sub_computation | reduce | bytes 2097154
  1593.4 16.7 fusion.187
  1614.6 17.9 fusion.39
  1781.3 65.1 %reduce-scatter.31.cloned.1.call-done = bf16[128,3072]{1,0:T(8,128)(2,1)} async-done(((bf16[1024,3072]{1,0:T(8,128)(2,1)}), bf16[128,3072]{1,0:T(8,128)(2,1)}) %reduce-scatter.31.cloned.1.call-update) | async-done | bytes 786448
  1846.5 85.3 %reduce-scatter.23.cloned.1.call-done = bf16[128,5120]{1,0:T(8,128)(2,1)} async-done(((bf16[1024,5120]{1,0:T(8,128)(2,1)}), bf16[128,5120]{1,0:T(8,128)(2,1)}) %reduce-scatter.23.cloned.1.call-update) | async-done | bytes 1310736 | tf_op jit(solution)/shard_map/reduce_scatter | solution.py:385
  1955.2 17.8 reduce-scatter.21.cloned.1.call-done
  1974.7 22.2 %reduce-scatter.33.cloned.1.call-done = bf16[32,3072]{1,0:T(8,128)(2,1)} async-done(((bf16[128,3072]{1,0:T(8,128)(2,1)}), bf16[32,3072]{1,0:T(8,128)(2,1)}) %reduce-scatter.33.cloned.1.call-update) | async-done | bytes 196624 | tf_op jit(solution)/shard_map/reduce_scatter | solution.py:396
  1999.0 30.6 %reduce-scatter.25.cloned.1.call-done = bf16[32,5120]{1,0:T(8,128)(2,1)} async-done(((bf16[128,5120]{1,0:T(8,128)(2,1)}), bf16[32,5120]{1,0:T(8,128)(2,1)}) %reduce-scatter.25.cloned.1.call-update) | async-done | bytes 327696 | tf_op jit(solution)/shard_map/reduce_scatter | solution.py:402
  (1291 shorter events, 1383.7 us)
Async XLA Ops:
  7.2 68.3 %all-gather.7.cloned.1.call-start = ((), (), s32[]{:S(2)}) async-start(), calls=%async_computation.22 | async-start | bytes 7077888 | tf_op jit(solution)/shard_map/all_gather | solution.py:161
  30.2 155.7 %all-gather.11.cloned.1.call-start = ((), (), s32[]{:S(2)}) async-start(), calls=%async_computation.24 | async-start | bytes 1638400 | tf_op jit(solution)/shard_map/all_gather | solution.py:157
  31.0 684.6 %all-gather.9.cloned.1.call-start = ((), (), s32[]{:S(2)}) async-start(), calls=%async_computation.23 | async-start | bytes 2359296 | tf_op jit(solution)/shard_map/all_gather | solution.py:162
  97.8 27.1 %all-to-all-start.3 = ((bf16[8,2,32768]{2,1,0:T(2,128)(2,1)}), bf16[8,2,32768]{2,1,0:T(2,128)(2,1)}, u32[]{:S(2)}, u32[]{:S(2)}) async-start(bf16[8,2,32768]{2,1,0:T(2,128)(2,1)} %reshape.3236), calls=%async_computation.3 | async-start | bytes 2097152 | tf_op jit(solution)/shard_map/all_to_all | solution.py:228
  124.9 27.9 %all-to-all-start.4 = ((bf16[8,2,32768]{2,1,0:T(2,128)(2,1)}), bf16[8,2,32768]{2,1,0:T(2,128)(2,1)}, u32[]{:S(2)}, u32[]{:S(2)}) async-start(bf16[8,2,32768]{2,1,0:T(2,128)(2,1)} %reshape.3234), calls=%async_computation.4 | async-start | bytes 2097152 | tf_op jit(solution)/shard_map/all_to_all | solution.py:229
  179.8 52.6 %all-to-all-start.1 = ((bf16[8,2,32768]{2,1,0:T(2,128)(2,1)}), bf16[8,2,32768]{2,1,0:T(2,128)(2,1)}, u32[]{:S(2)}, u32[]{:S(2)}) async-start(bf16[8,2,32768]{2,1,0:T(2,128)(2,1)} %reshape.3240), calls=%async_computation.1 | async-start | bytes 2097152 | tf_op jit(solution)/shard_map/all_to_all | solution.py:229
  184.1 553.4 %all-gather.13.cloned.1.call-start = ((), (), s32[]{:S(2)}) async-start(), calls=%async_computation.25 | async-start | bytes 11796480 | tf_op jit(solution)/shard_map/all_gather | solution.py:163
  489.3 191.4 %all-to-all-start.5 = ((bf16[8,2,32768]{2,1,0:T(2,128)(2,1)}), bf16[8,2,32768]{2,1,0:T(2,128)(2,1)}, u32[]{:S(2)}, u32[]{:S(2)}) async-start(bf16[8,2,32768]{2,1,0:T(2,128)(2,1)} %reshape.3242), calls=%async_computation.5 | async-start | bytes 2097152 | tf_op jit(solution)/shard_map/all_to_all | solution.py:252
  685.0 177.4 %reduce-scatter.27.cloned.1.call-start = ((), (), s32[]{:S(2)}) async-start(), calls=%async_computation.32 | async-start | bytes 9437184 | tf_op jit(solution)/shard_map/reduce_scatter | solution.py:388
  789.6 102.1 %reduce-scatter.29.cloned.1.call-start = ((), (), s32[]{:S(2)}) async-start(), calls=%async_computation.33 | async-start | bytes 1310720 | tf_op jit(solution)/shard_map/reduce_scatter | solution.py:405
  862.4 58.8 %all-gather.15.cloned.1.call-start = ((), (), s32[]{:S(2)}) async-start(), calls=%async_computation.26 | async-start | bytes 1310720 | tf_op jit(solution)/shard_map/all_gather | solution.py:158
  894.4 82.5 %all-gather.17.cloned.1.call-start = ((), (), s32[]{:S(2)}) async-start(), calls=%async_computation.27 | async-start | bytes 9437184 | tf_op jit(solution)/shard_map/all_gather | solution.py:164
  1391.1 99.3 %all-to-all-start.11 = ((bf16[8,2,32768]{2,1,0:T(2,128)(2,1)}), bf16[8,2,32768]{2,1,0:T(2,128)(2,1)}, u32[]{:S(2)}, u32[]{:S(2)}) async-start(bf16[8,2,32768]{2,1,0:T(2,128)(2,1)} %reshape.3254), calls=%async_computation.11 | async-start | bytes 2097152 | tf_op jit(solution)/shard_map/all_to_all | solution.py:310
  1490.4 63.7 %all-to-all-start.10 = ((bf16[8,2,32768]{2,1,0:T(2,128)(2,1)}), bf16[8,2,32768]{2,1,0:T(2,128)(2,1)}, u32[]{:S(2)}, u32[]{:S(2)}) async-start(bf16[8,2,32768]{2,1,0:T(2,128)(2,1)} %reshape.3256), calls=%async_computation.10 | async-start | bytes 2097152 | tf_op jit(solution)/shard_map/all_to_all | solution.py:317
  1554.1 56.0 %all-to-all-start.8 = ((bf16[8,2,32768]{2,1,0:T(2,128)(2,1)}), bf16[8,2,32768]{2,1,0:T(2,128)(2,1)}, u32[]{:S(2)}, u32[]{:S(2)}) async-start(bf16[8,2,32768]{2,1,0:T(2,128)(2,1)} %reshape.3250), calls=%async_computation.8 | async-start | bytes 2097152 | tf_op jit(solution)/shard_map/all_to_all | solution.py:310
  1610.1 46.3 %all-to-all-start.7 = ((bf16[8,2,32768]{2,1,0:T(2,128)(2,1)}), bf16[8,2,32768]{2,1,0:T(2,128)(2,1)}, u32[]{:S(2)}, u32[]{:S(2)}) async-start(bf16[8,2,32768]{2,1,0:T(2,128)(2,1)} %reshape.3252), calls=%async_computation.7 | async-start | bytes 2097152 | tf_op jit(solution)/shard_map/all_to_all | solution.py:317
  1614.5 156.4 %reduce-scatter.35.cloned.1.call-start = ((), (), s32[]{:S(2)}) async-start(), calls=%async_computation.36 | async-start | bytes 294912
  1698.8 82.5 %reduce-scatter.19.cloned.1.call-start = ((), (), s32[]{:S(2)}) async-start(), calls=%async_computation.28 | async-start | bytes 2359296 | tf_op jit(solution)/shard_map/reduce_scatter | solution.py:382
  1704.0 142.4 %reduce-scatter.31.cloned.1.call-start = ((), (), s32[]{:S(2)}) async-start(), calls=%async_computation.34 | async-start | bytes 7077888
  1732.4 199.4 %reduce-scatter.23.cloned.1.call-start = ((), (), s32[]{:S(2)}) async-start(), calls=%async_computation.30 | async-start | bytes 11796480 | tf_op jit(solution)/shard_map/reduce_scatter | solution.py:385
  1770.8 182.2 %reduce-scatter.37.cloned.1.call-start = ((), (), s32[]{:S(2)}) async-start(), calls=%async_computation.37 | async-start | bytes 40960
  1771.5 201.5 %reduce-scatter.21.cloned.1.call-start = ((), (), s32[]{:S(2)}) async-start(), calls=%async_computation.29 | async-start | bytes 327680 | tf_op jit(solution)/shard_map/reduce_scatter | solution.py:399
  1781.3 215.6 %reduce-scatter.33.cloned.1.call-start = ((), (), s32[]{:S(2)}) async-start(), calls=%async_computation.35 | async-start | bytes 983040 | tf_op jit(solution)/shard_map/reduce_scatter | solution.py:396
  1846.4 183.2 %reduce-scatter.25.cloned.1.call-start = ((), (), s32[]{:S(2)}) async-start(), calls=%async_computation.31 | async-start | bytes 1638400 | tf_op jit(solution)/shard_map/reduce_scatter | solution.py:402
  (239 other events, 5390.2 us)
Sparse Core Ops, SparseCore 0:
  30.3 45.2 all-gather.6
  77.7 32.6 all-gather.10
  112.3 35.1 all-gather.8
  186.5 64.5 all-gather.12
  789.7 72.5 reduce-scatter.26
  864.6 27.0 reduce-scatter.28
  894.5 26.5 all-gather.14
  923.0 53.8 all-gather.16
  1698.9 36.9 reduce-scatter.34
  1740.0 41.2 reduce-scatter.18
  1784.6 61.7 reduce-scatter.30
  1850.2 81.5 reduce-scatter.22
  1934.1 18.8 reduce-scatter.36
  1955.1 17.8 reduce-scatter.20
  1975.3 21.5 reduce-scatter.32
  1999.1 30.4 reduce-scatter.24
where the time goes:
time: 2050 us; the launch traced here: 2040 us
  other arithmetic  629 us (31%)
  waiting for transfers between devices  442 us (22%)
  local copies, waits for them, and re-layouts  439 us (21%)
  matrix products  402 us (20%)
  starting transfers between devices  70.7 us (3%)
  blocking collectives  36.7 us (2%)
    unnamed x25, other arithmetic  199 us
    unnamed x494, local copies, waits for them, and re-layouts  127 us
    dot_general x6, matrix products, wkv_by_block(): local_num = jnp.einsum('tic,mbic->mbtc', inner, weighted, precision=exact)  91.2 us
    reduce_scatter x1, waiting for transfers between devices, on_device(): lax.psum_scatter(grad_fkr.astype(jnp.bfloat16), 'tok', scatter_dimension=...  85.3 us
    dot_general x6, matrix products, wkv_by_block(): jnp.einsum('tic,mbic->mbtc', inner, weight_rows, precision=exact)  83.4 us
    dot_general x14, matrix products, apply_right(): jnp.einsum('mti,io->mto', inputs, weights, preferred_element_type=jnp.flo...  83.3 us
    add x64, other arithmetic, block_step(): step_decay * denom + plus_den  80.6 us
    dynamic_update_slice x128, other arithmetic, wkv_by_block(): lax.scan(block_step, (zero_state, zero_state), scan_inputs)  80 us
  transfers between devices with their start and end apart: 36, of which 16 were waited for; matrix products, arithmetic and copies ran while one was open for 50% of the time, Pallas kernels for 0%

commit v1 on v0

v1 whole, which is shorter than its diff:
```python
import functools
import math

import jax
import jax.numpy as jnp
from jax import lax
from jax.experimental import pallas as pl
from jax.experimental.pallas import tpu as pltpu
from jax.sharding import PartitionSpec as P

EMBED = 1024
FF = 4096
SEG_LEN = 2048
STEP = 10
CHUNKS = 8
GROUP = 16
STEPS = 16
ROWS = STEPS * GROUP
COLS = 512
EPS = 1e-05
F32 = jnp.float32
BF16 = jnp.bfloat16
VMEM_LIMIT = 60 * 1024 * 1024


def dot_nn(a, b):
    return jnp.dot(a, b, preferred_element_type=F32)


def dot_nt(a, b):
    return lax.dot_general(a, b, (((1,), (1,)), ((), ())), preferred_element_type=F32)


def dot_tn(a, b):
    return lax.dot_general(a, b, (((0,), (0,)), ((), ())), preferred_element_type=F32)


def sigmoid(v):
    return 1.0 / (1.0 + jnp.exp(-v))


def normalize(v):
    center = v - jnp.mean(v, axis=-1, keepdims=True)
    rstd = lax.rsqrt(jnp.mean(center * center, axis=-1, keepdims=True) + EPS)
    return center * rstd, rstd


def norm_back(e, n, rstd):
    return (e - jnp.mean(e, axis=-1, keepdims=True) - n * jnp.mean(e * n, axis=-1, keepdims=True)) * rstd


def swap_matrix():
    row = lax.broadcasted_iota(jnp.int32, (ROWS, ROWS), 0)
    col = lax.broadcasted_iota(jnp.int32, (ROWS, ROWS), 1)
    return jnp.where(col == (row % GROUP) * STEPS + row // GROUP, 1.0, 0.0).astype(BF16)


def swap_in(block):
    return dot_nn(swap_matrix(), block.reshape(ROWS, EMBED))


def swap_out(rows):
    moved = dot_nn(swap_matrix(), rows).astype(BF16)
    return moved.reshape(GROUP // CHUNKS, CHUNKS, STEPS, EMBED)


def col_chunks():
    return [slice(c * COLS, (c + 1) * COLS) for c in range(EMBED // COLS)]


def step_rows(j):
    return slice(j * GROUP, (j + 1) * GROUP)


def full(shape):
    return pl.BlockSpec(shape, lambda i: (0,) * len(shape), pipeline_mode=pl.Buffered(buffer_count=1))


def call(kernel, grid, in_specs, out_specs, out_shape, scratch, flops, name):
    return pl.pallas_call(
        kernel,
        grid=(grid,),
        in_specs=in_specs,
        out_specs=out_specs,
        out_shape=out_shape,
        scratch_shapes=scratch,
        compiler_params=pltpu.CompilerParams(
            dimension_semantics=("arbitrary",), vmem_limit_bytes=VMEM_LIMIT
        ),
        cost_estimate=pl.CostEstimate(flops=flops, bytes_accessed=flops // 400, transcendentals=0),
        name=name,
    )


def mix_one_kernel(
    tok_ref, edge_ref, vec_ref, w_ref,
    xp_ref, xk_ref, xv_ref, xr_ref, k_ref, v_ref, r_ref, end_ref, total_ref,
    carry, state_a, state_b,
):
    i = pl.program_id(0)

    @pl.when(i == 0)
    def _():
        carry[...] = edge_ref[...]
        state_a[...] = jnp.zeros_like(state_a)
        state_b[...] = jnp.zeros_like(state_b)

    x = swap_in(tok_ref[...])
    xp_ref[...] = x.astype(BF16)
    n, _ = normalize(x)
    h = n * vec_ref[0:1, :] + vec_ref[1:2, :]
    hp = jnp.concatenate([carry[...], h[:-GROUP]], axis=0)
    carry[...] = h[-GROUP:]
    diff = h - hp
    xk_ref[...] = (hp + diff * vec_ref[4:5, :]).astype(BF16)
    xv_ref[...] = (hp + diff * vec_ref[5:6, :]).astype(BF16)
    xr_ref[...] = (hp + diff * vec_ref[6:7, :]).astype(BF16)
    k_ref[...] = dot_nn(xk_ref[...], w_ref[:, :EMBED]).astype(BF16)
    v_ref[...] = dot_nn(xv_ref[...], w_ref[:, EMBED : 2 * EMBED]).astype(BF16)
    r_ref[...] = dot_nn(xr_ref[...], w_ref[:, 2 * EMBED :])
    for cols in col_chunks():
        retain = jnp.exp(-jnp.exp(vec_ref[9:10, cols]))
        a = state_a[:, cols]
        b = state_b[:, cols]
        for j in range(STEPS):
            weight = jnp.exp(k_ref[step_rows(j), cols].astype(F32))
            a = retain * a + weight * v_ref[step_rows(j), cols].astype(F32)
            b = retain * b + weight
        state_a[:, cols] = a
        state_b[:, cols] = b

    @pl.when(i == pl.num_programs(0) - 1)
    def _():
        end_ref[:GROUP, :] = state_a[...]
        end_ref[GROUP:, :] = state_b[...]
        rate = -jnp.exp(vec_ref[9:10, :])
        decay = jnp.exp(rate * float(STEPS * pl.num_programs(0)))
        for q in range(2 * GROUP // CHUNKS):
            total = end_ref[q * CHUNKS : q * CHUNKS + 1, :]
            for s in range(1, CHUNKS):
                total = decay * total + end_ref[q * CHUNKS + s : q * CHUNKS + s + 1, :]
            total_ref[q : q + 1, :] = total


def wkv_kernel(
    k_ref, v_ref, r_ref, xp_ref, vec_ref, start_ref, end_ref, w_ref,
    wkv_ref, y_ref, x1_ref, xk_ref, xr_ref, st_ref, first_ref, last_ref,
    carry, state_a, state_b,
):
    i = pl.program_id(0)

    @pl.when(i == 0)
    def _():
        rate = -jnp.exp(vec_ref[9:10, :])
        decay = jnp.exp(rate * float(STEPS * pl.num_programs(0)))
        for q in range(2 * GROUP // CHUNKS):
            state = start_ref[q : q + 1, :]
            target = state_a if q < GROUP // CHUNKS else state_b
            base = (q % (GROUP // CHUNKS)) * CHUNKS
            for s in range(CHUNKS):
                target[base + s : base + s + 1, :] = state
                state = decay * state + end_ref[q * CHUNKS + s : q * CHUNKS + s + 1, :]
        carry[...] = jnp.zeros_like(carry)

    st_ref[0, :GROUP, :] = state_a[...]
    st_ref[0, GROUP:, :] = state_b[...]
    for cols in col_chunks():
        retain = jnp.exp(-jnp.exp(vec_ref[9:10, cols]))
        bonus = vec_ref[10:11, cols]
        a = state_a[:, cols]
        b = state_b[:, cols]
        for j in range(STEPS):
            rows = step_rows(j)
            key = k_ref[rows, cols].astype(F32)
            value = v_ref[rows, cols].astype(F32)
            own = jnp.exp(bonus + key)
            weight = jnp.exp(key)
            wkv = ((a + own * value) / (b + own)).astype(BF16)
            wkv_ref[rows, cols] = wkv
            y_ref[rows, cols] = (sigmoid(r_ref[rows, cols]) * wkv.astype(F32)).astype(BF16)
            a = retain * a + weight * value
            b = retain * b + weight
        state_a[:, cols] = a
        state_b[:, cols] = b
    x1 = xp_ref[...].astype(F32) + dot_nn(y_ref[...], w_ref[...])
    x1_ref[...] = x1
    n, _ = normalize(x1)
    h = n * vec_ref[2:3, :] + vec_ref[3:4, :]
    hp = jnp.concatenate([carry[...], h[:-GROUP]], axis=0)
    carry[...] = h[-GROUP:]
    diff = h - hp
    xk_ref[...] = (hp + diff * vec_ref[7:8, :]).astype(BF16)
    xr_ref[...] = (hp + diff * vec_ref[8:9, :]).astype(BF16)

    @pl.when(i == 0)
    def _():
        first_ref[...] = h[:GROUP]

    last_ref[...] = h[-GROUP:]


def hidden_kernel(xk_ref, xr_ref, w_ref, kq_ref, gate_ref):
    for c in range(FF // EMBED):
        cols = slice(c * EMBED, (c + 1) * EMBED)
        active = jnp.maximum(dot_nn(xk_ref[...], w_ref[:, cols]), 0.0)
        kq_ref[:, cols] = (active * active).astype(BF16)
    gate_ref[...] = sigmoid(dot_nn(xr_ref[...], w_ref[:, FF:]))


def value_kernel(
    kq_ref, gate_ref, x1_ref, cot_ref, w_ref, mixed_ref, dvf_ref, drf_ref, dkf_ref, cp_ref
):
    vf = dot_nn(kq_ref[...], w_ref[...])
    gate = gate_ref[...]
    cot = swap_in(cot_ref[...])
    cp_ref[...] = cot.astype(BF16)
    mixed_ref[...] = swap_out((x1_ref[...] + gate * vf).astype(BF16))
    dvf_ref[...] = (cot * gate).astype(BF16)
    drf_ref[...] = (cot * vf * gate * (1.0 - gate)).astype(BF16)
    for c in range(FF // EMBED):
        cols = slice(c * EMBED, (c + 1) * EMBED)
        back = dot_nt(dvf_ref[...], w_ref[cols, :])
        dkf_ref[:, cols] = (back * 2.0 * jnp.sqrt(kq_ref[:, cols].astype(F32))).astype(BF16)


def middle_back_kernel(
    dkf_ref, drf_ref, w_ref, x1_ref, before_ref, edge_ref, later_ref, cp_ref, vec_ref, wo_ref,
    k_ref, v_ref, r_ref, wkv_ref, st_ref,
    dx1_ref, datt_ref, dwkv_ref, dr_ref, vsum_ref, first_ref, total_ref,
    carry, den, state_p, state_q,
):
    i = pl.program_id(0)
    count = pl.num_programs(0)

    @pl.when(i == 0)
    def _():
        carry[...] = later_ref[...]
        vsum_ref[...] = jnp.zeros_like(vsum_ref)
        state_p[...] = jnp.zeros_like(state_p)
        state_q[...] = jnp.zeros_like(state_q)

    gain = vec_ref[2:3, :]
    offset = vec_ref[3:4, :]
    share_k = vec_ref[7:8, :]
    share_r = vec_ref[8:9, :]
    dxk = dot_nt(dkf_ref[...], w_ref[:, :FF])
    dxr = dot_nt(drf_ref[...], w_ref[:, FF:])
    n, rstd = normalize(x1_ref[...])
    h = n * gain + offset
    n_before, _ = normalize(before_ref[...])
    h_before = jnp.where(i == count - 1, edge_ref[...], n_before * gain + offset)
    diff = h - jnp.concatenate([h_before, h[:-GROUP]], axis=0)
    shift = dxk * (1.0 - share_k) + dxr * (1.0 - share_r)
    dh = dxk * share_k + dxr * share_r + jnp.concatenate([shift[GROUP:], carry[...]], axis=0)
    carry[...] = shift[:GROUP]
    vsum_ref[0:1, :] += jnp.sum(dh * n, axis=0, keepdims=True)
    vsum_ref[1:2, :] += jnp.sum(dh, axis=0, keepdims=True)
    vsum_ref[2:3, :] += jnp.sum(dxk * diff, axis=0, keepdims=True)
    vsum_ref[3:4, :] += jnp.sum(dxr * diff, axis=0, keepdims=True)
    dx1 = cp_ref[...].astype(F32) + norm_back(dh * gain, n, rstd)
    dx1_ref[...] = dx1
    datt_ref[...] = dx1.astype(BF16)
    dy = dot_nt(datt_ref[...], wo_ref[...])
    gate = sigmoid(r_ref[...])
    dwkv_ref[...] = (dy * gate).astype(BF16)
    dr_ref[...] = (dy * wkv_ref[...].astype(F32) * gate * (1.0 - gate)).astype(BF16)
    for cols in col_chunks():
        retain = jnp.exp(-jnp.exp(vec_ref[9:10, cols]))
        bonus = vec_ref[10:11, cols]
        a = st_ref[0, :GROUP, cols]
        b = st_ref[0, GROUP:, cols]
        for j in range(STEPS):
            rows = step_rows(j)
            key = k_ref[rows, cols].astype(F32)
            value = v_ref[rows, cols].astype(F32)
            own = jnp.exp(bonus + key)
            weight = jnp.exp(key)
            scale = 1.0 / (b + own)
            den[0, rows, cols] = scale
            den[1, rows, cols] = (a + own * value) * scale
            a = retain * a + weight * value
            b = retain * b + weight
        p = state_p[:, cols]
        q = state_q[:, cols]
        for j in reversed(range(STEPS)):
            rows = step_rows(j)
            grad = dwkv_ref[rows, cols].astype(F32) * den[0, rows, cols]
            p = grad + retain * p
            q = retain * q - grad * den[1, rows, cols]
        state_p[:, cols] = p
        state_q[:, cols] = q

    @pl.when(i == count - 1)
    def _():
        first_ref[:GROUP, :] = state_p[...]
        first_ref[GROUP:, :] = state_q[...]
        rate = -jnp.exp(vec_ref[9:10, :])
        decay = jnp.exp(rate * float(STEPS * count))
        for q in range(2 * GROUP // CHUNKS):
            base = q * CHUNKS
            total = first_ref[base + CHUNKS - 1 : base + CHUNKS, :]
            for s in reversed(range(CHUNKS - 1)):
                total = decay * total + first_ref[base + s : base + s + 1, :]
            total_ref[q : q + 1, :] = total


def wkv_back_kernel(
    k_ref, v_ref, dwkv_ref, dr_ref, st_ref, vec_ref, later_ref, first_ref, w_ref,
    dk_ref, dv_ref, vsum_ref, edge_ref,
    past_a, past_b, state_p, state_q,
):
    i = pl.program_id(0)
    count = pl.num_programs(0)

    @pl.when(i == 0)
    def _():
        vsum_ref[...] = jnp.zeros_like(vsum_ref)
        rate = -jnp.exp(vec_ref[9:10, :])
        decay = jnp.exp(rate * float(STEPS * count))
        for q in range(2 * GROUP // CHUNKS):
            state = later_ref[q : q + 1, :]
            target = state_p if q < GROUP // CHUNKS else state_q
            base = (q % (GROUP // CHUNKS)) * CHUNKS
            for s in reversed(range(CHUNKS)):
                target[base + s : base + s + 1, :] = state
                state = decay * state + first_ref[q * CHUNKS + s : q * CHUNKS + s + 1, :]

    for cols in col_chunks():
        retain = jnp.exp(-jnp.exp(vec_ref[9:10, cols]))
        bonus = vec_ref[10:11, cols]
        a = st_ref[0, :GROUP, cols]
        b = st_ref[0, GROUP:, cols]
        for j in range(STEPS):
            rows = step_rows(j)
            weight = jnp.exp(k_ref[rows, cols].astype(F32))
            past_a[rows, cols] = a
            past_b[rows, cols] = b
            a = retain * a + weight * v_ref[rows, cols].astype(F32)
            b = retain * b + weight
        p = state_p[:, cols]
        q = state_q[:, cols]
        sum_decay = jnp.zeros((GROUP, COLS), F32)
        sum_bonus = jnp.zeros((GROUP, COLS), F32)
        for j in reversed(range(STEPS)):
            rows = step_rows(j)
            key = k_ref[rows, cols].astype(F32)
            value = v_ref[rows, cols].astype(F32)
            own = jnp.exp(bonus + key)
            weight = jnp.exp(key)
            a = past_a[rows, cols]
            b = past_b[rows, cols]
            scale = 1.0 / (b + own)
            wkv = (a + own * value) * scale
            grad = dwkv_ref[rows, cols].astype(F32) * scale
            own_grad = grad * own
            bonus_term = own_grad * (value - wkv)
            dv_ref[rows, cols] = (own_grad + weight * p).astype(BF16)
            dk_ref[rows, cols] = (bonus_term + weight * (value * p + q)).astype(BF16)
            sum_decay += a * p + b * q
            sum_bonus += bonus_term
            p = grad + retain * p
            q = retain * q - grad * wkv
        state_p[:, cols] = p
        state_q[:, cols] = q
        scaled = jnp.sum(sum_decay, axis=0, keepdims=True) * retain * -jnp.exp(vec_ref[9:10, cols])
        vsum_ref[0:1, cols] += scaled
        vsum_ref[1:2, cols] += jnp.sum(sum_bonus, axis=0, keepdims=True)

    @pl.when(i == count - 1)
    def _():
        rows = slice(0, GROUP)
        edge = dot_nt(dk_ref[rows, :], w_ref[:, :EMBED]) * (1.0 - vec_ref[4:5, :])
        edge += dot_nt(dv_ref[rows, :], w_ref[:, EMBED : 2 * EMBED]) * (1.0 - vec_ref[5:6, :])
        edge += dot_nt(dr_ref[rows, :], w_ref[:, 2 * EMBED :]) * (1.0 - vec_ref[6:7, :])
        edge_ref[...] = edge


def input_back_kernel(
    dk_ref, dv_ref, dr_ref, w_ref, xp_ref, before_ref, edge_ref, later_ref, dx1_ref, vec_ref,
    out_ref, vsum_ref, carry,
):
    i = pl.program_id(0)
    count = pl.num_programs(0)

    @pl.when(i == 0)
    def _():
        carry[...] = later_ref[...]
        vsum_ref[...] = jnp.zeros_like(vsum_ref)

    gain = vec_ref[0:1, :]
    offset = vec_ref[1:2, :]
    n, rstd = normalize(xp_ref[...].astype(F32))
    h = n * gain + offset
    n_before, _ = normalize(before_ref[...].astype(F32))
    h_before = jnp.where(i == count - 1, edge_ref[...], n_before * gain + offset)
    diff = h - jnp.concatenate([h_before, h[:-GROUP]], axis=0)
    dh = jnp.zeros((ROWS, EMBED), F32)
    shift = jnp.zeros((ROWS, EMBED), F32)
    for at, grad_ref in enumerate((dk_ref, dv_ref, dr_ref)):
        back = dot_nt(grad_ref[...], w_ref[:, at * EMBED : (at + 1) * EMBED])
        share = vec_ref[4 + at : 5 + at, :]
        vsum_ref[2 + at : 3 + at, :] += jnp.sum(back * diff, axis=0, keepdims=True)
        kept = back * share
        dh += kept
        shift += back - kept
    dh += jnp.concatenate([shift[GROUP:], carry[...]], axis=0)
    carry[...] = shift[:GROUP]
    vsum_ref[0:1, :] += jnp.sum(dh * n, axis=0, keepdims=True)
    vsum_ref[1:2, :] += jnp.sum(dh, axis=0, keepdims=True)
    out_ref[...] = swap_out((dx1_ref[...] + norm_back(dh * gain, n, rstd)).astype(BF16))


def adam_step(master, moment, second, gradient, rate, shrink):
    moment_new = 0.9 * moment + 0.1 * gradient
    second_new = 0.95 * second + 0.05 * gradient * gradient
    scaled = moment_new / (1.0 - 0.9**STEP) / (jnp.sqrt(second_new / (1.0 - 0.95**STEP)) + 1e-08)
    return (master - rate * (scaled + shrink * master), moment_new, second_new)


def neighbour(block, axis, distance):
    devices = range(lax.axis_size(axis))
    return lax.ppermute(block, axis, [(i, i + distance) for i in devices if i + distance in devices])


def everyone(block, axis):
    count = lax.axis_size(axis)
    return lax.all_to_all(
        jnp.broadcast_to(block[None], (count,) + block.shape), axis, 0, 0, tiled=True
    )


def gather_rows(weight):
    part = lax.all_gather(weight.astype(BF16), "rep", axis=0, tiled=True)
    return lax.all_gather(part, "tok", axis=0, tiled=True)


def scatter_rows(grad):
    part = lax.psum_scatter(grad.astype(BF16), "tok", scatter_dimension=0, tiled=True)
    return lax.psum_scatter(part, "rep", scatter_dimension=0, tiled=True).astype(F32)


def weight_grad(a, b):
    return lax.dot_general(a, b, (((0,), (0,)), ((), ())), preferred_element_type=F32).astype(BF16)


def on_device(
    tokens, cotangent, init_num, init_den, prev_att, seg_doc, w_kvr, w_out, f_kr, f_value, vectors,
    m_kvr, v_kvr, m_out, v_out, m_fkr, v_fkr, m_fvalue, v_fvalue, vec_m, vec_v,
):
    tok_count = lax.axis_size("tok")
    rep_count = lax.axis_size("rep")
    here = lax.axis_index("tok")
    flat_index = here * rep_count + lax.axis_index("rep")
    micro, _, local_len, _ = tokens.shape
    seg_count = seg_doc.shape[2]
    chunk = local_len // CHUNKS
    blocks = chunk // STEPS
    rows = micro * local_len

    kvr = gather_rows(w_kvr)
    out = gather_rows(w_out)
    fkr = gather_rows(f_kr)
    fvalue = gather_rows(f_value)

    documents = seg_doc[:, 0, :]
    marker = jnp.concatenate(
        [jnp.ones((micro, 1), jnp.bool_), documents[:, 1:] != documents[:, :-1]], axis=1
    )
    starts = jnp.arange(tok_count) * local_len
    fresh = jnp.logical_and(marker[:, starts // SEG_LEN], (starts % SEG_LEN == 0)[None, :])
    fresh_here = lax.dynamic_index_in_dim(fresh, here, 1, keepdims=True)
    seg_here = here * local_len // SEG_LEN
    prev_here = lax.dynamic_index_in_dim(prev_att[:, 0], seg_here, 1, keepdims=False).astype(F32)
    num_all = lax.all_gather(init_num[:, 0], "tok", axis=2, tiled=True)
    den_all = lax.all_gather(init_den[:, 0], "tok", axis=2, tiled=True)
    init_all = jnp.concatenate([num_all, den_all], axis=0)
    rate = -jnp.exp(vectors[9:10])
    fade = jnp.exp(rate * float(local_len))
    fresh_four = jnp.concatenate([fresh, fresh], axis=0)

    x4 = tokens.reshape(micro, CHUNKS, chunk, EMBED)
    c4 = cotangent.reshape(micro, CHUNKS, chunk, EMBED)

    def edge_back(last, incoming):
        moved = jnp.concatenate([incoming[:, None], last.reshape(micro, CHUNKS, EMBED)[:, :-1]], axis=1)
        return moved.reshape(GROUP, EMBED)

    def edge_forward(first, incoming):
        moved = jnp.concatenate([first.reshape(micro, CHUNKS, EMBED)[:, 1:], incoming[:, None]], axis=1)
        return moved.reshape(GROUP, EMBED)

    raw_in = neighbour(tokens[:, 0, -1, :], "tok", 1)
    raw_edge = edge_back(x4[:, :, -1, :], raw_in).astype(F32)
    edge_n, _ = normalize(raw_edge)
    edge_h = edge_n * vectors[0:1] + vectors[1:2]
    first_row = (jnp.arange(GROUP) % CHUNKS == 0)[:, None]
    fresh_rows = jnp.repeat(fresh_here[:, 0], CHUNKS)[:, None]
    replace = jnp.logical_and(first_row, fresh_rows)
    edge_one = jnp.where(replace, jnp.repeat(prev_here, CHUNKS, axis=0), edge_h)

    def up(width):
        return pl.BlockSpec((ROWS, width), lambda i: (i, 0))

    def down(width):
        return pl.BlockSpec((ROWS, width), lambda i: (blocks - 1 - i, 0))

    before_spec = pl.BlockSpec(
        (GROUP, EMBED), lambda i: (jnp.maximum((blocks - 1 - i) * STEPS - 1, 0), 0)
    )
    natural_up = pl.BlockSpec((micro, CHUNKS, STEPS, EMBED), lambda i: (0, 0, i, 0))
    natural_down = pl.BlockSpec((micro, CHUNKS, STEPS, EMBED), lambda i: (0, 0, blocks - 1 - i, 0))
    st_up = pl.BlockSpec((1, 2 * GROUP, EMBED), lambda i: (i, 0, 0))
    st_down = pl.BlockSpec((1, 2 * GROUP, EMBED), lambda i: (blocks - 1 - i, 0, 0))
    vec_spec = full(vectors.shape)
    edge_spec = full((GROUP, EMBED))
    state_spec = full((2 * GROUP, EMBED))
    total_spec = full((2 * micro, EMBED))
    sum_spec = full((8, EMBED))

    def like(width, dtype):
        return jax.ShapeDtypeStruct((rows, width), dtype)

    def small(count, dtype=F32):
        return jax.ShapeDtypeStruct((count, EMBED), dtype)

    state = pltpu.VMEM((GROUP, EMBED), F32)
    square = 2 * rows * EMBED * EMBED

    xp, xk, xv, xr, k, v, r, ends, totals = call(
        mix_one_kernel, blocks,
        [natural_up, edge_spec, vec_spec, full((EMBED, 3 * EMBED))],
        [up(EMBED)] * 7 + [state_spec, total_spec],
        [like(EMBED, BF16)] * 6 + [like(EMBED, F32), small(2 * GROUP), small(2 * micro)],
        [state] * 3, 4 * square, "mix_one",
    )(x4, edge_one, vectors, kvr)

    every = everyone(totals, "tok")
    carried = jnp.zeros((2 * micro, EMBED), F32)
    begin = jnp.zeros((2 * micro, EMBED), F32)
    for d in range(tok_count):
        seg = d * local_len // SEG_LEN
        carried = jnp.where(fresh_four[:, d : d + 1], init_all[:, seg], carried)
        begin = jnp.where(here == d, carried, begin)
        carried = fade * carried + every[d]

    wkv, y, x1, xk2, xr2, saved, first_two, last_two = call(
        wkv_kernel, blocks,
        [up(EMBED)] * 4 + [vec_spec, total_spec, state_spec, full((EMBED, EMBED))],
        [up(EMBED)] * 5 + [st_up, edge_spec, edge_spec],
        [like(EMBED, BF16), like(EMBED, BF16), like(EMBED, F32), like(EMBED, BF16), like(EMBED, BF16),
         jax.ShapeDtypeStruct((blocks, 2 * GROUP, EMBED), F32), small(GROUP), small(GROUP)],
        [state] * 3, 2 * square, "wkv",
    )(k, v, r, xp, vectors, begin, ends, out)

    row_in = neighbour(last_two.reshape(micro, CHUNKS, EMBED)[:, -1], "tok", 1)
    edge_two = jnp.where(replace, 0.0, edge_back(last_two, row_in))
    diff_two = first_two - edge_two
    xk2 = xk2.at[:GROUP].set((edge_two + diff_two * vectors[7:8]).astype(BF16))
    xr2 = xr2.at[:GROUP].set((edge_two + diff_two * vectors[8:9]).astype(BF16))

    kq, gate = call(
        hidden_kernel, blocks,
        [up(EMBED), up(EMBED), full((EMBED, FF + EMBED))],
        [up(FF), up(EMBED)],
        [like(FF, BF16), like(EMBED, F32)],
        [], 5 * square, "hidden",
    )(xk2, xr2, fkr)

    mixed, dvf, drf, dkf, cp = call(
        value_kernel, blocks,
        [up(FF), up(EMBED), up(EMBED), natural_up, full((FF, EMBED))],
        [natural_up, up(EMBED), up(EMBED), up(FF), up(EMBED)],
        [jax.ShapeDtypeStruct(x4.shape, BF16), like(EMBED, BF16), like(EMBED, BF16), like(FF, BF16),
         like(EMBED, BF16)],
        [], 9 * square, "value",
    )(kq, gate, x1, c4, fvalue)

    shift_two = dot_nt(dkf[:GROUP], fkr[:, :FF]) * (1.0 - vectors[7:8])
    shift_two += dot_nt(drf[:GROUP], fkr[:, FF:]) * (1.0 - vectors[8:9])

    def from_right(shift):
        incoming = neighbour(
            jnp.where(fresh_here, 0.0, shift.reshape(micro, CHUNKS, EMBED)[:, 0]), "tok", -1
        )
        return edge_forward(shift, incoming)

    later_two = from_right(shift_two)
    grad_fvalue = weight_grad(kq, dvf)
    grad_fkr = jnp.concatenate([weight_grad(xk2, dkf), weight_grad(xr2, drf)], axis=1)

    dx1, datt, dwkv, dr, vsum_two, firsts, back_totals = call(
        middle_back_kernel, blocks,
        [down(FF), down(EMBED), full((EMBED, FF + EMBED)), down(EMBED), before_spec, edge_spec,
         edge_spec, down(EMBED), vec_spec, full((EMBED, EMBED))] + [down(EMBED)] * 4 + [st_down],
        [down(EMBED)] * 4 + [sum_spec, state_spec, total_spec],
        [like(EMBED, F32), like(EMBED, BF16), like(EMBED, BF16), like(EMBED, BF16), small(8),
         small(2 * GROUP), small(2 * micro)],
        [state, pltpu.VMEM((2, ROWS, EMBED), F32), state, state], 6 * square, "middle_back",
    )(dkf, drf, fkr, x1, x1, edge_two, later_two, cp, vectors, out, k, v, r, wkv, saved)

    every_back = everyone(back_totals, "tok")
    grad_out = weight_grad(y, datt)
    grad_r = weight_grad(xr, dr)
    carried = jnp.zeros((2 * micro, EMBED), F32)
    later = jnp.zeros((2 * micro, EMBED), F32)
    for d in reversed(range(tok_count)):
        later = jnp.where(here == d, carried, later)
        carried = jnp.where(fresh_four[:, d : d + 1], 0.0, fade * carried + every_back[d])

    dk, dv, vsum_wkv, shift_one = call(
        wkv_back_kernel, blocks,
        [down(EMBED)] * 4 + [st_down, vec_spec, total_spec, state_spec, full((EMBED, 3 * EMBED))],
        [down(EMBED), down(EMBED), sum_spec, edge_spec],
        [like(EMBED, BF16), like(EMBED, BF16), small(8), small(GROUP)],
        [pltpu.VMEM((ROWS, EMBED), F32)] * 2 + [state] * 2, square, "wkv_back",
    )(k, v, dwkv, dr, saved, vectors, later, firsts, kvr)

    later_one = from_right(shift_one)
    grad_kvr = jnp.concatenate([weight_grad(xk, dk), weight_grad(xv, dv), grad_r], axis=1)

    token_grad, vsum_one = call(
        input_back_kernel, blocks,
        [down(EMBED)] * 3 + [full((EMBED, 3 * EMBED)), down(EMBED), before_spec, edge_spec, edge_spec,
         down(EMBED), vec_spec],
        [natural_down, sum_spec],
        [jax.ShapeDtypeStruct(x4.shape, BF16), small(8)],
        [state], 3 * square, "input_back",
    )(dk, dv, dr, kvr, xp, xp, edge_one, later_one, dx1, vectors)

    grad_vec = jnp.concatenate(
        [vsum_one[0:2], vsum_two[0:2], vsum_one[2:5], vsum_two[2:4], vsum_wkv[0:2]], axis=0
    )
    columns = vec_m.shape[1]
    pieces = jnp.moveaxis(grad_vec.reshape(vectors.shape[0], tok_count * rep_count, columns), 1, 0)
    sum_vec = jnp.sum(lax.all_to_all(pieces, ("tok", "rep"), 0, 0, tiled=True), axis=0)

    sum_kvr = scatter_rows(grad_kvr)
    sum_out = scatter_rows(grad_out)
    sum_fkr = scatter_rows(grad_fkr)
    sum_fvalue = scatter_rows(grad_fvalue)

    base_rate = 2.5 / math.sqrt(EMBED)
    new_kvr = adam_step(w_kvr, m_kvr, v_kvr, sum_kvr, base_rate, 0.01)
    new_out = adam_step(w_out, m_out, v_out, sum_out, 4.0 * base_rate, 0.01)
    new_fkr = adam_step(f_kr, m_fkr, v_fkr, sum_fkr, base_rate, 0.01)
    new_fvalue = adam_step(f_value, m_fvalue, v_fvalue, sum_fvalue, 2.5 / math.sqrt(FF), 0.01)
    vec_master = lax.dynamic_slice_in_dim(vectors, flat_index * columns, columns, 1)
    vec_rates = jnp.array([0.6, 0.3, 0.6, 0.3, 0.3, 0.3, 0.3, 0.3, 0.3, 3.0, 0.5], F32)[:, None]
    new_vectors = adam_step(vec_master, vec_m, vec_v, sum_vec, vec_rates, 0.0)
    shape = tokens.shape
    return (
        (mixed.reshape(shape), token_grad.reshape(shape))
        + new_kvr + new_out + new_fkr + new_fvalue + new_vectors
    )


def solution(mesh):
    rows = P(("tok", "rep"), None)
    columns = P(None, ("tok", "rep"))
    token_spec = P(None, "rep", "tok", None)
    channel_spec = P(None, "rep", None, "tok")
    placed = (
        (token_spec, token_spec, channel_spec, channel_spec, P(None, "rep", None, None), P(None, "rep", None))
        + (rows,) * 4 + (P(),) + (rows,) * 8 + (columns,) * 2
    )
    return jax.shard_map(
        on_device,
        mesh=mesh,
        in_specs=placed,
        out_specs=(token_spec, token_spec) + (rows,) * 12 + (columns,) * 3,
        check_vma=False,
    )
```

time: 2050 us -> 766 us (0.37)
  other arithmetic: 629 us -> 43.6 us
  local copies, waits for them, and re-layouts: 439 us -> 22.2 us
  matrix products: 402 us -> 55.5 us
  Pallas kernels: 0 us -> 139 us
  starting transfers between devices: 70.7 us -> 23.1 us
  waiting for transfers between devices: 442 us -> 397 us
  blocking collectives: 36.7 us -> 63.5 us
    dot_general x56 -> x9, matrix products: 402 us -> 55.5 us  [the longest x7 47.5 us: weight_grad(): lax.dot_general(a, b, (((0,), (0,)), ((), ())), preferred_element_type=F32)]
    unnamed x25 -> x0, other arithmetic: 199 us -> none
    pallas_call x0 -> x7, Pallas kernels: none -> 139 us  [the longest x1 31.6 us: on_device(): call(middle_back_kernel, blocks, [down(FF), down(EMBED), full((EMBED, FF...]
    convert_element_type x34 -> x0, local copies, waits for them, and re-layouts: 121 us -> none  [the longest x6 19.5 us: run(): value_chan.astype(jnp.float32)]
    unnamed x494 -> x79, local copies, waits for them, and re-layouts: 127 us -> 13.2 us
    add x70 -> x0, other arithmetic: 82.9 us -> none  [the longest x64 80.6 us: block_step(): step_decay * denom + plus_den]
    add_any x75 -> x0, other arithmetic: 81.9 us -> none  [the longest x64 76.3 us: block_step(): step_decay * numer + plus_num]
    dynamic_update_slice x130 -> x0, other arithmetic: 81.4 us -> none  [the longest x128 80 us: wkv_by_block(): lax.scan(block_step, (zero_state, zero_state), scan_inputs)]
  transfers between devices with their start and end apart: 36 -> 21, of which waited for: 16 -> 17; matrix products, arithmetic and copies ran while one was open for 50% -> 13% of each run, Pallas kernels for 0% -> 10%
where the time goes in v1:
time: 766 us; the launch traced here: 759 us
  waiting for transfers between devices  397 us (52%)
  Pallas kernels  139 us (18%)
  blocking collectives  63.5 us (8%)
  matrix products  55.5 us (7%)
  other arithmetic  43.6 us (6%)
  starting transfers between devices  23.1 us (3%)
  local copies, waits for them, and re-layouts  22.2 us (3%)
  between operations  15.1 us (2%)
    reduce_scatter x3, waiting for transfers between devices, scatter_rows(): lax.psum_scatter(grad.astype(BF16), 'tok', scatter_dimension=0, tiled=True)  160 us
    all_gather x4, waiting for transfers between devices, gather_rows(): return lax.all_gather(part, 'tok', axis=0, tiled=True)  109 us
    reduce_scatter x4, waiting for transfers between devices, scatter_rows(): lax.psum_scatter(part, 'rep', scatter_dimension=0, tiled=True).astype(F32)  59 us
    dot_general x7, matrix products, weight_grad(): lax.dot_general(a, b, (((0,), (0,)), ((), ())), preferred_element_type=F32)  47.5 us
    all_gather x2, blocking collectives, gather_rows(): part = lax.all_gather(weight.astype(BF16), 'rep', axis=0, tiled=True)  45.4 us
    pallas_call x1, Pallas kernels, on_device(): call(middle_back_kernel, blocks, [down(FF), down(EMBED), full((EMBED, FF...  31.6 us
    pallas_call x1, Pallas kernels, on_device(): call(value_kernel, blocks, [up(FF), up(EMBED), up(EMBED), natural_up, ful...  29.7 us
    all_gather x2, waiting for transfers between devices, gather_rows(): part = lax.all_gather(weight.astype(BF16), 'rep', axis=0, tiled=True)  28.8 us
  transfers between devices with their start and end apart: 21, of which 17 were waited for; matrix products, arithmetic and copies ran while one was open for 13% of the time, Pallas kernels for 10%

profile of v1, /device:TPU:0, one launch (start us, length us, event | category | flops | bytes accessed | tf_op | source)
XLA Modules:
  0.0 759.0 jit_solution(17848076210690403689)
XLA Ops:
  11.1 28.5 %all_gather.30 = bf16[128,3072]{1,0:T(8,128)(2,1)} all-gather(bf16[32,3072]{1,0:T(8,128)(2,1)S(1)} %convert_element_type.72), channel_id=1, replica_groups=mesh['tok'=8,'rep'=4] {'rep'}, dimensions={0}, use_global_device_ids=true | all-gather | bytes 983040 | tf_op jit(solution)/shard_map/all_gather | solution.py:433
  39.7 16.9 %all_gather.34 = bf16[128,1024]{1,0:T(8,128)(2,1)} all-gather(bf16[32,1024]{1,0:T(8,128)(2,1)S(1)} %convert_element_type.73), channel_id=1, replica_groups=mesh['tok'=8,'rep'=4] {'rep'}, dimensions={0}, use_global_device_ids=true | all-gather | bytes 327680 | tf_op jit(solution)/shard_map/all_gather | solution.py:433
  57.3 28.8 %all-gather.17.cloned.1.call-done = bf16[512,1024]{1,0:T(8,128)(2,1)} async-done(((bf16[128,1024]{1,0:T(8,128)(2,1)}), bf16[512,1024]{1,0:T(8,128)(2,1)}) %all-gather.17.cloned.1.call-update) | async-done | bytes 1048592 | tf_op jit(solution)/shard_map/all_gather | solution.py:433
  90.8 9.2 %all-gather = f32[2,1,2,1024]{3,0,2,1:T(2,128)S(1)} all-gather(f32[2,1,2,128]{3,0,2,1:T(2,128)S(1)} %copy.119), channel_id=2, replica_groups=mesh['tok'=8,'rep'=4] {'tok'}, dimensions={3}, use_global_device_ids=true | all-gather | bytes 18432 | tf_op jit(solution)/shard_map/all_gather | solution.py:474
  101.1 9.0 %all-gather.1 = f32[2,1,2,1024]{3,0,2,1:T(2,128)S(1)} all-gather(f32[2,1,2,128]{3,0,2,1:T(2,128)S(1)} %copy.120), channel_id=3, replica_groups=mesh['tok'=8,'rep'=4] {'tok'}, dimensions={3}, use_global_device_ids=true | all-gather | bytes 18432 | tf_op jit(solution)/shard_map/all_gather | solution.py:475
  111.2 21.9 %all-gather.9.cloned.1.call-done.w_ref = bf16[1024,3072]{1,0:T(8,128)(2,1)} async-done(((bf16[128,3072]{1,0:T(8,128)(2,1)}), bf16[1024,3072]{1,0:T(8,128)(2,1)}) %all-gather.9.cloned.1.call-update) | async-done | bytes 6291472 | tf_op jit(solution)/shard_map/all_gather | solution.py:434
  133.1 15.1 %mix_one.1 = (bf16[1024,1024]{1,0:T(8,128)(2,1)}, bf16[1024,1024]{1,0:T(8,128)(2,1)}, bf16[1024,1024]{1,0:T(8,128)(2,1)}, bf16[1024,1024]{1,0:T(8,128)(2,1)}, bf...) custom-call(bf16[2,8,64,1024]{3,2,1,0:T(8,128)(2,1)} %bitcast.258, ...), custom_call_target="tpu_custom_call" | custom-call | flops 8589934592 | bytes 21474836 | tf_op jit(solution)/shard_map/mix_one/pallas_call | solution.py:529
  164.1 13.5 %wkv.1 = (bf16[1024,1024]{1,0:T(8,128)(2,1)}, bf16[1024,1024]{1,0:T(8,128)(2,1)}, f32[1024,1024]{1,0:T(8,128)}, bf16[1024,1024]{1,0:T(8,128)(2,1)}, bf16[1024,10...) custom-call(bf16[1024,1024]{1,0:T(8,128)(2,1)} %get-tuple-element.78.k_ref, ...), custom_call_target="tpu_custom_call" | custom-call | flops 4294967296 | bytes 10737418 | tf_op jit(solution)/shard_map/wkv/pallas_call | solution.py:546
  184.6 44.6 %all-gather.15.cloned.1.call-done.w_ref = bf16[1024,5120]{1,0:T(8,128)(2,1)} async-done(((bf16[128,5120]{1,0:T(8,128)(2,1)}), bf16[1024,5120]{1,0:T(8,128)(2,1)}) %all-gather.15.cloned.1.call-update) | async-done | bytes 10485776 | tf_op jit(solution)/shard_map/all_gather | solution.py:434
  229.2 17.3 %hidden.1 = (bf16[1024,4096]{1,0:T(8,128)(2,1)}, f32[1024,1024]{1,0:T(8,128)}) custom-call(bf16[1024,1024]{1,0:T(8,128)(2,1)} %fusion.33.xk_ref, bf16[1024,1024]{1,0:T(8,128)(2,1)} %get-tuple-element.215.xr_ref, bf16[1024,5120]{1,0:T(8,128)(2,1)} %all-gather.15.cloned.1.call-done.w_ref), custom_call_target="tpu_custom_call" | custom-call | flops 10737418240 | bytes 26843544 | tf_op jit(solution)/shard_map/hidden/pallas_call | solution.py:561
  246.5 38.9 %all-gather.19.cloned.1.call-done.w_ref = bf16[4096,1024]{1,0:T(8,128)(2,1)} async-done(((bf16[512,1024]{1,0:T(8,128)(2,1)}), bf16[4096,1024]{1,0:T(8,128)(2,1)}) %all-gather.19.cloned.1.call-update) | async-done | bytes 8388624 | tf_op jit(solution)/shard_map/all_gather | solution.py:434
  285.4 29.7 %value.1 = (bf16[2,8,64,1024]{3,2,1,0:T(8,128)(2,1)}, bf16[1024,1024]{1,0:T(8,128)(2,1)}, bf16[1024,1024]{1,0:T(8,128)(2,1)}, bf16[1024,4096]{1,0:T(8,128)(2,1)}, bf16[1024,1024]{1,0:T(8,128)(2,1)}) custom-call(bf16[1024,4096]{1,0:T(8,128)(2,1)} %get-tuple-element.88.kq_ref, f32[1024,1024]{1,0:T(8,128)} %get-tuple-element.89.gate_ref, ...), custom_call_target="tpu_custom_call" | custom-call | flops 19327352832 | bytes 48318384 | tf_op jit(solution)/shard_map/value/pallas_call | solution.py:569
  327.0 31.6 %middle_back.1 = (f32[1024,1024]{1,0:T(8,128)}, bf16[1024,1024]{1,0:T(8,128)(2,1)}, bf16[1024,1024]{1,0:T(8,128)(2,1)}, bf16[1024,1024]{1,0:T(8,128)(2,1)}, f32[...) custom-call(bf16[1024,4096]{1,0:T(8,128)(2,1)} %get-tuple-element.92.dkf_ref, ...), custom_call_target="tpu_custom_call" | custom-call | flops 12884901888 | bytes 32212254 | tf_op jit(solution)/shard_map/middle_back/pallas_call | solution.py:591
  376.3 13.9 %wkv_back.1 = (bf16[1024,1024]{1,0:T(8,128)(2,1)}, bf16[1024,1024]{1,0:T(8,128)(2,1)}, f32[8,1024]{1,0:T(8,128)}, f32[16,1024]{1,0:T(8,128)}) custom-call(bf16[1024,1024]{1,0:T(8,128)(2,1)} %get-tuple-element.78.k_ref, bf16[1024,1024]{1,0:T(8,128)(2,1)} %get-tuple-element.79.v_ref, bf16[1024,1024]{1,0:T(8,128)(2,1)} %get-tuple-element.97.dwkv_ref, ...), custom_call_target="tpu_custom_call" | custom-call | flops 2147483648 | bytes 5368709 | tf_op jit(solution)/shard_map/wkv_back/pallas_call | solution.py:610
  396.8 13.3 %pad_maximum_fusion.1 = bf16[1024,3072]{0,1:T(8,128)(2,1)} fusion(bf16[1024,1024]{0,1:T(8,128)(2,1)S(1)} %copy-done.3, bf16[1024,1024]{0,1:T(8,128)(2,1)S(1)} %convolution_convert_fusion.5, bf16[1024,1024]{0,1:T(8,128)(2,1)S(1)} %convolution_convert_fusion.6), kind=kLoop, calls=%fused_computation.6 | loop fusion | flops 18874368 | bytes 12582912 | tf_op jit(solution)/shard_map/concatenate | solution.py:619
  410.1 8.8 %copy.131 = bf16[1024,3072]{1,0:T(8,128)(2,1)} copy(bf16[1024,3072]{0,1:T(8,128)(2,1)} %pad_maximum_fusion.1) | data formatting | bytes 12582912
  420.5 14.6 %convolution_convert_fusion = bf16[4096,1024]{1,0:T(8,128)(2,1)} fusion(bf16[1024,4096]{1,0:T(8,128)(2,1)} %get-tuple-element.88.kq_ref, bf16[1024,1024]{1,0:T(8,128)(2,1)S(1)} %copy-done.33), kind=kOutput, calls=%fused_computation.4 | convolution fusion | flops 8594128896 | bytes 18874368 | tf_op jit(solution)/shard_map/dot_general | solution.py:443
  440.9 11.6 %convolution_convert_fusion.1 = bf16[1024,4096]{1,0:T(8,128)(2,1)S(1)} fusion(bf16[1024,1024]{1,0:T(8,128)(2,1)S(1)} %copy-done.29, bf16[1024,4096]{1,0:T(8,128)(2,1)} %get-tuple-element.92.dkf_ref), kind=kOutput, calls=%fused_computation.5 | convolution fusion | flops 8594128896 | bytes 18874368 | tf_op jit(solution)/shard_map/dot_general | solution.py:443
  461.0 21.0 %reduce-scatter.25.cloned.1.call-done = bf16[128,3072]{1,0:T(8,128)(2,1)} async-done(((bf16[1024,3072]{1,0:T(8,128)(2,1)}), bf16[128,3072]{1,0:T(8,128)(2,1)}) %reduce-scatter.25.cloned.1.call-update) | async-done | bytes 786448
  482.1 74.7 %reduce-scatter.21.cloned.1.call-done = bf16[512,1024]{1,0:T(8,128)(2,1)} async-done(((bf16[4096,1024]{1,0:T(8,128)(2,1)}), bf16[512,1024]{1,0:T(8,128)(2,1)}) %reduce-scatter.21.cloned.1.call-update) | async-done | bytes 1048592 | tf_op jit(solution)/shard_map/reduce_scatter | solution.py:438
  556.9 85.2 %reduce-scatter.17.cloned.1.call-done = bf16[128,5120]{1,0:T(8,128)(2,1)} async-done(((bf16[1024,5120]{1,0:T(8,128)(2,1)}), bf16[128,5120]{1,0:T(8,128)(2,1)}) %reduce-scatter.17.cloned.1.call-update) | async-done | bytes 1310736 | tf_op jit(solution)/shard_map/reduce_scatter | solution.py:438
  646.0 17.7 %input_back.1 = (bf16[2,8,64,1024]{3,2,1,0:T(8,128)(2,1)}, f32[8,1024]{1,0:T(8,128)}) custom-call(bf16[1024,1024]{1,0:T(8,128)(2,1)} %get-tuple-element.101.dk_ref, bf16[1024,1024]{1,0:T(8,128)(2,1)} %get-tuple-element.102.dv_ref, bf16[1024,1024]{1,0:T(8,128)(2,1)} %get-tuple-element.98.dr_ref, bf16[1024,3072]{1,0:T(8,128)(2,1)} %all-gather.9.cloned.1.call-done.w_ref, ...), custom_call_target="tpu_custom_call" | custom-call | flops 6442450944 | bytes 16106127 | tf_op jit(solution)/shard_map/input_back/pallas_call | solution.py:621
  690.6 26.8 %reduce-scatter.23.cloned.1.call-done = bf16[128,1024]{1,0:T(8,128)(2,1)} async-done(((bf16[512,1024]{1,0:T(8,128)(2,1)}), bf16[128,1024]{1,0:T(8,128)(2,1)}) %reduce-scatter.23.cloned.1.call-update) | async-done | bytes 262160 | tf_op jit(solution)/shard_map/reduce_scatter | solution.py:439
  719.7 29.8 %reduce-scatter.19.cloned.1.call-done = bf16[32,5120]{1,0:T(8,128)(2,1)} async-done(((bf16[128,5120]{1,0:T(8,128)(2,1)}), bf16[32,5120]{1,0:T(8,128)(2,1)}) %reduce-scatter.19.cloned.1.call-update) | async-done | bytes 327696 | tf_op jit(solution)/shard_map/reduce_scatter | solution.py:439
  (198 shorter events, 121.6 us)
Async XLA Ops:
  7.2 49.5 %all-gather.13.cloned.1.call-start = ((), (), s32[]{:S(2)}) async-start(), calls=%async_computation.13 | async-start | bytes 1638400 | tf_op jit(solution)/shard_map/all_gather | solution.py:433
  9.2 76.9 %all-gather.17.cloned.1.call-start = ((), (), s32[]{:S(2)}) async-start(), calls=%async_computation.15 | async-start | bytes 1310720 | tf_op jit(solution)/shard_map/all_gather | solution.py:433
  11.0 122.0 %all-gather.9.cloned.1.call-start = ((), (), s32[]{:S(2)}) async-start(), calls=%async_computation.11 | async-start | bytes 7077888 | tf_op jit(solution)/shard_map/all_gather | solution.py:434
  39.6 124.5 %all-gather.11.cloned.1.call-start = ((), (), s32[]{:S(2)}) async-start(), calls=%async_computation.12 | async-start | bytes 2359296 | tf_op jit(solution)/shard_map/all_gather | solution.py:434
  56.6 172.5 %all-gather.15.cloned.1.call-start = ((), (), s32[]{:S(2)}) async-start(), calls=%async_computation.14 | async-start | bytes 11796480 | tf_op jit(solution)/shard_map/all_gather | solution.py:434
  57.2 228.2 %all-gather.19.cloned.1.call-start = ((), (), s32[]{:S(2)}) async-start(), calls=%async_computation.16 | async-start | bytes 9437184 | tf_op jit(solution)/shard_map/all_gather | solution.py:434
  86.9 23.1 %collective-permute-start = (bf16[2,1024]{1,0:T(2,128)(2,1)S(1)}, bf16[2,1024]{1,0:T(2,128)(2,1)S(1)}, u32[]{:S(2)}, u32[]{:S(2)}) collective-permute-start(bf16[2,1024]{1,0:T(2,128)(2,1)S(1)} %bitcast.254), channel_id=1, source_target_pairs={{0,4},{4,8},{8,12},{12,16},{16,20},{20,24},{24,28},{1,5},{5,9},{9,... | collective-permute-start | bytes 12296 | tf_op jit(solution)/shard_map/ppermute | solution.py:422
  149.6 10.2 %all-to-all-start = ((f32[8,4,1024]{2,1,0:T(4,128)}), f32[8,4,1024]{2,1,0:T(4,128)S(1)}, u32[]{:S(2)}, u32[]{:S(2)}) async-start(f32[8,4,1024]{2,1,0:T(4,128)} %broadcast_in_dim.181), calls=%async_computation | async-start | bytes 262144 | tf_op jit(solution)/shard_map/all_to_all | solution.py:427
  153.0 307.4 %reduce-scatter.13.cloned.1.call-start = ((), (), s32[]{:S(2)}) async-start(), calls=%async_computation.17 | async-start | bytes 2359296 | tf_op jit(solution)/shard_map/reduce_scatter | solution.py:438
  178.6 3.0 collective-permute-start.1
  183.1 63.4 %copy-start.14 = (f32[16,1024]{1,0:T(8,128)}, f32[16,1024]{1,0:T(8,128)S(1)}, u32[]{:S(2)}) copy-start(f32[16,1024]{1,0:T(8,128)S(1)} %get-tuple-element.216.edge_ref) | copy-start | bytes 196612
  323.3 3.1 collective-permute-start.2
  364.6 10.9 %all-to-all-start.1 = ((f32[8,4,1024]{2,1,0:T(4,128)}), f32[8,4,1024]{2,1,0:T(4,128)S(1)}, u32[]{:S(2)}, u32[]{:S(2)}) async-start(f32[8,4,1024]{2,1,0:T(4,128)} %broadcast_in_dim.187), calls=%async_computation.1 | async-start | bytes 262144 | tf_op jit(solution)/shard_map/all_to_all | solution.py:427
  370.0 112.0 %reduce-scatter.25.cloned.1.call-start = ((), (), s32[]{:S(2)}) async-start(), calls=%async_computation.23 | async-start | bytes 7077888
  418.9 137.9 %reduce-scatter.21.cloned.1.call-start = ((), (), s32[]{:S(2)}) async-start(), calls=%async_computation.21 | async-start | bytes 9437184 | tf_op jit(solution)/shard_map/reduce_scatter | solution.py:438
  435.1 207.1 %reduce-scatter.17.cloned.1.call-start = ((), (), s32[]{:S(2)}) async-start(), calls=%async_computation.19 | async-start | bytes 11796480 | tf_op jit(solution)/shard_map/reduce_scatter | solution.py:438
  460.2 96.7 %copy-start.17 = (f32[16,1024]{1,0:T(8,128)S(1)}, f32[16,1024]{1,0:T(8,128)}, u32[]{:S(2)}) copy-start(f32[16,1024]{1,0:T(8,128)} %get-tuple-element.103) | copy-start | bytes 196612
  460.2 183.3 %copy-start.21 = (f32[8,1024]{1,0:T(8,128)S(1)}, f32[8,1024]{1,0:T(8,128)}, u32[]{:S(2)}) copy-start(f32[8,1024]{1,0:T(8,128)} %get-tuple-element.113) | copy-start | bytes 98308
  460.3 224.1 %reduce-scatter.15.cloned.1.call-start = ((), (), s32[]{:S(2)}) async-start(), calls=%async_computation.18 | async-start | bytes 327680 | tf_op jit(solution)/shard_map/reduce_scatter | solution.py:439
  461.0 227.5 %reduce-scatter.27.cloned.1.call-start = ((), (), s32[]{:S(2)}) async-start(), calls=%async_computation.24 | async-start | bytes 983040 | tf_op jit(solution)/shard_map/reduce_scatter | solution.py:439
  482.1 235.3 %reduce-scatter.23.cloned.1.call-start = ((), (), s32[]{:S(2)}) async-start(), calls=%async_computation.22 | async-start | bytes 1310720 | tf_op jit(solution)/shard_map/reduce_scatter | solution.py:439
  556.8 192.7 %reduce-scatter.19.cloned.1.call-start = ((), (), s32[]{:S(2)}) async-start(), calls=%async_computation.20 | async-start | bytes 1638400 | tf_op jit(solution)/shard_map/reduce_scatter | solution.py:439
  642.2 3.1 collective-permute-start.3
  666.5 15.0 %all-to-all-start.2 = ((f32[32,1,352]{2,1,0:T(1,128)}), f32[32,1,352]{2,1,0:T(1,128)S(1)}, u32[]{:S(2)}, u32[]{:S(2)}) async-start(f32[32,1,352]{2,1,0:T(1,128)} %reshape.288), calls=%async_computation.8 | async-start | bytes 98304 | tf_op jit(solution)/shard_map/all_to_all | solution.py:635
  (31 other events, 876.2 us)
Sparse Core Ops, SparseCore 0:
  10.2 45.6 all-gather.12
  58.0 28.0 all-gather.16
  88.0 45.0 all-gather.8
  134.8 29.2 all-gather.10
  165.9 63.2 all-gather.14
  230.9 54.4 all-gather.18
  364.0 43.8 reduce-scatter.12
  419.0 62.9 reduce-scatter.24
  485.5 71.2 reduce-scatter.20
  560.6 81.5 reduce-scatter.16
  644.5 19.5 reduce-scatter.14
  666.3 22.1 reduce-scatter.26
  690.7 26.5 reduce-scatter.22
  719.6 29.8 reduce-scatter.18

commit v2 on v1

v2 whole, which is shorter than its diff:
```python
import functools
import math

import jax
import jax.numpy as jnp
from jax import lax
from jax.experimental import pallas as pl
from jax.experimental.pallas import tpu as pltpu
from jax.sharding import PartitionSpec as P

EMBED = 1024
FF = 4096
SEG_LEN = 2048
STEP = 10
CHUNKS = 8
GROUP = 16
STEPS = 16
ROWS = STEPS * GROUP
COLS = 256
EPS = 1e-05
TINY = 1.2e-38
COSTS = dict(
    value=60, edge=14, grad_value=30, middle_back=60, grad_value_add_first=50, wkv_back=24, grad_value_merge=50,
    grad_hidden_add_first=50, grad_early_add_first=50, input_back_high=24,
)
F32 = jnp.float32
BF16 = jnp.bfloat16
MIB = 1024 * 1024
VMEM = dict(
    mix_one=30, wkv=28, hidden=36, value=60, edge=60, grad_value=60, middle_back=60, wkv_back=60, input_back_high=44,
    input_back_low=36,
)


def dot_nn(a, b):
    return jnp.dot(a, b, preferred_element_type=F32)


def dot_nt(a, b):
    return lax.dot_general(a, b, (((1,), (1,)), ((), ())), preferred_element_type=F32)


def dot_tn(a, b):
    return lax.dot_general(a, b, (((0,), (0,)), ((), ())), preferred_element_type=F32)


def sigmoid(v):
    return 0.5 * jnp.tanh(0.5 * v) + 0.5


def normalize(v):
    center = v - jnp.mean(v, axis=-1, keepdims=True)
    rstd = lax.rsqrt(jnp.mean(center * center, axis=-1, keepdims=True) + EPS)
    return center * rstd, rstd


def norm_back(e, n, rstd):
    return (e - jnp.mean(e, axis=-1, keepdims=True) - n * jnp.mean(e * n, axis=-1, keepdims=True)) * rstd


def swap_matrix():
    row = lax.broadcasted_iota(jnp.int32, (ROWS, ROWS), 0)
    col = lax.broadcasted_iota(jnp.int32, (ROWS, ROWS), 1)
    return jnp.where(col == (row % GROUP) * STEPS + row // GROUP, 1.0, 0.0).astype(BF16)


def swap_in(block):
    return dot_nn(swap_matrix(), block.reshape(ROWS, EMBED))


def swap_out(rows):
    moved = dot_nn(swap_matrix(), rows).astype(BF16)
    return moved.reshape(GROUP // CHUNKS, CHUNKS, STEPS, EMBED)


def part(at, count=1):
    return slice(at * EMBED, (at + count) * EMBED)


def col_chunks():
    return [slice(c * COLS, (c + 1) * COLS) for c in range(EMBED // COLS)]


def step_rows(j):
    return slice(j * GROUP, (j + 1) * GROUP)


def full(shape):
    return pl.BlockSpec(shape, lambda i: (0,) * len(shape), pipeline_mode=pl.Buffered(buffer_count=1))


def ordered(kernel, skip, count):
    return lambda *refs: kernel(*refs[:skip], *refs[skip + count :])


def cost(name):
    return pl.CostEstimate(flops=int(COSTS.get(name, 2) * 1e9), bytes_accessed=0, transcendentals=0)


def call(kernel, grid, in_specs, out_specs, out_shape, scratch, name, after=(), bits=None, weights=(), aliases=None):
    if weights:
        kernel = grouped(kernel, [len(pieces) for pieces in weights])
        in_specs = [SMEM_SPEC] + [ANY_SPEC] * sum(len(pieces) for pieces in weights) + in_specs
    made = pl.pallas_call(
        ordered(kernel, 0, len(after)),
        grid=(grid,),
        in_specs=[ANY_SPEC] * len(after) + in_specs,
        out_specs=out_specs,
        out_shape=out_shape,
        scratch_shapes=scratch,
        compiler_params=pltpu.CompilerParams(
            dimension_semantics=("arbitrary",), vmem_limit_bytes=VMEM.get(name, 16) * MIB
        ),
        cost_estimate=cost(name),
        input_output_aliases=aliases or {},
        name=name,
    )
    head = (bits,) + tuple(piece for pieces in weights for piece in pieces) if weights else ()
    return lambda *args: made(*after, *head, *args)


def grouped(kernel, counts):
    def run(bits_ref, *refs):
        groups = []
        for count in counts:
            groups.append(refs[:count])
            refs = refs[count:]
        return kernel(bits_ref, *groups, *refs)

    return run


SMEM_SPEC = pl.BlockSpec(memory_space=pltpu.SMEM)
ANY_SPEC = pl.BlockSpec(memory_space=pl.ANY)


def column_loads(pieces, target, sems, first, low, high, base=0, bits_ref=None):
    cols, place = slice(low, high), slice(low - base, high - base)
    if len(pieces) == 1:
        return [pltpu.make_async_copy(pieces[0].at[:, cols], target.at[:, place], sems.at[first])]
    copies = []
    height = target.shape[0] // 8
    for piece, core in zip(pieces, (bits_ref[0], 1 - bits_ref[0])):
        for q in range(4):
            rows = pl.ds(pl.multiple_of((2 * q + core) * height, height), height)
            copies.append(
                pltpu.make_async_copy(
                    piece.at[q * height : (q + 1) * height, cols], target.at[rows, place],
                    sems.at[first + len(copies)],
                )
            )
    return copies


def start_loads(*loads):
    @pl.when(pl.program_id(0) == 0)
    def _():
        for copies in loads:
            for copy in copies:
                copy.start()


def wait_all(copies):
    for copy in copies:
        copy.wait()


def wait_load(copies):
    pl.when(pl.program_id(0) == 0)(lambda: wait_all(copies))


def first_and_rest(body):
    pl.when(pl.program_id(0) == 0)(lambda: body(True))
    pl.when(pl.program_id(0) > 0)(lambda: body(False))


def mix_one_kernel(
    bits_ref, pieces, tok_ref, edge_ref, vec_ref,
    xp_ref, mix_ref, k_ref, v_ref, r_ref, end_ref, total_ref,
    carry, state_a, state_b, w_ref, sems,
):
    i = pl.program_id(0)
    loads = [
        column_loads(pieces, w_ref, sems, 16 * at, at * EMBED, (at + 1) * EMBED) for at in range(3)
    ]
    start_loads(*loads)

    @pl.when(i == 0)
    def _():
        carry[...] = edge_ref[...]
        state_a[...] = jnp.zeros_like(state_a)
        state_b[...] = jnp.zeros_like(state_b)

    xp_ref[...] = swap_in(tok_ref[...]).astype(BF16)
    hp = carry[...]
    for j in range(STEPS):
        rows = step_rows(j)
        n, _ = normalize(xp_ref[rows, :].astype(F32))
        h = n * vec_ref[0:1, :] + vec_ref[1:2, :]
        diff = h - hp
        for at in range(3):
            mix_ref[rows, part(at)] = (hp + diff * vec_ref[4 + at : 5 + at, :]).astype(BF16)
        hp = h
    carry[...] = hp

    def project(first):
        for at, out_ref in enumerate((k_ref, v_ref, r_ref)):
            if first:
                wait_all(loads[at])
            out_ref[...] = dot_nn(mix_ref[:, part(at)], w_ref[:, part(at)]).astype(out_ref.dtype)

    first_and_rest(project)
    for cols in col_chunks():
        retain = jnp.exp(-jnp.exp(vec_ref[9:10, cols]))
        a = state_a[:, cols]
        b = state_b[:, cols]
        for j in range(STEPS):
            weight = jnp.exp(k_ref[step_rows(j), cols].astype(F32))
            a = retain * a + weight * v_ref[step_rows(j), cols].astype(F32)
            b = retain * b + weight
        state_a[:, cols] = a
        state_b[:, cols] = b

    @pl.when(i == pl.num_programs(0) - 1)
    def _():
        end_ref[:GROUP, :] = state_a[...]
        end_ref[GROUP:, :] = state_b[...]
        rate = -jnp.exp(vec_ref[9:10, :])
        decay = jnp.exp(rate * float(STEPS * pl.num_programs(0)))
        for q in range(2 * GROUP // CHUNKS):
            total = end_ref[q * CHUNKS : q * CHUNKS + 1, :]
            for s in range(1, CHUNKS):
                total = decay * total + end_ref[q * CHUNKS + s : q * CHUNKS + s + 1, :]
            total_ref[q : q + 1, :] = total


def wkv_kernel(
    bits_ref, pieces, k_ref, v_ref, r_ref, xp_ref, vec_ref, start_ref, end_ref,
    wkv_ref, y_ref, x1_ref, mix_ref, st_ref, first_ref, last_ref,
    carry, state_a, state_b, w_ref, sems,
):
    i = pl.program_id(0)
    loads = column_loads(pieces, w_ref, sems, 0, 3 * EMBED, 4 * EMBED, 3 * EMBED)
    start_loads(loads)

    @pl.when(i == 0)
    def _():
        rate = -jnp.exp(vec_ref[9:10, :])
        decay = jnp.exp(rate * float(STEPS * pl.num_programs(0)))
        for q in range(2 * GROUP // CHUNKS):
            state = start_ref[q : q + 1, :]
            target = state_a if q < GROUP // CHUNKS else state_b
            base = (q % (GROUP // CHUNKS)) * CHUNKS
            for s in range(CHUNKS):
                target[base + s : base + s + 1, :] = state
                state = decay * state + end_ref[q * CHUNKS + s : q * CHUNKS + s + 1, :]
        carry[...] = jnp.zeros_like(carry)

    st_ref[0, :GROUP, :] = state_a[...]
    st_ref[0, GROUP:, :] = state_b[...]
    for cols in col_chunks():
        retain = jnp.exp(-jnp.exp(vec_ref[9:10, cols]))
        bonus = vec_ref[10:11, cols]
        a = state_a[:, cols]
        b = state_b[:, cols]
        for j in range(STEPS):
            rows = step_rows(j)
            key = k_ref[rows, cols].astype(F32)
            value = v_ref[rows, cols].astype(F32)
            own = jnp.exp(bonus + key)
            weight = jnp.exp(key)
            wkv = ((a + own * value) * pl.reciprocal(b + own)).astype(BF16)
            wkv_ref[rows, cols] = wkv
            y_ref[rows, cols] = (sigmoid(r_ref[rows, cols].astype(F32)) * wkv.astype(F32)).astype(BF16)
            a = retain * a + weight * value
            b = retain * b + weight
        state_a[:, cols] = a
        state_b[:, cols] = b
    wait_load(loads)
    x1_ref[...] = xp_ref[...].astype(F32) + dot_nn(y_ref[...], w_ref[...])
    hp = carry[...]
    for j in range(STEPS):
        rows = step_rows(j)
        n, _ = normalize(x1_ref[rows, :])
        h = n * vec_ref[2:3, :] + vec_ref[3:4, :]
        diff = h - hp
        for at in range(2):
            mix_ref[rows, part(at)] = (hp + diff * vec_ref[7 + at : 8 + at, :]).astype(BF16)
        if j == 0:

            @pl.when(i == 0)
            def _(h=h):
                first_ref[...] = h

        hp = h
    carry[...] = hp
    last_ref[...] = hp


def hidden_kernel(bits_ref, pieces, mix_ref, kq_ref, gate_ref, w_ref, sems):
    loads = [
        column_loads(pieces, w_ref, sems, 16 * at, at * EMBED, (at + 1) * EMBED) for at in range(5)
    ]
    start_loads(*loads)

    def project(first):
        for c in range(FF // EMBED):
            if first:
                wait_all(loads[c])
            active = jnp.maximum(dot_nn(mix_ref[:, part(0)], w_ref[:, part(c)]), 0.0)
            kq_ref[:, part(c)] = (active * active).astype(BF16)
        if first:
            wait_all(loads[4])
        gate_ref[...] = dot_nn(mix_ref[:, part(1)], w_ref[:, FF:]).astype(BF16)

    first_and_rest(project)


def rep_loads(bits_ref, pieces, target, sems, first, low):
    copies = []
    for at, piece in enumerate(pieces):
        high = bits_ref[4] if at % 2 == 0 else 1 - bits_ref[4]
        bit = bits_ref[3] if at < 2 else 1 - bits_ref[3]
        height = target.shape[0] // 32
        for block in range(8):
            rows = pl.ds(pl.multiple_of((4 * block + 2 * high + bit) * height, height), height)
            copies.append(
                pltpu.make_async_copy(
                    piece.at[block * height : (block + 1) * height, :], target.at[rows, low:],
                    sems.at[first + len(copies)],
                )
            )
    return copies


def value_kernel(
    bits_ref, pieces, others, kq_ref, gate_ref, x1_ref, cot_ref,
    mixed_ref, dvf_ref, grad_ref, cp_ref, w_ref, vf_ref, out_ref, sems,
):
    half = EMBED // 2
    if others:
        loads = [
            column_loads(pieces, w_ref, sems, 0, 0, half),
            rep_loads(bits_ref, others, w_ref, sems, 1, half),
        ]
    else:
        loads = [column_loads(pieces, w_ref, sems, at, at * half, (at + 1) * half) for at in range(2)]
    start_loads(*loads)
    cp_ref[...] = swap_in(cot_ref[...]).astype(BF16)

    def project(first):
        if not first:
            vf_ref[...] = dot_nn(kq_ref[...], w_ref[...])
            return
        for at in range(2):
            wait_all(loads[at])
            cols = slice(at * half, (at + 1) * half)
            vf_ref[:, cols] = dot_nn(kq_ref[...], w_ref[:, cols])

    first_and_rest(project)
    for j in range(STEPS):
        rows = step_rows(j)
        gate = sigmoid(gate_ref[rows, :].astype(F32))
        vf = vf_ref[rows, :]
        out_ref[rows, :] = (x1_ref[rows, :] + gate * vf).astype(BF16)
        scaled = cp_ref[rows, :].astype(F32) * gate
        dvf_ref[rows, :] = scaled.astype(BF16)
        grad_ref[rows, FF:] = (scaled * vf * (1.0 - gate)).astype(BF16)
    for c in range(FF // EMBED):
        back = dot_nt(dvf_ref[...], w_ref[part(c), :])
        square = kq_ref[:, part(c)].astype(F32)
        root = square * lax.rsqrt(jnp.maximum(square, TINY))
        grad_ref[:, part(c)] = (back * (2.0 * root)).astype(BF16)
    mixed_ref[...] = swap_out(out_ref[...])


def send_rows(flag_ref, shift, send_ref):
    for m in range(send_ref.shape[0]):
        row = shift[m * CHUNKS : m * CHUNKS + 1]
        send_ref[m : m + 1, :] = jnp.where(flag_ref[m] > 0, 0.0, row)


def take_rows(carry, shift_ref, got_ref):
    for m in range(got_ref.shape[0]):
        base = m * CHUNKS
        carry[base : base + CHUNKS - 1, :] = shift_ref[base + 1 : base + CHUNKS, :]
        carry[base + CHUNKS - 1 : base + CHUNKS, :] = got_ref[m : m + 1, :]


def edge_kernel(bits_ref, pieces, flag_ref, grad_ref, vec_ref, shift_ref, send_ref, w_ref, sems):
    loads = column_loads(pieces, w_ref, sems, 0, 0, FF + EMBED)
    start_loads(loads)
    wait_all(loads)
    shift = dot_nt(grad_ref[:, :FF], w_ref[:, :FF]) * (1.0 - vec_ref[7:8, :])
    shift += dot_nt(grad_ref[:, FF:], w_ref[:, FF:]) * (1.0 - vec_ref[8:9, :])
    shift_ref[...] = shift
    send_rows(flag_ref, shift, send_ref)


def add_sums(sums, values):
    for at, value in enumerate(values):
        sums[at] += value


def middle_back_kernel(weights, ins, outs, scratch, copies, grad):
    pieces, out_pieces = weights
    (
        grad_ref, x1_ref, before_ref, edge_ref, later_ref, got_ref, cp_ref, vec_ref, k_ref, v_ref, r_ref, wkv_ref,
        st_ref,
    ) = ins
    dx1_ref, out_ref, dwkv_ref, vsum_ref, first_ref, total_ref = outs
    carry, den, state_p, state_q, w_ref, wo_ref, dxk_ref, dxr_ref, sums, sems = scratch
    i = pl.program_id(0)
    count = pl.num_programs(0)
    loads = [
        column_loads((pieces,), w_ref, sems, 0, 0, FF + EMBED),
        column_loads((out_pieces,), wo_ref, sems, 16, 3 * EMBED, 4 * EMBED, 3 * EMBED),
    ]
    start_loads(*loads)

    @pl.when(i == 0)
    def _():
        take_rows(carry, later_ref, got_ref)
        sums[...] = jnp.zeros_like(sums)
        state_p[...] = jnp.zeros_like(state_p)
        state_q[...] = jnp.zeros_like(state_q)

    for cols in col_chunks():
        retain = jnp.exp(-jnp.exp(vec_ref[9:10, cols]))
        bonus = vec_ref[10:11, cols]
        a = st_ref[0, :GROUP, cols]
        b = st_ref[0, GROUP:, cols]
        for j in range(STEPS):
            rows = step_rows(j)
            key = k_ref[rows, cols].astype(F32)
            value = v_ref[rows, cols].astype(F32)
            own = jnp.exp(bonus + key)
            weight = jnp.exp(key)
            scale = pl.reciprocal(b + own)
            den[0, rows, cols] = scale
            den[1, rows, cols] = (a + own * value) * scale
            a = retain * a + weight * value
            b = retain * b + weight
    wait_load(loads[0] + loads[1] + copies)
    dxk_ref[...] = dot_nt(grad_ref[:, :FF], w_ref[:, :FF])
    dxr_ref[...] = dot_nt(grad_ref[:, FF:], w_ref[:, FF:])
    grad()
    gain = vec_ref[2:3, :]
    offset = vec_ref[3:4, :]
    share_k = vec_ref[7:8, :]
    share_r = vec_ref[8:9, :]
    n, rstd = normalize(x1_ref[step_rows(STEPS - 1), :])
    later = carry[...]
    for j in reversed(range(STEPS)):
        rows = step_rows(j)
        if j > 0:
            n_next, rstd_next = normalize(x1_ref[step_rows(j - 1), :])
            h_before = n_next * gain + offset
        else:
            n_before, _ = normalize(before_ref[...])
            h_before = jnp.where(i == count - 1, edge_ref[...], n_before * gain + offset)
        diff = n * gain + offset - h_before
        dxk = dxk_ref[rows, :]
        dxr = dxr_ref[rows, :]
        kept_k = dxk * share_k
        kept_r = dxr * share_r
        dh = kept_k + kept_r + later
        later = (dxk - kept_k) + (dxr - kept_r)
        add_sums(sums, (dh * n, dh, dxk * diff, dxr * diff))
        dx1 = cp_ref[rows, :].astype(F32) + norm_back(dh * gain, n, rstd)
        dx1_ref[rows, :] = dx1
        out_ref[rows, part(0)] = dx1.astype(BF16)
        if j > 0:
            n, rstd = n_next, rstd_next
    carry[...] = later
    dxk_ref[...] = dot_nt(out_ref[:, part(0)], wo_ref[...])
    for cols in col_chunks():
        retain = jnp.exp(-jnp.exp(vec_ref[9:10, cols]))
        right = slice(EMBED + cols.start, EMBED + cols.stop)
        p = state_p[:, cols]
        q = state_q[:, cols]
        for j in reversed(range(STEPS)):
            rows = step_rows(j)
            gate = sigmoid(r_ref[rows, cols].astype(F32))
            scaled = dxk_ref[rows, cols] * gate
            dwkv = scaled.astype(BF16)
            dwkv_ref[rows, cols] = dwkv
            out_ref[rows, right] = (scaled * wkv_ref[rows, cols].astype(F32) * (1.0 - gate)).astype(BF16)
            grad = dwkv.astype(F32) * den[0, rows, cols]
            p = grad + retain * p
            q = retain * q - grad * den[1, rows, cols]
        state_p[:, cols] = p
        state_q[:, cols] = q

    @pl.when(i == count - 1)
    def _():
        vsum_ref[...] = jnp.zeros_like(vsum_ref)
        for at in range(4):
            vsum_ref[at : at + 1, :] = jnp.sum(sums[at], axis=0, keepdims=True)
        first_ref[:GROUP, :] = state_p[...]
        first_ref[GROUP:, :] = state_q[...]
        rate = -jnp.exp(vec_ref[9:10, :])
        decay = jnp.exp(rate * float(STEPS * count))
        for q in range(2 * GROUP // CHUNKS):
            base = q * CHUNKS
            total = first_ref[base + CHUNKS - 1 : base + CHUNKS, :]
            for s in reversed(range(CHUNKS - 1)):
                total = decay * total + first_ref[base + s : base + s + 1, :]
            for d in range(total_ref.shape[0]):
                total_ref[d, q : q + 1, :] = total


def wkv_back_kernel(weights, ins, outs, scratch, copies, grad):
    (pieces,) = weights
    flag_ref, k_ref, v_ref, dwkv_ref, dr_ref, st_ref, vec_ref, every_ref, first_ref = ins
    out_ref, vsum_ref, edge_ref, send_ref = outs
    past_a, past_b, state_p, state_q, sums, w_ref, sems = scratch
    i = pl.program_id(0)
    count = pl.num_programs(0)
    loads = column_loads((pieces,), w_ref, sems, 0, 0, 3 * EMBED)
    start_loads(loads)

    @pl.when(i == 0)
    def _():
        sums[...] = jnp.zeros_like(sums)
        rate = -jnp.exp(vec_ref[9:10, :])
        decay = jnp.exp(rate * float(STEPS * count))
        devices, four, _ = every_ref.shape
        micro = four // 2
        whole = jnp.exp(rate * float(STEPS * count * CHUNKS))
        for q in range(2 * GROUP // CHUNKS):
            state = jnp.zeros((1, EMBED), F32)
            passed = state
            for d in reversed(range(devices)):
                state = jnp.where(flag_ref[micro] == d, passed, state)
                begins = flag_ref[micro + 1 + d * micro + q % micro]
                passed = jnp.where(begins > 0, 0.0, whole * passed + every_ref[d, q : q + 1, :])
            target = state_p if q < GROUP // CHUNKS else state_q
            base = (q % (GROUP // CHUNKS)) * CHUNKS
            for s in reversed(range(CHUNKS)):
                target[base + s : base + s + 1, :] = state
                state = decay * state + first_ref[q * CHUNKS + s : q * CHUNKS + s + 1, :]

    wait_load(copies)
    grad()
    for cols in col_chunks():
        right = slice(EMBED + cols.start, EMBED + cols.stop)
        retain = jnp.exp(-jnp.exp(vec_ref[9:10, cols]))
        bonus = vec_ref[10:11, cols]
        a = st_ref[0, :GROUP, cols]
        b = st_ref[0, GROUP:, cols]
        for j in range(STEPS):
            rows = step_rows(j)
            weight = jnp.exp(k_ref[rows, cols].astype(F32))
            past_a[rows, cols] = a
            past_b[rows, cols] = b
            a = retain * a + weight * v_ref[rows, cols].astype(F32)
            b = retain * b + weight
        p = state_p[:, cols]
        q = state_q[:, cols]
        sum_decay = sums[0, :, cols]
        sum_bonus = sums[1, :, cols]
        for j in reversed(range(STEPS)):
            rows = step_rows(j)
            key = k_ref[rows, cols].astype(F32)
            value = v_ref[rows, cols].astype(F32)
            own = jnp.exp(bonus + key)
            weight = jnp.exp(key)
            a = past_a[rows, cols]
            b = past_b[rows, cols]
            scale = pl.reciprocal(b + own)
            wkv = (a + own * value) * scale
            grad = dwkv_ref[rows, cols].astype(F32) * scale
            own_grad = grad * own
            bonus_term = own_grad * (value - wkv)
            out_ref[rows, cols] = (bonus_term + weight * (value * p + q)).astype(BF16)
            out_ref[rows, right] = (own_grad + weight * p).astype(BF16)
            sum_decay += a * p + b * q
            sum_bonus += bonus_term
            p = grad + retain * p
            q = retain * q - grad * wkv
        state_p[:, cols] = p
        state_q[:, cols] = q
        sums[0, :, cols] = sum_decay
        sums[1, :, cols] = sum_bonus

    @pl.when(i == count - 1)
    def _():
        rate = -jnp.exp(vec_ref[9:10, :])
        vsum_ref[...] = jnp.zeros_like(vsum_ref)
        vsum_ref[0:1, :] = jnp.sum(sums[0], axis=0, keepdims=True) * jnp.exp(rate) * rate
        vsum_ref[1:2, :] = jnp.sum(sums[1], axis=0, keepdims=True)
        wait_all(loads)
        rows = slice(0, GROUP)
        edge = dot_nt(out_ref[rows, part(0)], w_ref[:, part(0)]) * (1.0 - vec_ref[4:5, :])
        edge += dot_nt(out_ref[rows, part(1)], w_ref[:, part(1)]) * (1.0 - vec_ref[5:6, :])
        edge += dot_nt(dr_ref[rows, :], w_ref[:, part(2)]) * (1.0 - vec_ref[6:7, :])
        edge_ref[...] = edge
        send_rows(flag_ref, edge, send_ref)


def input_back_kernel(lowest, weights, ins, outs, scratch, copies=(), grad=None):
    (pieces,) = weights
    grad_ref, dr_ref, xp_ref, before_ref, edge_ref, later_ref, got_ref, dx1_ref, vec_ref = ins[:9]
    out_ref, vsum_ref, later_out = outs
    carry, w_ref, back, rows_ref, sums, sems = scratch
    i = pl.program_id(0)
    count = pl.num_programs(0)
    loads = column_loads((pieces,), w_ref, sems, 0, 0, 3 * EMBED)
    start_loads(loads)

    @pl.when(i == 0)
    def _():
        if lowest:
            carry[...] = later_ref[...]
        else:
            take_rows(carry, later_ref, got_ref)
        sums[...] = jnp.zeros_like(sums)

    wait_load(loads + list(copies))
    if grad is not None:
        grad()
    for at, grads in enumerate((grad_ref[:, part(0)], grad_ref[:, part(1)], dr_ref[...])):
        back[at] = dot_nt(grads, w_ref[:, part(at)])
    gain = vec_ref[0:1, :]
    offset = vec_ref[1:2, :]
    n, rstd = normalize(xp_ref[step_rows(STEPS - 1), :].astype(F32))
    later = carry[...]
    for j in reversed(range(STEPS)):
        rows = step_rows(j)
        if j > 0:
            n_next, rstd_next = normalize(xp_ref[step_rows(j - 1), :].astype(F32))
            h_before = n_next * gain + offset
        else:
            n_before, _ = normalize(before_ref[...].astype(F32))
            h_before = n_before * gain + offset
            if lowest:
                h_before = jnp.where(i == count - 1, edge_ref[...], h_before)
        diff = n * gain + offset - h_before
        dh = later
        later = None
        for at in range(3):
            grad = back[at, rows, :]
            kept = grad * vec_ref[4 + at : 5 + at, :]
            sums[2 + at] += grad * diff
            dh = dh + kept
            passed = grad - kept
            later = passed if later is None else later + passed
        sums[0] += dh * n
        sums[1] += dh
        rows_ref[rows, :] = (dx1_ref[rows, :] + norm_back(dh * gain, n, rstd)).astype(BF16)
        if j > 0:
            n, rstd = n_next, rstd_next
    carry[...] = later
    later_out[...] = later
    out_ref[...] = swap_out(rows_ref[...])

    @pl.when(i == count - 1)
    def _():
        vsum_ref[...] = jnp.zeros_like(vsum_ref)
        for at in range(5):
            vsum_ref[at : at + 1, :] = jnp.sum(sums[at], axis=0, keepdims=True)
        if lowest:
            vsum_ref[...] += ins[10][...]


def adam_step(master, moment, second, gradient, rate, shrink):
    moment_new = 0.9 * moment + 0.1 * gradient
    second_new = 0.95 * second + 0.05 * gradient * gradient
    scaled = moment_new / (1.0 - 0.9**STEP) / (jnp.sqrt(second_new / (1.0 - 0.95**STEP)) + 1e-08)
    return (master - rate * (scaled + shrink * master), moment_new, second_new)


def neighbour(block, axis, distance):
    devices = range(lax.axis_size(axis))
    return lax.ppermute(block, axis, [(i, i + distance) for i in devices if i + distance in devices])


def everyone(block, axis):
    count = lax.axis_size(axis)
    return lax.all_to_all(
        jnp.broadcast_to(block[None], (count,) + block.shape), axis, 0, 0, tiled=True
    )


def scatter_rows(grad):
    part = lax.psum_scatter(grad.astype(BF16), "tok", scatter_dimension=0, tiled=True)
    return lax.psum_scatter(part, "rep", scatter_dimension=0, tiled=True).astype(F32)


def weight_grad(a, b):
    return dot_tn(a, b).astype(BF16)


def flip(block, axis, bit):
    return lax.ppermute(block, axis, [(i, i ^ bit) for i in range(lax.axis_size(axis))])


def place_all_kernel(bits_ref, own, far, near, both, out):
    height = own.shape[0]
    for source, high, low in (
        (own, bits_ref[4], bits_ref[3]), (far, 1 - bits_ref[4], bits_ref[3]),
        (near, bits_ref[4], 1 - bits_ref[3]), (both, 1 - bits_ref[4], 1 - bits_ref[3]),
    ):
        out[pl.ds(pl.multiple_of((2 * high + low) * height, height), height), :] = source[...]


def place(kernel, bits, inputs, shapes, name, after=()):
    vmem = pl.BlockSpec(memory_space=pltpu.VMEM)
    return pl.pallas_call(
        ordered(kernel, 0, len(after)),
        in_specs=[ANY_SPEC] * len(after) + [SMEM_SPEC] + [vmem] * len(inputs),
        out_specs=[vmem] * len(shapes),
        out_shape=[jax.ShapeDtypeStruct(shape, BF16) for shape in shapes],
        compiler_params=pltpu.CompilerParams(vmem_limit_bytes=VMEM.get(name, 16) * MIB),
        cost_estimate=cost(name),
        name=name,
    )(*after, bits, *inputs)


def cast_kernel(source, target):
    target[...] = source[...].astype(BF16)


def cast(shard, after, name):
    block = pl.BlockSpec(shard.shape, lambda i: (0, 0))
    return call(
        cast_kernel, 1, [block], block, jax.ShapeDtypeStruct(shard.shape, BF16), [], name, after
    )(shard)


def gather_plain(shard):
    return [lax.all_gather(lax.all_gather(shard, "rep", axis=0, tiled=True), "tok", axis=0, tiled=True)]


def rep_rows(shard):
    far = flip(shard, "rep", 2)
    return shard, far, flip(shard, "rep", 1), flip(far, "rep", 1)


def gather_rep(shard, bits, name, after=()):
    height, width = shard.shape
    return place(place_all_kernel, bits, rep_rows(shard), [(4 * height, width)], name + "_rep", after)[0]


def held(array, after, name):
    return pl.pallas_call(
        lambda *refs: None,
        in_specs=[ANY_SPEC] * (1 + len(after)),
        out_specs=ANY_SPEC,
        out_shape=jax.ShapeDtypeStruct(array.shape, array.dtype),
        input_output_aliases={0: 0},
        cost_estimate=cost(name),
        name=name,
    )(array, *after)


SLOTS = ((0, 0), (0, 1), (1, 0), (1, 1))


def store_slot(outs, slot, value, left):
    dy, dx = SLOTS[slot]
    if left:
        outs[dx][dy] = value
    else:
        outs[2 + dy][dx] = value


def beside(main, counts, pairs, takes, bits_ref, *refs):
    lists, lhs_count = [], 2 * len(pairs)
    for count in (counts[0], counts[1], lhs_count, 2 * len(takes), counts[2], 4, counts[3], 3):
        lists.append(refs[:count])
        refs = refs[count:]
    weights, ins, lhs_refs, rhs_refs, outs, grads, scratch, (lhs, made, sems) = lists
    i = pl.program_id(0)
    steps = pl.num_programs(0)
    height = EMBED // 8
    copies = []
    for at, base in enumerate(pairs):
        for which in range(2):
            for slot, (dy, dx) in enumerate(SLOTS):
                block = base + 4 * (bits_ref[2] ^ dy) + 2 * (bits_ref[1] ^ dx) + bits_ref[0]
                cols = pl.ds(pl.multiple_of(block * height, height), height)
                copies.append(
                    pltpu.make_async_copy(
                        lhs_refs[2 * at + which].at[:, cols],
                        lhs.at[2 * at + which, :, slot * height : (slot + 1) * height],
                        sems.at[len(copies)],
                    )
                )
    start_loads(copies)

    def grad():
        column = 0
        for at, (width, of_step) in enumerate(takes):
            pair = of_step[0] if len(set(of_step)) == 1 else i * len(pairs) // steps
            total = dot_tn(lhs[2 * pair], rhs_refs[2 * at][...]) + dot_tn(lhs[2 * pair + 1], rhs_refs[2 * at + 1][...])
            made[:, column : column + width] = total.astype(BF16)
            column += width

    main(weights, ins, outs, scratch, copies, grad)
    for left in (True, False):

        @pl.when((i < steps // 2) == left)
        def _(left=left):
            for slot in range(4):
                store_slot(grads, slot, made[slot * height : (slot + 1) * height, :], left)


def alone(main, counts, bits_ref, *refs):
    lists = []
    for count in counts:
        lists.append(refs[:count])
        refs = refs[count:]
    main(*lists, [], lambda: None)


def call_main(
    kernel, grid, ins, in_specs, out_specs, out_shape, scratch, name, after, bits, weights, lhs=(), takes=(),
    rhs=(), aliases=None,
):
    counts = (len(weights), len(in_specs), len(out_specs), len(scratch))
    if lhs:
        rows = rhs[0].shape[0]
        height = EMBED // 8
        lhs_args = [array for own, other, _ in lhs for array in (own, other)]
        rhs_specs, rhs_args = [], []
        for width, base, _ in takes:
            rhs_specs += [pl.BlockSpec((rows, width), lambda i, base=base: (0, base + i))] * 2
            rhs_args += rhs
        total = sum(width for width, _, _ in takes)
        left = pl.BlockSpec((2, height, total), lambda i: (0, 0, jnp.minimum(i, grid // 2 - 1)))
        right = pl.BlockSpec((2, height, total), lambda i: (0, 0, jnp.maximum(i - grid // 2, 0)))
        body = functools.partial(
            beside, kernel, counts, [base for _, _, base in lhs], [(width, pair) for width, _, pair in takes]
        )
        in_specs = in_specs + [ANY_SPEC] * len(lhs_args) + rhs_specs
        out_specs = out_specs + [left, left, right, right]
        out_shape = out_shape + [jax.ShapeDtypeStruct((2, height, total * grid // 2), BF16)] * 4
        scratch = scratch + [
            pltpu.VMEM((2 * len(lhs), rows, 4 * height), BF16), pltpu.VMEM((4 * height, total), BF16),
            pltpu.SemaphoreType.DMA((8 * len(lhs),)),
        ]
        ins = (*ins, *lhs_args, *rhs_args)
    else:
        body = functools.partial(alone, kernel, counts)
    heads = len(weights)

    def run(bits_ref, *refs):
        body(bits_ref, *[group[0] for group in refs[:heads]], *refs[heads:])

    results = call(
        run, grid, in_specs, out_specs, out_shape, scratch, name, after, bits, weights, aliases
    )(*ins)
    return results[: counts[2]], results[counts[2] :]


def tall_kernel(bits_ref, lhs_own, lhs_other, rhs_own, rhs_other, *outs):
    i = pl.program_id(0)
    total = dot_tn(lhs_own[...], rhs_own[...]) + dot_tn(lhs_other[...], rhs_other[...])
    total = total.astype(BF16)
    half = total.shape[1] // 2
    for at, (left, right) in enumerate(((0, 2), (0, 3), (1, 2), (1, 3))):

        @pl.when(i == at)
        def _(left=left, right=right):
            outs[left][0] = total[:, :half]
            outs[right][0] = total[:, half:]


def core_grad(bits, lhs, rhs, name, after=()):
    rows, height, width = rhs[0].shape[0], lhs[0].shape[1] // 8, rhs[0].shape[1] // 2

    def column(i, b):
        return (0, 4 * (b[2] ^ (i % 2)) + 2 * (b[1] ^ (i // 2)) + b[0])

    spec = pl.BlockSpec((rows, height), column)
    whole = pl.BlockSpec((rows, 2 * width), lambda i, b: (0, 0))
    return pl.pallas_call(
        ordered(tall_kernel, 1, len(after)),
        grid_spec=pltpu.PrefetchScalarGridSpec(
            num_scalar_prefetch=1,
            grid=(4,),
            in_specs=[ANY_SPEC] * len(after) + [spec, spec, whole, whole],
            out_specs=[
                pl.BlockSpec((1, height, width), lambda i, b: (jnp.minimum(i, 1), 0, 0)),
                pl.BlockSpec((1, height, width), lambda i, b: (jnp.maximum(i - 2, 0), 0, 0)),
                pl.BlockSpec((1, height, width), lambda i, b: (i // 2, 0, 0)),
                pl.BlockSpec((1, height, width), lambda i, b: (i // 2, 0, 0)),
            ],
        ),
        out_shape=[jax.ShapeDtypeStruct((2, height, width), BF16)] * 4,
        compiler_params=pltpu.CompilerParams(
            dimension_semantics=("arbitrary",), vmem_limit_bytes=VMEM.get(name, 16) * MIB
        ),
        cost_estimate=cost(name),
        name=name,
    )(bits, *after, *lhs, *rhs)


def add_kernel(count, bits_ref, *refs):
    for at in range(count):
        total = refs[2 * at][...].astype(F32) + refs[2 * at + 1][...].astype(F32)
        refs[2 * count + at][...] = total.astype(BF16)


def add_split(bits, grid, sums, name, after=()):
    in_specs, out_specs, shapes, args = [], [], [], []
    for a, b, block, source, shape, target in sums:
        in_specs += [pl.BlockSpec(block, source)] * 2
        args += [a, b]
        out_specs.append(pl.BlockSpec(block, target))
        shapes.append(jax.ShapeDtypeStruct(shape, BF16))
    return pl.pallas_call(
        ordered(functools.partial(add_kernel, len(sums)), 1, len(after)),
        grid_spec=pltpu.PrefetchScalarGridSpec(
            num_scalar_prefetch=1, grid=grid, in_specs=[ANY_SPEC] * len(after) + in_specs, out_specs=out_specs
        ),
        out_shape=shapes,
        compiler_params=pltpu.CompilerParams(vmem_limit_bytes=VMEM.get(name, 16) * MIB),
        cost_estimate=cost(name),
        name=name,
    )(bits, *after, *args)


def merge_kernel(moves, bits_ref, p_keep, p_got, q_keep, q_got, *outs):
    p = (p_keep[...].astype(F32) + p_got[...].astype(F32)).astype(BF16)
    q = (q_keep[...].astype(F32) + q_got[...].astype(F32)).astype(BF16)
    half = p.shape[-1]
    if len(outs) == 1:
        for side, start, width, column in moves or ((0, 0, half, 0), (1, 0, q.shape[-1], half)):
            outs[0][:, column : column + width] = (p, q)[side][0, :, start : start + width]
        return
    height = p.shape[1] // 2
    moves = moves or ((0, 0, half, 0), (1, 0, q.shape[-1], half))
    for out, low in ((outs[0], 1 - bits_ref[3]), (outs[1], bits_ref[3])):
        for at in range(2):

            @pl.when(low == at)
            def _(out=out, at=at):
                rows = slice(at * height, (at + 1) * height)
                for side, start, width, column in moves:
                    out[0, :, column : column + width] = (p, q)[side][0, rows, start : start + width]


def merge(bits, p_keep, p_got, q_keep, q_got, shapes, name, after, moves=()):
    _, block, p_width = p_keep.shape
    q_width = q_keep.shape[2]
    in_specs = [
        pl.BlockSpec((1, block // 2, width), lambda h, b: (0, h, 0))
        for width in (p_width, p_width, q_width, q_width)
    ]
    if len(shapes) == 1:
        out_specs = [pl.BlockSpec((block // 2, p_width + q_width), lambda h, b: (h, 0))]
    else:
        out_specs = [pl.BlockSpec((1,) + shapes[0][1:], lambda h, b: (h, 0, 0))] * 2
    return pl.pallas_call(
        ordered(functools.partial(merge_kernel, moves), 1, len(after)),
        grid_spec=pltpu.PrefetchScalarGridSpec(
            num_scalar_prefetch=1, grid=(2,), in_specs=[ANY_SPEC] * len(after) + in_specs, out_specs=out_specs
        ),
        out_shape=[jax.ShapeDtypeStruct(shape, BF16) for shape in shapes],
        compiler_params=pltpu.CompilerParams(vmem_limit_bytes=VMEM.get(name, 16) * MIB),
        cost_estimate=cost(name),
        name=name,
    )(bits, *after, p_keep, p_got, q_keep, q_got)


def reduce_grad(bits, made, offload, name, moves=()):
    p_keep, p_send, q_keep, q_send = made
    p_got, q_got = flip(p_send, "tok", 2), flip(q_send, "tok", 4)
    after = yield p_keep
    _, block, p_width = p_keep.shape
    q_width = q_keep.shape[2]
    half = block // 2
    sums = []
    for which in (1, 0):
        for keep, got, width in ((p_keep, p_got, p_width), (q_keep, q_got, q_width)):
            sums.append((
                keep, got, (1, half, width), lambda r, b, which=which: (which, r, 0),
                (1, block, width), lambda r, b: (0, r, 0),
            ))
    p_send, q_send, p_keep, q_keep = add_split(bits, (2,), sums, name + "_add_first", after)
    p_got, q_got = flip(p_send, "tok", 4), flip(q_send, "tok", 2)
    after = yield p_keep
    width = p_width + q_width
    if offload:
        (total,) = merge(bits, p_keep, p_got, q_keep, q_got, [(block, width)], name + "_merge", after, moves)
        yield total
        part = lax.psum_scatter(total, "rep", scatter_dimension=0, tiled=True)
        yield part
        yield part.astype(F32)
        return
    shape = (2, block // 4, width)
    send, keep = merge(bits, p_keep, p_got, q_keep, q_got, [shape] * 2, name + "_merge", after, moves)
    got = flip(send, "rep", 1)
    after = yield keep
    sums = [
        (keep, got, (1,) + shape[1:], lambda i, b, f=f: (b[4] ^ f, 0, 0), (1,) + shape[1:], lambda i, b: (0, 0, 0))
        for f in (1, 0)
    ]
    send, keep = add_split(bits, (1,), sums, name + "_add_low", after)
    got = flip(send, "rep", 2)
    yield keep
    yield got
    yield (keep.astype(F32) + got.astype(F32))[0]


def reduce_plain(lhs, rhs):
    sums, column = [], 0
    for array, _, base, tiles in lhs:
        if array.shape[1] > EMBED and array.shape[1] != FF:
            array = array[:, base * EMBED // 8 : base * EMBED // 8 + EMBED]
        sums.append(scatter_rows(weight_grad(array, rhs[0][:, part(column, tiles)])))
        column += tiles
    total = jnp.concatenate(sums, axis=1)
    for _ in range(5):
        yield total[:8]
    yield total


def advance(work, *after):
    return work.send(tuple(after))


def on_device(
    tokens, cotangent, init_num, init_den, prev_att, seg_doc, w_kvr, w_out, f_kr, f_value, vectors,
    m_kvr, v_kvr, m_out, v_out, m_fkr, v_fkr, m_fvalue, v_fvalue, vec_m, vec_v,
):
    tok_count = lax.axis_size("tok")
    rep_count = lax.axis_size("rep")
    here = lax.axis_index("tok")
    flat_index = here * rep_count + lax.axis_index("rep")
    micro, _, local_len, _ = tokens.shape
    seg_count = seg_doc.shape[2]
    chunk = local_len // CHUNKS
    blocks = chunk // STEPS
    rows = micro * local_len

    rep_index = lax.axis_index("rep")
    bits = jnp.stack([here & 1, (here >> 1) & 1, (here >> 2) & 1, rep_index & 1, (rep_index >> 1) & 1])
    bits = bits.astype(jnp.int32)
    paired = tok_count == 8 and rep_count == 4
    att_shard = jnp.concatenate([w_kvr, w_out], axis=1).astype(BF16)
    before_mix = before_wkv = before_hidden = ()
    if paired:
        half_cols = EMBED // 2
        value_left, value_raw = f_value[:, :half_cols].astype(BF16), f_value[:, half_cols:].astype(BF16)
        att_part = gather_rep(att_shard, bits, "place_att")
        att_w = [lax.all_gather(att_part, "tok", axis=0, tiled=True)]
        hidden_part = gather_rep(cast(f_kr, (att_part,), "cast_hidden"), bits, "place_hidden")
        fkr = [lax.all_gather(hidden_part, "tok", axis=0, tiled=True)]
        value_rows = lax.all_gather(value_raw, "tok", axis=0, tiled=True)
        value_part = gather_rep(value_left, bits, "place_value", (hidden_part,))
        fvalue = [lax.all_gather(value_part, "tok", axis=0, tiled=True)]
        value_rows = held(value_rows, (value_part,), "hold_value")
        value_far = flip(value_rows, "rep", 2)
        value_near = flip(value_rows, "rep", 1)
        value_others = [value_rows, value_far, value_near, flip(value_far, "rep", 1)]
        before_mix = (value_rows,)
        before_wkv = (value_far, value_near)
    else:
        value_others = []
        att_w, fkr, fvalue = gather_plain(att_shard), gather_plain(f_kr.astype(BF16)), gather_plain(f_value.astype(BF16))

    def other_core(array):
        return flip(array, "tok", 1) if paired else None

    documents = seg_doc[:, 0, :]
    marker = jnp.concatenate(
        [jnp.ones((micro, 1), jnp.bool_), documents[:, 1:] != documents[:, :-1]], axis=1
    )
    starts = jnp.arange(tok_count) * local_len
    fresh = jnp.logical_and(marker[:, starts // SEG_LEN], (starts % SEG_LEN == 0)[None, :])
    fresh_here = lax.dynamic_index_in_dim(fresh, here, 1, keepdims=True)
    seg_here = here * local_len // SEG_LEN
    prev_here = lax.dynamic_index_in_dim(prev_att[:, 0], seg_here, 1, keepdims=False).astype(F32)
    init_all = everyone(jnp.concatenate([init_num[:, 0], init_den[:, 0]], axis=0), "tok")
    init_all = jnp.moveaxis(init_all, 0, 2).reshape(2 * micro, seg_count, EMBED)
    rate = -jnp.exp(vectors[9:10])
    fade = jnp.exp(rate * float(local_len))
    fresh_four = jnp.concatenate([fresh, fresh], axis=0)
    flags = jnp.concatenate(
        [fresh_here[:, 0].astype(jnp.int32), jnp.reshape(here, (1,)).astype(jnp.int32),
         jnp.moveaxis(fresh, 1, 0).reshape(-1).astype(jnp.int32)]
    )

    x4 = tokens.reshape(micro, CHUNKS, chunk, EMBED)
    c4 = cotangent.reshape(micro, CHUNKS, chunk, EMBED)

    def edge_back(last, incoming):
        moved = jnp.concatenate([incoming[:, None], last.reshape(micro, CHUNKS, EMBED)[:, :-1]], axis=1)
        return moved.reshape(GROUP, EMBED)

    raw_in = neighbour(tokens[:, 0, -1, :], "tok", 1)
    raw_edge = edge_back(x4[:, :, -1, :], raw_in).astype(F32)
    edge_n, _ = normalize(raw_edge)
    edge_h = edge_n * vectors[0:1] + vectors[1:2]
    first_row = (jnp.arange(GROUP) % CHUNKS == 0)[:, None]
    fresh_rows = jnp.repeat(fresh_here[:, 0], CHUNKS)[:, None]
    replace = jnp.logical_and(first_row, fresh_rows)
    edge_one = jnp.where(replace, jnp.repeat(prev_here, CHUNKS, axis=0), edge_h)

    def up(width):
        return pl.BlockSpec((ROWS, width), lambda i: (i, 0))

    def down(width):
        return pl.BlockSpec((ROWS, width), lambda i: (blocks - 1 - i, 0))

    before_spec = pl.BlockSpec(
        (GROUP, EMBED), lambda i: (jnp.maximum((blocks - 1 - i) * STEPS - 1, 0), 0)
    )
    natural_up = pl.BlockSpec((micro, CHUNKS, STEPS, EMBED), lambda i: (0, 0, i, 0))
    natural_down = pl.BlockSpec((micro, CHUNKS, STEPS, EMBED), lambda i: (0, 0, blocks - 1 - i, 0))
    st_up = pl.BlockSpec((1, 2 * GROUP, EMBED), lambda i: (i, 0, 0))
    st_down = pl.BlockSpec((1, 2 * GROUP, EMBED), lambda i: (blocks - 1 - i, 0, 0))
    vec_spec = full(vectors.shape)
    edge_spec = full((GROUP, EMBED))
    state_spec = full((2 * GROUP, EMBED))
    total_spec = full((2 * micro, EMBED))
    sum_spec = full((8, EMBED))

    def like(width, dtype):
        return jax.ShapeDtypeStruct((rows, width), dtype)

    def small(count, dtype=F32):
        return jax.ShapeDtypeStruct((count, EMBED), dtype)

    def weight(height, width):
        return pltpu.VMEM((height, width), BF16)

    sems = pltpu.SemaphoreType.DMA((80,))
    state = pltpu.VMEM((GROUP, EMBED), F32)
    square = 2 * rows * EMBED * EMBED

    xp, mix, k, v, r, ends, totals = call(
        mix_one_kernel, blocks,
        [natural_up, edge_spec, vec_spec],
        [up(EMBED), up(3 * EMBED)] + [up(EMBED)] * 3 + [state_spec, total_spec],
        [like(EMBED, BF16), like(3 * EMBED, BF16), like(EMBED, BF16), like(EMBED, BF16), like(EMBED, BF16),
         small(2 * GROUP), small(2 * micro)],
        [state] * 3 + [weight(EMBED, 3 * EMBED), sems], "mix_one", before_mix, bits, (att_w,),
    )(x4, edge_one, vectors)

    every = everyone(totals, "tok")
    carried = jnp.zeros((2 * micro, EMBED), F32)
    begin = jnp.zeros((2 * micro, EMBED), F32)
    for d in range(tok_count):
        seg = d * local_len // SEG_LEN
        carried = jnp.where(fresh_four[:, d : d + 1], init_all[:, seg], carried)
        begin = jnp.where(here == d, carried, begin)
        carried = fade * carried + every[d]

    wkv, y, x1, mix_two, saved, first_two, last_two = call(
        wkv_kernel, blocks,
        [up(EMBED)] * 4 + [vec_spec, total_spec, state_spec],
        [up(EMBED)] * 3 + [up(2 * EMBED), st_up, edge_spec, edge_spec],
        [like(EMBED, BF16), like(EMBED, BF16), like(EMBED, F32), like(2 * EMBED, BF16),
         jax.ShapeDtypeStruct((blocks, 2 * GROUP, EMBED), F32), small(GROUP), small(GROUP)],
        [state] * 3 + [weight(EMBED, EMBED), sems], "wkv", before_wkv, bits, (att_w,),
    )(k, v, r, xp, vectors, begin, ends)

    if paired:
        mix = held(mix, (last_two,), "hold_mix")
    row_in = neighbour(last_two.reshape(micro, CHUNKS, EMBED)[:, -1], "tok", 1)
    edge_two = jnp.where(replace, 0.0, edge_back(last_two, row_in))
    diff_two = first_two - edge_two
    fixed = jnp.concatenate([edge_two + diff_two * vectors[7:8], edge_two + diff_two * vectors[8:9]], axis=1)
    mix_two = lax.dynamic_update_slice(mix_two, fixed.astype(BF16), (0, 0))

    kq, gate = call(
        hidden_kernel, blocks,
        [up(2 * EMBED)],
        [up(FF), up(EMBED)],
        [like(FF, BF16), like(EMBED, BF16)],
        [weight(EMBED, FF + EMBED), sems], "hidden", before_hidden, bits, (fkr,),
    )(mix_two)
    kq_other, mix_two_other, y_other, mix_other = [other_core(array) for array in (kq, mix_two, y, mix)]

    known = (mix_two_other, y_other, mix_other) if paired else ()
    mixed, dvf, dkf, cp = call(
        value_kernel, blocks,
        [up(FF), up(EMBED), up(EMBED), natural_up],
        [natural_up, up(EMBED), up(FF + EMBED), up(EMBED)],
        [jax.ShapeDtypeStruct(x4.shape, BF16), like(EMBED, BF16), like(FF + EMBED, BF16),
         like(EMBED, BF16)],
        [weight(FF, EMBED), pltpu.VMEM((ROWS, EMBED), F32), weight(ROWS, EMBED), sems],
        "value", known, bits, (fvalue, value_others),
    )(kq, gate, x1, c4)
    row_spec = full((micro, EMBED))
    shift_two, send_two = call(
        edge_kernel, 1,
        [SMEM_SPEC, pl.BlockSpec((GROUP, FF + EMBED), lambda i: (0, 0)), vec_spec], [edge_spec, row_spec],
        [small(GROUP), small(micro)],
        [weight(EMBED, FF + EMBED), sems], "edge", (), bits, (fkr,),
    )(flags, dkf, vectors)

    got_two = neighbour(send_two, "tok", -1)

    def reduced(made, plain, offload, name, moves=()):
        work = reduce_grad(bits, made, offload, name, moves) if paired else reduce_plain(*plain)
        next(work)
        return work

    def fused(kernel, grid, ins, in_specs, out_specs, out_shape, scratch, name, after, weights, lhs, takes, rhs,
              aliases=None):
        if not paired:
            lhs = takes = rhs = ()
        return call_main(
            kernel, grid, ins, in_specs, out_specs, out_shape, scratch, name, after, bits, weights, lhs, takes,
            rhs, aliases,
        )

    wide, narrow = FF // blocks, EMBED // blocks
    dvf_other = other_core(dvf)
    if paired:
        dkf = held(dkf, (dvf_other, shift_two), "hold_dkf")
    dkf_other = other_core(dkf)
    made = core_grad(bits, (kq, kq_other), (dvf, dvf_other), "grad_value", (shift_two,)) if paired else (shift_two,)
    value_sum = reduced(made, ([(kq, None, 0, 1)], (dvf, None)), True, "grad_value")

    got_two = held(got_two, (made[0],), "hold_row")
    every_spec = full((tok_count, 2 * micro, EMBED))
    (dx1, datt, dwkv, vsum_two, firsts, back_totals), grads = fused(
        middle_back_kernel, blocks,
        (dkf, x1, x1, edge_two, shift_two, got_two, cp, vectors, k, v, r, wkv, saved),
        [down(FF + EMBED), down(EMBED), before_spec, edge_spec,
         edge_spec, row_spec, down(EMBED), vec_spec] + [down(EMBED)] * 4 + [st_down],
        [down(EMBED), down(2 * EMBED), down(EMBED)] + [sum_spec, state_spec, every_spec],
        [like(EMBED, F32), like(2 * EMBED, BF16), like(EMBED, BF16), small(8),
         small(2 * GROUP), jax.ShapeDtypeStruct((tok_count, 2 * micro, EMBED), F32)],
        [state, pltpu.VMEM((2, ROWS, EMBED), F32), state, state, weight(EMBED, FF + EMBED),
         weight(EMBED, EMBED), pltpu.VMEM((ROWS, EMBED), F32), pltpu.VMEM((ROWS, EMBED), F32),
         pltpu.VMEM((4, GROUP, EMBED), F32), sems],
        "middle_back", (made[0],), (fkr, att_w),
        [(mix_two, mix_two_other, 0), (mix_two, mix_two_other, 8)],
        [(FF // blocks, 0, (0,) * blocks), (EMBED // blocks, FF * blocks // EMBED, (1,) * blocks)], (dkf, dkf_other),
    )
    hidden_sum = reduced(
        grads, ([(mix_two, None, 0, 4), (mix_two, None, 8, 1)], (dkf, None)), False, "grad_hidden",
        [(at // (blocks // 2), at % (blocks // 2) * (wide + narrow), wide, at * wide) for at in range(blocks)]
        + [(at // (blocks // 2), at % (blocks // 2) * (wide + narrow) + wide, narrow, FF + at * narrow)
           for at in range(blocks)],
    )

    every_back = lax.all_to_all(back_totals, "tok", 0, 0, tiled=True)
    made = advance(value_sum, firsts)
    datt_other = other_core(datt)
    right_down = pl.BlockSpec((ROWS, EMBED), lambda i: (blocks - 1 - i, 1))
    (dkv, vsum_wkv, shift_one, send_one), grads = fused(
        wkv_back_kernel, blocks,
        (flags, k, v, dwkv, datt, saved, vectors, every_back, firsts),
        [SMEM_SPEC] + [down(EMBED)] * 3 + [right_down, st_down, vec_spec, every_spec, state_spec],
        [down(2 * EMBED), sum_spec, edge_spec, row_spec],
        [like(2 * EMBED, BF16), small(8), small(GROUP), small(micro)],
        [pltpu.VMEM((ROWS, EMBED), F32)] * 2 + [state] * 2
        + [pltpu.VMEM((2, GROUP, EMBED), F32), weight(EMBED, 3 * EMBED), sems],
        "wkv_back", (made,), (att_w,),
        [(y, y_other, 0), (mix, mix_other, 16)], [(2 * EMBED // blocks, 0, (0, 0, 1, 1))], (datt, datt_other),
    )
    early_sum = reduced(grads, ([(y, None, 0, 1), (mix, None, 16, 1)], (datt, None)), False, "grad_early")
    dkv_other = other_core(dkv)

    got_one = neighbour(send_one, "tok", -1)
    made = advance(value_sum, dkv)
    value_part = advance(value_sum)
    made = advance(hidden_sum, made)
    made = advance(early_sum, made)

    half = blocks // 2

    def input_back(high, before, later_rows, started):
        def at(width, column=0):
            return pl.BlockSpec((ROWS, width), lambda i: (high - i, column))

        before_block = pl.BlockSpec((GROUP, EMBED), lambda i: (jnp.maximum((high - i) * STEPS - 1, 0), 0))
        natural = pl.BlockSpec((micro, CHUNKS, STEPS, EMBED), lambda i: (0, 0, high - i, 0))
        return fused(
            functools.partial(input_back_kernel, bool(started)), half,
            (dkv, datt, xp, xp, edge_one, later_rows, got_one, dx1, vectors, *started),
            [at(2 * EMBED), at(EMBED, 1), at(EMBED), before_block, edge_spec, edge_spec, row_spec, at(EMBED), vec_spec]
            + [ANY_SPEC, sum_spec][: len(started)],
            [natural, sum_spec, edge_spec],
            [jax.ShapeDtypeStruct(x4.shape, BF16), small(8), small(GROUP)],
            [state, weight(EMBED, 3 * EMBED), pltpu.VMEM((3, ROWS, EMBED), F32), weight(ROWS, EMBED),
             pltpu.VMEM((5, GROUP, EMBED), F32), sems],
            "input_back_low" if started else "input_back_high", before, (att_w,),
            () if started else [(mix, mix_other, 0), (mix, mix_other, 8)], [(EMBED, 0, (0, 1))], (dkv, dkv_other),
            {len(before) + 1 + len(att_w) + 9: 0} if started else None,
        )

    (token_high, vsum_high, later_half), grads = input_back(blocks - 1, (made,), shift_one, ())
    late_sum = reduced(grads, ([(mix, None, 0, 1), (mix, None, 8, 1)], (dkv, None)), False, "grad_late")
    made = advance(hidden_sum, vsum_high)
    made = advance(early_sum, made)
    (token_grad, vsum_one, _), _ = input_back(half - 1, (made, value_part), later_half, (token_high, vsum_high))

    made = advance(late_sum, vsum_one)
    made = advance(hidden_sum, made)
    hidden_got = advance(hidden_sum)
    made = advance(late_sum, made)
    made = advance(early_sum, made)
    early_got = advance(early_sum)
    columns = vec_m.shape[1]
    grad_vec = held(jnp.concatenate([vsum_one, vsum_two, vsum_wkv], axis=0), (made,), "hold_vec")
    pieces = jnp.moveaxis(grad_vec.reshape(grad_vec.shape[0], tok_count * rep_count, columns), 1, 0)
    vec_terms = lax.all_to_all(pieces, ("tok", "rep"), 0, 0, tiled=True)
    made = advance(late_sum, made, hidden_got, early_got)
    advance(late_sum)
    sum_fvalue = advance(value_sum)
    if not paired:
        sum_fvalue = advance(value_sum)
    sum_fkr = advance(hidden_sum)
    sum_early = advance(early_sum)
    sum_late = advance(late_sum)
    sums = jnp.sum(held(vec_terms, (made,), "hold_terms"), axis=0)
    sum_vec = jnp.concatenate([sums[0:2], sums[8:10], sums[2:5], sums[10:12], sums[16:18]], axis=0)
    sum_out = sum_early[:, :EMBED]
    sum_kvr = jnp.concatenate([sum_late, sum_early[:, EMBED:]], axis=1)

    base_rate = 2.5 / math.sqrt(EMBED)
    new_kvr = adam_step(w_kvr, m_kvr, v_kvr, sum_kvr, base_rate, 0.01)
    new_out = adam_step(w_out, m_out, v_out, sum_out, 4.0 * base_rate, 0.01)
    new_fkr = adam_step(f_kr, m_fkr, v_fkr, sum_fkr, base_rate, 0.01)
    new_fvalue = adam_step(f_value, m_fvalue, v_fvalue, sum_fvalue, 2.5 / math.sqrt(FF), 0.01)
    vec_master = lax.dynamic_slice_in_dim(vectors, flat_index * columns, columns, 1)
    vec_rates = jnp.array([0.6, 0.3, 0.6, 0.3, 0.3, 0.3, 0.3, 0.3, 0.3, 3.0, 0.5], F32)[:, None]
    new_vectors = adam_step(vec_master, vec_m, vec_v, sum_vec, vec_rates, 0.0)
    shape = tokens.shape
    return (
        (mixed.reshape(shape), token_grad.reshape(shape))
        + new_kvr + new_out + new_fkr + new_fvalue + new_vectors
    )


def solution(mesh):
    rows = P(("tok", "rep"), None)
    columns = P(None, ("tok", "rep"))
    token_spec = P(None, "rep", "tok", None)
    channel_spec = P(None, "rep", None, "tok")
    placed = (
        (token_spec, token_spec, channel_spec, channel_spec, P(None, "rep", None, None), P(None, "rep", None))
        + (rows,) * 4 + (P(),) + (rows,) * 8 + (columns,) * 2
    )
    return jax.shard_map(
        on_device,
        mesh=mesh,
        in_specs=placed,
        out_specs=(token_spec, token_spec) + (rows,) * 12 + (columns,) * 3,
        check_vma=False,
    )
```

time: 766 us -> 496 us (0.65)
  waiting for transfers between devices: 397 us -> 108 us
  Pallas kernels: 139 us -> 217 us
  blocking collectives: 63.5 us -> 0 us
  matrix products: 55.5 us -> 0 us
  starting transfers between devices: 23.1 us -> 67.3 us
  local copies, waits for them, and re-layouts: 22.2 us -> 62 us
  other arithmetic: 43.6 us -> 18.6 us
    reduce_scatter x7 -> x1, waiting for transfers between devices: 219 us -> 0.01 us  [reduce_grad(): part = lax.psum_scatter(total, 'rep', scatter_dimension=0, tiled=True)]
    all_gather x6 -> x4, waiting for transfers between devices: 138 us -> 5.94 us  [the longest x1 5.35 us: on_device(): att_w = [lax.all_gather(att_part, 'tok', axis=0, tiled=True)]]
    ppermute x0 -> x42, waiting for transfers between devices: none -> 82.9 us  [flip(): lax.ppermute(block, axis, [(i, i ^ bit) for i in range(lax.axis_size(axis...]
    pallas_call x7 -> x31, Pallas kernels: 139 us -> 217 us  [the longest x10 180 us: call(): return lambda *args: made(*after, *head, *args)]
    all_gather x4 -> x0, blocking collectives: 63.5 us -> none  [the longest x2 45.4 us: gather_rows(): part = lax.all_gather(weight.astype(BF16), 'rep', axis=0, tiled=True)]
    dot_general x9 -> x0, matrix products: 55.5 us -> none  [the longest x7 47.5 us: weight_grad(): lax.dot_general(a, b, (((0,), (0,)), ((), ())), preferred_element_type=F32)]
    ppermute x0 -> x42, starting transfers between devices: none -> 45.8 us  [flip(): lax.ppermute(block, axis, [(i, i ^ bit) for i in range(lax.axis_size(axis...]
    unnamed x79 -> x164, local copies, waits for them, and re-layouts: 13.2 us -> 52.1 us
  transfers between devices with their start and end apart: 21 -> 55, of which waited for: 17 -> 20; matrix products, arithmetic and copies ran while one was open for 13% -> 6% of each run, Pallas kernels for 10% -> 38%
where the time goes in v2:
time: 496 us; the launch traced here: 487 us
  Pallas kernels  217 us (44%)
  waiting for transfers between devices  108 us (22%)
  starting transfers between devices  67.3 us (14%)
  local copies, waits for them, and re-layouts  62 us (12%)
  other arithmetic  18.6 us (4%)
  between operations  15 us (3%)
    pallas_call x10, Pallas kernels, call(): return lambda *args: made(*after, *head, *args)  180 us
    ppermute x42, waiting for transfers between devices, flip(): lax.ppermute(block, axis, [(i, i ^ bit) for i in range(lax.axis_size(axis...  82.9 us
    unnamed x164, local copies, waits for them, and re-layouts  52.1 us
    ppermute x42, starting transfers between devices, flip(): lax.ppermute(block, axis, [(i, i ^ bit) for i in range(lax.axis_size(axis...  45.8 us
    pallas_call x1, Pallas kernels, core_grad(): pl.pallas_call(ordered(tall_kernel, 1, len(after)), grid_spec=pltpu.Prefe...  15.1 us
    pallas_call x7, Pallas kernels, add_split(): pl.pallas_call(ordered(functools.partial(add_kernel, len(sums)), 1, len(a...  10.5 us
  transfers between devices with their start and end apart: 55, of which 20 were waited for; matrix products, arithmetic and copies ran while one was open for 6% of the time, Pallas kernels for 38%

profile of v2, /device:TPU:0, one launch (start us, length us, event | category | flops | bytes accessed | tf_op | source)
XLA Modules:
  0.0 487.4 jit_solution(6488446941440452906)
XLA Ops:
  16.7 10.5 %collective-permute-done.refs_2_ = bf16[32,4096]{1,0:T(8,128)(2,1)S(1)} collective-permute-done((bf16[32,4096]{1,0:T(8,128)(2,1)S(1)}, bf16[32,4096]{1,0:T(8,128)(2,1)S(1)}, u32[]{:S(2)}, u32[]{:S(2)}) %collective-permute-start) | collective-permute-done | bytes 262176 | tf_op jit(solution)/shard_map/ppermute | solution.py:696
  27.9 6.7 %collective-permute-done.2.refs_4_ = bf16[32,4096]{1,0:T(8,128)(2,1)S(1)} collective-permute-done((bf16[32,4096]{1,0:T(8,128)(2,1)S(1)}, bf16[32,4096]{1,0:T(8,128)(2,1)S(1)}, u32[]{:S(2)}, u32[]{:S(2)}) %collective-permute-start.2) | collective-permute-done | bytes 262176 | tf_op jit(solution)/shard_map/ppermute | solution.py:696
  41.2 12.9 %collective-permute-done.3.refs_2_ = bf16[32,5120]{1,0:T(8,128)(2,1)S(1)} collective-permute-done((bf16[32,5120]{1,0:T(8,128)(2,1)S(1)}, bf16[32,5120]{1,0:T(8,128)(2,1)S(1)}, u32[]{:S(2)}, u32[]{:S(2)}) %collective-permute-start.3) | collective-permute-done | bytes 327712 | tf_op jit(solution)/shard_map/ppermute | solution.py:696
  54.7 8.1 %collective-permute-done.5.refs_4_ = bf16[32,5120]{1,0:T(8,128)(2,1)S(1)} collective-permute-done((bf16[32,5120]{1,0:T(8,128)(2,1)S(1)}, bf16[32,5120]{1,0:T(8,128)(2,1)S(1)}, u32[]{:S(2)}, u32[]{:S(2)}) %collective-permute-start.5) | collective-permute-done | bytes 327712 | tf_op jit(solution)/shard_map/ppermute | solution.py:696
  72.1 4.6 all-to-all-start
  80.9 5.8 %collective-permute-done.8.refs_5_ = bf16[128,512]{1,0:T(8,128)(2,1)S(1)} collective-permute-done((bf16[128,512]{1,0:T(8,128)(2,1)S(1)}, bf16[128,512]{1,0:T(8,128)(2,1)S(1)}, u32[]{:S(2)}, u32[]{:S(2)}) %collective-permute-start.8) | collective-permute-done | bytes 131104 | tf_op jit(solution)/shard_map/ppermute | solution.py:696
  88.6 5.3 %all-gather.7.cloned.1.call-done.refs_2_.refs_3_ = bf16[1024,4096]{1,0:T(8,128)(2,1)} async-done(((bf16[128,4096]{1,0:T(8,128)(2,1)}), bf16[1024,4096]{1,0:T(8,128)(2,1)}) %all-gather.7.cloned.1.call-update) | async-done | bytes 8388624 | tf_op jit(solution)/shard_map/all_gather | solution.py:1050
  96.8 14.9 %mix_one.1 = (bf16[1024,1024]{1,0:T(8,128)(2,1)S(1)}, bf16[1024,3072]{1,0:T(8,128)(2,1)S(1)}, bf16[1024,1024]{1,0:T(8,128)(2,1)S(1)}, bf16[1024,1024]{1,0:T(8,12...) custom-call(bf16[1024,512]{1,0:T(8,128)(2,1)S(1)} %copy-done.16, ...), custom_call_target="tpu_custom_call" | custom-call | flops 2000000000 | tf_op jit(solution)/shard_map/mix_one/pallas_call | solution.py:119
  123.1 5.5 %all-to-all-done.1 = f32[8,4,1024]{2,1,0:T(4,128)} async-done(((f32[8,4,1024]{2,1,0:T(4,128)}), f32[8,4,1024]{2,1,0:T(4,128)}, u32[]{:S(2)}, u32[]{:S(2)}) %all-to-all-start.1) | async-done | bytes 131104 | tf_op jit(solution)/shard_map/all_to_all | solution.py:681
  129.5 5.1 %collective-permute-done.10.refs_1_.refs_7_ = bf16[1024,512]{1,0:T(8,128)(2,1)S(1)} collective-permute-done((bf16[1024,512]{1,0:T(8,128)(2,1)}, bf16[1024,512]{1,0:T(8,128)(2,1)S(1)}, u32[]{:S(2)}, u32[]{:S(2)}) %collective-permute-start.10) | collective-permute-done | bytes 1048608 | tf_op jit(solution)/shard_map/ppermute | solution.py:696
  142.1 11.2 %wkv.1 = (bf16[1024,1024]{1,0:T(8,128)(2,1)S(1)}, bf16[1024,1024]{1,0:T(8,128)(2,1)S(1)}, f32[1024,1024]{1,0:T(8,128)S(1)}, bf16[1024,2048]{1,0:T(8,128)(2,1)S(1...) custom-call(bf16[1024,512]{1,0:T(8,128)(2,1)} %collective-permute-done.9.refs_0_.refs_6_, ...), custom_call_target="tpu_custom_call" | custom-call | flops 2000000000 | tf_op jit(solution)/shard_map/wkv/pallas_call | solution.py:119
  164.0 7.2 %collective-permute-done.12 = f32[2,1024]{1,0:T(2,128)S(1)} collective-permute-done((f32[2,1024]{1,0:T(2,128)S(1)}, f32[2,1024]{1,0:T(2,128)S(1)}, u32[]{:S(2)}, u32[]{:S(2)}) %collective-permute-start.12) | collective-permute-done | bytes 8224 | tf_op jit(solution)/shard_map/ppermute | solution.py:676
  174.6 15.1 %hidden.1 = (bf16[1024,4096]{1,0:T(8,128)(2,1)S(1)}, bf16[1024,1024]{1,0:T(8,128)(2,1)S(1)}) custom-call(s32[5]{0:T(128)S(1)} %stack.23.refs_0_.refs_1_.refs_2_.refs_3_, bf16[1024,5120]{1,0:T(8,128)(2,1)} %all-gather.11.cloned.1.call-done.refs_1_.refs_2_, bf16[1024,2048]{1,0:T(8,128)(2,1)S(1)} %copy-done.2), custom_call_target="tpu_custom_call" | custom-call | flops 2000000000 | tf_op jit(solution)/shard_map/hidden/pallas_call | solution.py:119
  198.8 29.9 %value.1 = (bf16[2,8,64,1024]{3,2,1,0:T(8,128)(2,1)}, bf16[1024,1024]{1,0:T(8,128)(2,1)}, bf16[1024,5120]{1,0:T(8,128)(2,1)}, bf16[1024,1024]{1,0:T(8,128)(2,1)}) custom-call(bf16[1024,2048]{1,0:T(8,128)(2,1)} %collective-permute-done.13.refs_0_.refs_18_.refs_20_, bf16[1024,1024]{1,0:T(8,128)(2,1)} %collective-permute-done.14.refs_1_.refs_13_, ...), custom_call_target="tpu_custom_call" | custom-call | flops 60000002048 | tf_op jit(solution)/shard_map/value/pallas_call | solution.py:119
  229.9 9.1 %edge.1 = (f32[16,1024]{1,0:T(8,128)}, f32[2,1024]{1,0:T(2,128)}) custom-call(s32[5]{0:T(128)} %copy-done.28, bf16[1024,5120]{1,0:T(8,128)(2,1)} %all-gather.11.cloned.1.call-done.refs_1_.refs_2_, s32[19]{0:T(128)} %pad_add_fusion.1.refs_2_.refs_3_, bf16[1024,5120]{1,0:T(8,128)(2,1)} %get-tuple-element.113.refs_3_.refs_0_, f32[11,1024]{1,0:T(8,128)} %refs_12_.1), custom_call_target="tpu_custom_call" | custom-call | flops 14000000000 | tf_op jit(solution)/shard_map/edge/pallas_call | solution.py:119
  241.0 4.2 collective-permute-done.17.refs_3_
  245.3 15.1 %grad_value.1 = (bf16[2,512,512]{2,1,0:T(8,128)(2,1)}, bf16[2,512,512]{2,1,0:T(8,128)(2,1)}, bf16[2,512,512]{2,1,0:T(8,128)(2,1)}, bf16[2,512,512]{2,1,0:T(8,128)(2,1)}) custom-call(s32[5]{0:T(128)} %copy-done.28, f32[16,1024]{1,0:T(8,128)} %get-tuple-element.114.refs_1_.refs_2_.refs_8_, bf16[1024,4096]{1,0:T(8,128)(2,1)} %copy-done.31, ...), custom_call_target="tpu_custom_call" | custom-call | flops 30000001024 | tf_op jit(solution)/shard_map/grad_value/pallas_call | solution.py:879
  263.0 47.7 %middle_back.1 = (f32[1024,1024]{1,0:T(8,128)}, bf16[1024,2048]{1,0:T(8,128)(2,1)}, bf16[1024,1024]{1,0:T(8,128)(2,1)}, f32[8,1024]{1,0:T(8,128)}, f32[32,1024]{...) custom-call(bf16[2,512,512]{2,1,0:T(8,128)(2,1)} %get-tuple-element., ...), custom_call_target="tpu_custom_call" | custom-call | flops 60000002048 | tf_op jit(solution)/shard_map/middle_back/pallas_call | solution.py:119
  327.3 20.5 %wkv_back.1 = (bf16[1024,2048]{1,0:T(8,128)(2,1)}, f32[8,1024]{1,0:T(8,128)}, f32[16,1024]{1,0:T(8,128)}, f32[2,1024]{1,0:T(2,128)}, bf16[2,128,1024]{2,1,0:T(8,...) custom-call(bf16[1,512,512]{2,1,0:T(8,128)(2,1)} %copy-done.48, ...), custom_call_target="tpu_custom_call" | custom-call | flops 24000000000 | tf_op jit(solution)/shard_map/wkv_back/pallas_call | solution.py:119
  357.9 9.3 %collective-permute-done.26.refs_3_.refs_7_ = bf16[2,128,2560]{2,1,0:T(8,128)(2,1)} collective-permute-done((bf16[2,128,2560]{2,1,0:T(8,128)(2,1)}, bf16[2,128,2560]{2,1,0:T(8,128)(2,1)}, u32[]{:S(2)}, u32[]{:S(2)}) %collective-permute-start.26) | collective-permute-done | bytes 1310752 | tf_op jit(solution)/shard_map/ppermute | solution.py:696
  393.1 19.6 %input_back_high.1 = (bf16[2,8,64,1024]{3,2,1,0:T(8,128)(2,1)}, f32[8,1024]{1,0:T(8,128)S(1)}, f32[16,1024]{1,0:T(8,128)S(1)}, bf16[2,128,1024]{2,1,0:T(8,128)(2...) custom-call(bf16[1,128,1024]{2,1,0:T(8,128)(2,1)S(1)} %copy-done.43,, ...), custom_call_target="tpu_custom_call" | custom-call | flops 24000000000 | tf_op jit(solution)/shard_map/input_back_high/pallas_call | solution.py:119
  421.1 11.5 %input_back_low.1 = (bf16[2,8,64,1024]{3,2,1,0:T(8,128)(2,1)}, f32[8,1024]{1,0:T(8,128)S(1)}, f32[16,1024]{1,0:T(8,128)}) custom-call(bf16[2,32,2048]{2,1,0:T(8,128)(2,1)S(1)} %get-tuple-element.154.refs_0_.refs_2_.refs_4_, bf16[128,1024]{1,0:T(8,128)(2,1)S(1)} %copy-done.15, s32[5]{0:T(128)S(1)} %copy-done.30, ...), custom_call_target="tpu_custom_call", output_to_operand_aliasing={{0}: (13, {})} | custom-call | flops 2000000000 | tf_op jit(solution)/shard_map/input_back_low/pallas_call | solution.py:119
  456.9 6.1 %all-to-all-done.3 = f32[32,1,768]{2,1,0:T(1,128)S(1)} async-done(((f32[32,1,768]{2,1,0:T(1,128)}), f32[32,1,768]{2,1,0:T(1,128)S(1)}, u32[]{:S(2)}, u32[]{:S(2)}) %all-to-all-start.3) | async-done | bytes 98336 | tf_op jit(solution)/shard_map/all_to_all | solution.py:1307
  472.0 7.3 %collective-permute-done.45 = bf16[1,32,2048]{2,1,0:T(8,128)(2,1)S(1)} collective-permute-done((bf16[1,32,2048]{2,1,0:T(8,128)(2,1)S(1)}, bf16[1,32,2048]{2,1,0:T(8,128)(2,1)S(1)}, u32[]{:S(2)}, u32[]{:S(2)}) %collective-permute-start.45) | collective-permute-done | bytes 131104 | tf_op jit(solution)/shard_map/ppermute | solution.py:696
  (347 shorter events, 179.1 us)
Async XLA Ops:
  7.2 80.9 %all-gather.5.cloned.1.call-start = ((), (), s32[]{:S(2)}) async-start(), calls=%async_computation.5 | async-start | bytes 1179648 | tf_op jit(solution)/shard_map/all_gather | solution.py:1053
  9.0 84.9 %all-gather.7.cloned.1.call-start = ((), (), s32[]{:S(2)}) async-start(), calls=%async_computation.6 | async-start | bytes 9437184 | tf_op jit(solution)/shard_map/all_gather | solution.py:1050
  36.2 136.2 %all-gather.11.cloned.1.call-start = ((), (), s32[]{:S(2)}) async-start(), calls=%async_computation.8 | async-start | bytes 11796480 | tf_op jit(solution)/shard_map/all_gather | solution.py:1052
  72.1 46.2 %all-to-all-start = ((f32[8,4,2,128]{3,1,2,0:T(4,128)}), f32[8,4,2,128]{3,1,2,0:T(4,128)S(1)}, u32[]{:S(2)}, u32[]{:S(2)}) async-start(f32[8,4,2,128]{3,1,2,0:T(4,128)} %broadcast_in_dim.113), calls=%async_computation | async-start | bytes 65536 | tf_op jit(solution)/shard_map/all_to_all | solution.py:681
  76.7 122.0 %all-gather.9.cloned.1.call-start = ((), (), s32[]{:S(2)}) async-start(), calls=%async_computation.7 | async-start | bytes 4718592 | tf_op jit(solution)/shard_map/all_gather | solution.py:1055
  88.1 46.5 %collective-permute-start.10 = (bf16[1024,512]{1,0:T(8,128)(2,1)}, bf16[1024,512]{1,0:T(8,128)(2,1)S(1)}, u32[]{:S(2)}, u32[]{:S(2)}) collective-permute-start(bf16[1024,512]{1,0:T(8,128)(2,1)} %hold_value.1.refs_0_.refs_5_), channel_id=1, source_target_pairs={{0,1},{1,0},{2,3},{3,2},{4,5},{5,4},{6,7},{7,6},{8,9},{9,8},{10,11... | collective-permute-start | bytes 3145736 | tf_op jit(solution)/shard_map/ppermute | solution.py:696
  88.4 48.7 %collective-permute-start.9 = (bf16[1024,512]{1,0:T(8,128)(2,1)}, bf16[1024,512]{1,0:T(8,128)(2,1)}, u32[]{:S(2)}, u32[]{:S(2)}) collective-permute-start(bf16[1024,512]{1,0:T(8,128)(2,1)} %hold_value.1.refs_0_.refs_5_), channel_id=1, source_target_pairs={{0,2},{1,3},{2,0},{3,1},{4,6},{5,7},{6,4},{7,5},{8,10},{9,11},{10,... | collective-permute-start | bytes 3145736 | tf_op jit(solution)/shard_map/ppermute | solution.py:696
  161.3 37.4 %collective-permute-start.15 = (bf16[1024,3072]{1,0:T(8,128)(2,1)}, bf16[1024,3072]{1,0:T(8,128)(2,1)}, u32[]{:S(2)}, u32[]{:S(2)}) collective-permute-start(bf16[1024,3072]{1,0:T(8,128)(2,1)} %hold_mix.1.refs_14_.refs_12_), channel_id=1, source_target_pairs={{0,4},{4,0},{8,12},{12,8},{16,20},{20,16},{24,28},{28,24},{1,5},{5... | collective-permute-start | bytes 18874376 | tf_op jit(solution)/shard_map/ppermute | solution.py:696
  171.9 26.9 %collective-permute-start.13 = (bf16[1024,2048]{1,0:T(8,128)(2,1)}, bf16[1024,2048]{1,0:T(8,128)(2,1)}, u32[]{:S(2)}, u32[]{:S(2)}) collective-permute-start(bf16[1024,2048]{1,0:T(8,128)(2,1)} %maximum_dynamic-update-slice_fusion.refs_2_.refs_17_.refs_19_), channel_id=1, source_target_pairs={{0,4},{4,0},{8,12},{12,8},{16,20},{20,16},{24,28},{28,24},{1,5},{5... | collective-permute-start | bytes 12582920 | tf_op jit(solution)/shard_map/ppermute | solution.py:696
  172.3 26.5 %collective-permute-start.14 = (bf16[1024,1024]{1,0:T(8,128)(2,1)}, bf16[1024,1024]{1,0:T(8,128)(2,1)}, u32[]{:S(2)}, u32[]{:S(2)}) collective-permute-start(bf16[1024,1024]{1,0:T(8,128)(2,1)} %copy-done.33), channel_id=1, source_target_pairs={{0,4},{4,0},{8,12},{12,8},{16,20},{20,16},{24,28},{28,24},{1,5},{5... | collective-permute-start | bytes 6291464 | tf_op jit(solution)/shard_map/ppermute | solution.py:696
  172.4 25.8 %collective-permute-start.16 = (bf16[1024,512]{1,0:T(8,128)(2,1)}, bf16[1024,512]{1,0:T(8,128)(2,1)}, u32[]{:S(2)}, u32[]{:S(2)}) collective-permute-start(bf16[1024,512]{1,0:T(8,128)(2,1)} %collective-permute-done.9.refs_0_.refs_6_), channel_id=1, source_target_pairs={{0,1},{1,0},{2,3},{3,2},{4,5},{5,4},{6,7},{7,6},{8,9},{9,8},{10,11... | collective-permute-start | bytes 3145736 | tf_op jit(solution)/shard_map/ppermute | solution.py:696
  260.3 54.2 %collective-permute-start.21 = (bf16[2,512,512]{2,1,0:T(8,128)(2,1)}, bf16[2,512,512]{2,1,0:T(8,128)(2,1)}, u32[]{:S(2)}, u32[]{:S(2)}) collective-permute-start(bf16[2,512,512]{2,1,0:T(8,128)(2,1)} %get-tuple-element.122), channel_id=1, source_target_pairs={{0,8},{4,12},{8,0},{12,4},{16,24},{20,28},{24,16},{28,20},{1,9},{5... | collective-permute-start | bytes 3145736 | tf_op jit(solution)/shard_map/ppermute | solution.py:696
  261.8 52.7 %collective-permute-start.22 = (bf16[2,512,512]{2,1,0:T(8,128)(2,1)}, bf16[2,512,512]{2,1,0:T(8,128)(2,1)}, u32[]{:S(2)}, u32[]{:S(2)}) collective-permute-start(bf16[2,512,512]{2,1,0:T(8,128)(2,1)} %get-tuple-element.124), channel_id=1, source_target_pairs={{0,16},{4,20},{8,24},{12,28},{16,0},{20,4},{24,8},{28,12},{1,17},{... | collective-permute-start | bytes 3145736 | tf_op jit(solution)/shard_map/ppermute | solution.py:696
  314.1 71.4 %reduce-scatter.2.cloned.1.call-start = ((), (), s32[]{:S(2)}) async-start(), calls=%async_computation.9 | async-start | bytes 1310720 | tf_op jit(solution)/shard_map/reduce_scatter | solution.py:990
  322.6 25.3 %collective-permute-start.24 = (bf16[1,512,512]{2,1,0:T(8,128)(2,1)}, bf16[1,512,512]{2,1,0:T(8,128)(2,1)}, u32[]{:S(2)}, u32[]{:S(2)}) collective-permute-start(bf16[1,512,512]{2,1,0:T(8,128)(2,1)} %get-tuple-element.130), channel_id=1, source_target_pairs={{0,16},{4,20},{8,24},{12,28},{16,0},{20,4},{24,8},{28,12},{1,17},{... | collective-permute-start | bytes 1572872 | tf_op jit(solution)/shard_map/ppermute | solution.py:696
  325.7 41.5 %collective-permute-start.26 = (bf16[2,128,2560]{2,1,0:T(8,128)(2,1)}, bf16[2,128,2560]{2,1,0:T(8,128)(2,1)}, u32[]{:S(2)}, u32[]{:S(2)}) collective-permute-start(bf16[2,128,2560]{2,1,0:T(8,128)(2,1)} %get-tuple-element.134), channel_id=1, source_target_pairs={{0,8},{4,12},{8,0},{12,4},{16,24},{20,28},{24,16},{28,20},{1,9},{5... | collective-permute-start | bytes 3932168 | tf_op jit(solution)/shard_map/ppermute | solution.py:696
  326.3 41.3 %collective-permute-start.27 = (bf16[2,128,2560]{2,1,0:T(8,128)(2,1)}, bf16[2,128,2560]{2,1,0:T(8,128)(2,1)}, u32[]{:S(2)}, u32[]{:S(2)}) collective-permute-start(bf16[2,128,2560]{2,1,0:T(8,128)(2,1)} %get-tuple-element.136), channel_id=1, source_target_pairs={{0,16},{4,20},{8,24},{12,28},{16,0},{20,4},{24,8},{28,12},{1,17},{... | collective-permute-start | bytes 3932168 | tf_op jit(solution)/shard_map/ppermute | solution.py:696
  347.8 42.2 %collective-permute-start.31 = (bf16[1024,2048]{1,0:T(8,128)(2,1)}, bf16[1024,2048]{1,0:T(8,128)(2,1)}, u32[]{:S(2)}, u32[]{:S(2)}) collective-permute-start(bf16[1024,2048]{1,0:T(8,128)(2,1)} %get-tuple-element.129.refs_1_.refs_3_.refs_16_.refs_4_), channel_id=1, source_target_pairs={{0,4},{4,0},{8,12},{12,8},{16,20},{20,16},{24,28},{28,24},{1,5},{5... | collective-permute-start | bytes 12582920 | tf_op jit(solution)/shard_map/ppermute | solution.py:696
  353.9 34.5 %collective-permute-start.30 = (f32[2,1024]{1,0:T(2,128)S(1)}, f32[2,1024]{1,0:T(2,128)S(1)}, u32[]{:S(2)}, u32[]{:S(2)}) collective-permute-start(f32[2,1024]{1,0:T(2,128)S(1)} %copy-done.75), channel_id=1, source_target_pairs={{4,0},{8,4},{12,8},{16,12},{20,16},{24,20},{28,24},{5,1},{9,5},{13... | collective-permute-start | bytes 24584 | tf_op jit(solution)/shard_map/ppermute | solution.py:676
  373.4 39.7 %collective-permute-start.32 = (bf16[1,128,2560]{2,1,0:T(8,128)(2,1)}, bf16[1,128,2560]{2,1,0:T(8,128)(2,1)}, u32[]{:S(2)}, u32[]{:S(2)}) collective-permute-start(bf16[1,128,2560]{2,1,0:T(8,128)(2,1)} %get-tuple-element.147), channel_id=1, source_target_pairs={{0,16},{4,20},{8,24},{12,28},{16,0},{20,4},{24,8},{28,12},{1,17},{... | collective-permute-start | bytes 1966088 | tf_op jit(solution)/shard_map/ppermute | solution.py:696
  377.6 37.3 %collective-permute-start.33 = (bf16[1,128,2560]{2,1,0:T(8,128)(2,1)S(1)}, bf16[1,128,2560]{2,1,0:T(8,128)(2,1)}, u32[]{:S(2)}, u32[]{:S(2)}) collective-permute-start(bf16[1,128,2560]{2,1,0:T(8,128)(2,1)S(1)} %get-tuple-element.149), channel_id=1, source_target_pairs={{0,8},{4,12},{8,0},{12,4},{16,24},{20,28},{24,16},{28,20},{1,9},{5... | collective-permute-start | bytes 1966088 | tf_op jit(solution)/shard_map/ppermute | solution.py:696
  385.1 33.8 %collective-permute-start.34 = (bf16[1,128,1024]{2,1,0:T(8,128)(2,1)}, bf16[1,128,1024]{2,1,0:T(8,128)(2,1)S(1)}, u32[]{:S(2)}, u32[]{:S(2)}) collective-permute-start(bf16[1,128,1024]{2,1,0:T(8,128)(2,1)} %get-tuple-element.151), channel_id=1, source_target_pairs={{0,16},{4,20},{8,24},{12,28},{16,0},{20,4},{24,8},{28,12},{1,17},{... | collective-permute-start | bytes 786440 | tf_op jit(solution)/shard_map/ppermute | solution.py:696
  388.4 30.6 %collective-permute-start.35 = (bf16[1,128,1024]{2,1,0:T(8,128)(2,1)S(1)}, bf16[1,128,1024]{2,1,0:T(8,128)(2,1)S(1)}, u32[]{:S(2)}, u32[]{:S(2)}) collective-permute-start(bf16[1,128,1024]{2,1,0:T(8,128)(2,1)S(1)} %get-tuple-element.153), channel_id=1, source_target_pairs={{0,8},{4,12},{8,0},{12,4},{16,24},{20,28},{24,16},{28,20},{1,9},{5... | collective-permute-start | bytes 786440 | tf_op jit(solution)/shard_map/ppermute | solution.py:696
  437.0 28.4 %collective-permute-start.42 = (bf16[1,32,5120]{2,1,0:T(8,128)(2,1)S(1)}, bf16[1,32,5120]{2,1,0:T(8,128)(2,1)S(1)}, u32[]{:S(2)}, u32[]{:S(2)}) collective-permute-start(bf16[1,32,5120]{2,1,0:T(8,128)(2,1)S(1)} %get-tuple-element.172), channel_id=1, source_target_pairs={{0,2},{1,3},{2,0},{3,1},{4,6},{5,7},{6,4},{7,5},{8,10},{9,11},{10,... | collective-permute-start | bytes 983048 | tf_op jit(solution)/shard_map/ppermute | solution.py:696
  (109 other events, 1307.1 us)
Sparse Core Ops, SparseCore 0:
  10.5 26.1 all-gather.4
  39.2 54.7 all-gather.6
  96.4 63.2 all-gather.10
  162.0 36.7 all-gather.8
  354.0 28.3 reduce-scatter.1

commit v3 on v2

--- a/solution.py
+++ b/solution.py
@@ -20,15 +20,15 @@
 EPS = 1e-05
 TINY = 1.2e-38
 COSTS = dict(
-    value=60, edge=14, grad_value=30, middle_back=60, grad_value_add_first=50, wkv_back=24, grad_value_merge=50,
-    grad_hidden_add_first=50, grad_early_add_first=50, input_back_high=24,
+    value=60, edge=14, grad_value=30, grad_hidden=40, grad_value_add_first=8, grad_hidden_add_first=100, wkv_back=24,
+    grad_value_merge=50, grad_hidden_merge=50, input_back_high=24,
 )
 F32 = jnp.float32
 BF16 = jnp.bfloat16
 MIB = 1024 * 1024
 VMEM = dict(
     mix_one=30, wkv=28, hidden=36, value=60, edge=60, grad_value=60, middle_back=60, wkv_back=60, input_back_high=44,
-    input_back_low=36,
+    input_back_low=60, grad_hidden_merge=60, grad_value_add_first=60, grad_hidden_add_first=60, grad_value_merge=60, grad_hidden=60,
 )
 
 
@@ -98,7 +98,7 @@
 
 
 def call(kernel, grid, in_specs, out_specs, out_shape, scratch, name, after=(), bits=None, weights=(), aliases=None):
-    if weights:
+    if bits is not None:
         kernel = grouped(kernel, [len(pieces) for pieces in weights])
         in_specs = [SMEM_SPEC] + [ANY_SPEC] * sum(len(pieces) for pieces in weights) + in_specs
     made = pl.pallas_call(
@@ -115,7 +115,7 @@
         input_output_aliases=aliases or {},
         name=name,
     )
-    head = (bits,) + tuple(piece for pieces in weights for piece in pieces) if weights else ()
+    head = (bits,) + tuple(piece for pieces in weights for piece in pieces) if bits is not None else ()
     return lambda *args: made(*after, *head, *args)
 
 
@@ -855,6 +855,11 @@
     return results[: counts[2]], results[counts[2] :]
 
 
+def grad_only(weights, ins, outs, scratch, copies, grad):
+    wait_load(copies)
+    grad()
+
+
 def tall_kernel(bits_ref, lhs_own, lhs_other, rhs_own, rhs_other, *outs):
     i = pl.program_id(0)
     total = dot_tn(lhs_own[...], rhs_own[...]) + dot_tn(lhs_other[...], rhs_other[...])
@@ -988,8 +993,8 @@
         (total,) = merge(bits, p_keep, p_got, q_keep, q_got, [(block, width)], name + "_merge", after, moves)
         yield total
         part = lax.psum_scatter(total, "rep", scatter_dimension=0, tiled=True)
-        yield part
-        yield part.astype(F32)
+        after = yield part
+        yield held(part, after, name + "_hold").astype(F32)
         return
     shape = (2, block // 4, width)
     send, keep = merge(bits, p_keep, p_got, q_keep, q_got, [shape] * 2, name + "_merge", after, moves)
@@ -1002,7 +1007,9 @@
     send, keep = add_split(bits, (1,), sums, name + "_add_low", after)
     got = flip(send, "rep", 2)
     yield keep
-    yield got
+    after = yield got
+    if after:
+        got = held(got, after, name + "_hold")
     yield (keep.astype(F32) + got.astype(F32))[0]
 
 
@@ -1216,11 +1223,22 @@
     if paired:
         dkf = held(dkf, (dvf_other, shift_two), "hold_dkf")
     dkf_other = other_core(dkf)
-    made = core_grad(bits, (kq, kq_other), (dvf, dvf_other), "grad_value", (shift_two,)) if paired else (shift_two,)
+    made = core_grad(bits, (kq, kq_other), (dvf, dvf_other), "grad_value", (shift_two, got_two)) if paired else (shift_two,)
     value_sum = reduced(made, ([(kq, None, 0, 1)], (dvf, None)), True, "grad_value")
 
-    got_two = held(got_two, (made[0],), "hold_row")
     every_spec = full((tok_count, 2 * micro, EMBED))
+    _, grads = fused(
+        grad_only, blocks, (vectors,), [vec_spec], [], [], [], "grad_hidden", (made[0],), (),
+        [(mix_two, mix_two_other, 0), (mix_two, mix_two_other, 8)],
+        [(wide, 0, (0,) * blocks), (narrow, FF // narrow, (1,) * blocks)], (dkf, dkf_other),
+    ) if paired else (None, made)
+    hidden_sum = reduced(
+        grads, ([(mix_two, None, 0, 4), (mix_two, None, 8, 1)], (dkf, None)), False, "grad_hidden",
+        [(at // (blocks // 2), at % (blocks // 2) * (wide + narrow), wide, at * wide) for at in range(blocks)]
+        + [(at // (blocks // 2), at % (blocks // 2) * (wide + narrow) + wide, narrow, FF + at * narrow)
+           for at in range(blocks)],
+    )
+    made = grads
     (dx1, datt, dwkv, vsum_two, firsts, back_totals), grads = fused(
         middle_back_kernel, blocks,
         (dkf, x1, x1, edge_two, shift_two, got_two, cp, vectors, k, v, r, wkv, saved),
@@ -1232,19 +1250,11 @@
         [state, pltpu.VMEM((2, ROWS, EMBED), F32), state, state, weight(EMBED, FF + EMBED),
          weight(EMBED, EMBED), pltpu.VMEM((ROWS, EMBED), F32), pltpu.VMEM((ROWS, EMBED), F32),
          pltpu.VMEM((4, GROUP, EMBED), F32), sems],
-        "middle_back", (made[0],), (fkr, att_w),
-        [(mix_two, mix_two_other, 0), (mix_two, mix_two_other, 8)],
-        [(FF // blocks, 0, (0,) * blocks), (EMBED // blocks, FF * blocks // EMBED, (1,) * blocks)], (dkf, dkf_other),
+        "middle_back", (made[0],), (fkr, att_w), (), (), (),
     )
-    hidden_sum = reduced(
-        grads, ([(mix_two, None, 0, 4), (mix_two, None, 8, 1)], (dkf, None)), False, "grad_hidden",
-        [(at // (blocks // 2), at % (blocks // 2) * (wide + narrow), wide, at * wide) for at in range(blocks)]
-        + [(at // (blocks // 2), at % (blocks // 2) * (wide + narrow) + wide, narrow, FF + at * narrow)
-           for at in range(blocks)],
-    )
-
     every_back = lax.all_to_all(back_totals, "tok", 0, 0, tiled=True)
     made = advance(value_sum, firsts)
+    made = advance(hidden_sum, made)
     datt_other = other_core(datt)
     right_down = pl.BlockSpec((ROWS, EMBED), lambda i: (blocks - 1 - i, 1))
     (dkv, vsum_wkv, shift_one, send_one), grads = fused(
@@ -1265,7 +1275,6 @@
     made = advance(value_sum, dkv)
     value_part = advance(value_sum)
     made = advance(hidden_sum, made)
-    made = advance(early_sum, made)
 
     half = blocks // 2
 
@@ -1291,27 +1300,27 @@
 
     (token_high, vsum_high, later_half), grads = input_back(blocks - 1, (made,), shift_one, ())
     late_sum = reduced(grads, ([(mix, None, 0, 1), (mix, None, 8, 1)], (dkv, None)), False, "grad_late")
-    made = advance(hidden_sum, vsum_high)
-    made = advance(early_sum, made)
-    (token_grad, vsum_one, _), _ = input_back(half - 1, (made, value_part), later_half, (token_high, vsum_high))
-
-    made = advance(late_sum, vsum_one)
+    made = advance(early_sum, vsum_high)
     made = advance(hidden_sum, made)
     hidden_got = advance(hidden_sum)
-    made = advance(late_sum, made)
+    (token_grad, vsum_one, _), _ = input_back(half - 1, (made, value_part), later_half, (token_high, vsum_high))
+
+    made = advance(late_sum, vsum_one)
     made = advance(early_sum, made)
-    early_got = advance(early_sum)
+    made = advance(late_sum, made, hidden_got)
     columns = vec_m.shape[1]
     grad_vec = held(jnp.concatenate([vsum_one, vsum_two, vsum_wkv], axis=0), (made,), "hold_vec")
     pieces = jnp.moveaxis(grad_vec.reshape(grad_vec.shape[0], tok_count * rep_count, columns), 1, 0)
     vec_terms = lax.all_to_all(pieces, ("tok", "rep"), 0, 0, tiled=True)
-    made = advance(late_sum, made, hidden_got, early_got)
+    made = advance(early_sum, made)
+    advance(early_sum)
+    made = advance(late_sum, made)
     advance(late_sum)
-    sum_fvalue = advance(value_sum)
     if not paired:
-        sum_fvalue = advance(value_sum)
-    sum_fkr = advance(hidden_sum)
-    sum_early = advance(early_sum)
+        advance(value_sum)
+    sum_fvalue = advance(value_sum, made)
+    sum_fkr = advance(hidden_sum, made)
+    sum_early = advance(early_sum, made)
     sum_late = advance(late_sum)
     sums = jnp.sum(held(vec_terms, (made,), "hold_terms"), axis=0)
     sum_vec = jnp.concatenate([sums[0:2], sums[8:10], sums[2:5], sums[10:12], sums[16:18]], axis=0)

time: 496 us -> 478 us (0.964)
  waiting for transfers between devices: 108 us -> 87.9 us
  Pallas kernels: 217 us -> 229 us
  local copies, waits for them, and re-layouts: 62 us -> 52.6 us
    ppermute x42, waiting for transfers between devices: 82.9 us -> 60.5 us  [flip(): lax.ppermute(block, axis, [(i, i ^ bit) for i in range(lax.axis_size(axis...]
    unnamed x164 -> x176, local copies, waits for them, and re-layouts: 52.1 us -> 45.2 us
    pallas_call x10 -> x11, Pallas kernels: 180 us -> 186 us  [call(): return lambda *args: made(*after, *head, *args)]
  transfers between devices with their start and end apart: 55 -> 55, of which waited for: 20 -> 18; matrix products, arithmetic and copies ran while one was open for 6% -> 5% of each run, Pallas kernels for 38% -> 42%
where the time goes in v3:
time: 478 us; the launch traced here: 469 us
  Pallas kernels  229 us (48%)
  waiting for transfers between devices  87.9 us (18%)
  starting transfers between devices  65 us (14%)
  local copies, waits for them, and re-layouts  52.6 us (11%)
  other arithmetic  19.2 us (4%)
  between operations  15.2 us (3%)
    pallas_call x11, Pallas kernels, call(): return lambda *args: made(*after, *head, *args)  186 us
    ppermute x42, waiting for transfers between devices, flip(): lax.ppermute(block, axis, [(i, i ^ bit) for i in range(lax.axis_size(axis...  60.5 us
    unnamed x176, local copies, waits for them, and re-layouts  45.2 us
    ppermute x42, starting transfers between devices, flip(): lax.ppermute(block, axis, [(i, i ^ bit) for i in range(lax.axis_size(axis...  44.3 us
    pallas_call x1, Pallas kernels, core_grad(): pl.pallas_call(ordered(tall_kernel, 1, len(after)), grid_spec=pltpu.Prefe...  15.1 us
    pallas_call x7, Pallas kernels, add_split(): pl.pallas_call(ordered(functools.partial(add_kernel, len(sums)), 1, len(a...  13.3 us
    ppermute x4, waiting for transfers between devices, neighbour(): lax.ppermute(block, axis, [(i, i + distance) for i in devices if i + dist...  11.1 us
  transfers between devices with their start and end apart: 55, of which 18 were waited for; matrix products, arithmetic and copies ran while one was open for 5% of the time, Pallas kernels for 42%

profile of v3, /device:TPU:0, one launch (start us, length us, event | category | flops | bytes accessed | tf_op | source)
XLA Modules:
  0.0 468.8 jit_solution(3670452035175922027)
XLA Ops:
  16.7 10.5 %collective-permute-done.refs_2_ = bf16[32,4096]{1,0:T(8,128)(2,1)S(1)} collective-permute-done((bf16[32,4096]{1,0:T(8,128)(2,1)S(1)}, bf16[32,4096]{1,0:T(8,128)(2,1)S(1)}, u32[]{:S(2)}, u32[]{:S(2)}) %collective-permute-start) | collective-permute-done | bytes 262176 | tf_op jit(solution)/shard_map/ppermute | solution.py:696
  27.9 6.7 %collective-permute-done.2.refs_4_ = bf16[32,4096]{1,0:T(8,128)(2,1)S(1)} collective-permute-done((bf16[32,4096]{1,0:T(8,128)(2,1)S(1)}, bf16[32,4096]{1,0:T(8,128)(2,1)S(1)}, u32[]{:S(2)}, u32[]{:S(2)}) %collective-permute-start.2) | collective-permute-done | bytes 262176 | tf_op jit(solution)/shard_map/ppermute | solution.py:696
  41.2 12.9 %collective-permute-done.3.refs_2_ = bf16[32,5120]{1,0:T(8,128)(2,1)S(1)} collective-permute-done((bf16[32,5120]{1,0:T(8,128)(2,1)S(1)}, bf16[32,5120]{1,0:T(8,128)(2,1)S(1)}, u32[]{:S(2)}, u32[]{:S(2)}) %collective-permute-start.3) | collective-permute-done | bytes 327712 | tf_op jit(solution)/shard_map/ppermute | solution.py:696
  54.7 8.1 %collective-permute-done.5.refs_4_ = bf16[32,5120]{1,0:T(8,128)(2,1)S(1)} collective-permute-done((bf16[32,5120]{1,0:T(8,128)(2,1)S(1)}, bf16[32,5120]{1,0:T(8,128)(2,1)S(1)}, u32[]{:S(2)}, u32[]{:S(2)}) %collective-permute-start.5) | collective-permute-done | bytes 327712 | tf_op jit(solution)/shard_map/ppermute | solution.py:696
  72.1 4.6 all-to-all-start
  80.9 5.8 %collective-permute-done.8.refs_5_ = bf16[128,512]{1,0:T(8,128)(2,1)S(1)} collective-permute-done((bf16[128,512]{1,0:T(8,128)(2,1)S(1)}, bf16[128,512]{1,0:T(8,128)(2,1)S(1)}, u32[]{:S(2)}, u32[]{:S(2)}) %collective-permute-start.8) | collective-permute-done | bytes 131104 | tf_op jit(solution)/shard_map/ppermute | solution.py:696
  88.6 5.3 %all-gather.7.cloned.1.call-done.refs_2_.refs_3_ = bf16[1024,4096]{1,0:T(8,128)(2,1)} async-done(((bf16[128,4096]{1,0:T(8,128)(2,1)}), bf16[1024,4096]{1,0:T(8,128)(2,1)}) %all-gather.7.cloned.1.call-update) | async-done | bytes 8388624 | tf_op jit(solution)/shard_map/all_gather | solution.py:1057
  96.8 14.9 %mix_one.1 = (bf16[1024,1024]{1,0:T(8,128)(2,1)S(1)}, bf16[1024,3072]{1,0:T(8,128)(2,1)S(1)}, bf16[1024,1024]{1,0:T(8,128)(2,1)S(1)}, bf16[1024,1024]{1,0:T(8,12...) custom-call(bf16[1024,512]{1,0:T(8,128)(2,1)S(1)} %copy-done.18, ...), custom_call_target="tpu_custom_call" | custom-call | flops 2000000000 | tf_op jit(solution)/shard_map/mix_one/pallas_call | solution.py:119
  123.1 5.5 %all-to-all-done.1 = f32[8,4,1024]{2,1,0:T(4,128)} async-done(((f32[8,4,1024]{2,1,0:T(4,128)}), f32[8,4,1024]{2,1,0:T(4,128)}, u32[]{:S(2)}, u32[]{:S(2)}) %all-to-all-start.1) | async-done | bytes 131104 | tf_op jit(solution)/shard_map/all_to_all | solution.py:681
  129.5 5.1 %collective-permute-done.10.refs_1_.refs_7_ = bf16[1024,512]{1,0:T(8,128)(2,1)S(1)} collective-permute-done((bf16[1024,512]{1,0:T(8,128)(2,1)}, bf16[1024,512]{1,0:T(8,128)(2,1)S(1)}, u32[]{:S(2)}, u32[]{:S(2)}) %collective-permute-start.10) | collective-permute-done | bytes 1048608 | tf_op jit(solution)/shard_map/ppermute | solution.py:696
  142.1 11.2 %wkv.1 = (bf16[1024,1024]{1,0:T(8,128)(2,1)S(1)}, bf16[1024,1024]{1,0:T(8,128)(2,1)S(1)}, f32[1024,1024]{1,0:T(8,128)S(1)}, bf16[1024,2048]{1,0:T(8,128)(2,1)S(1...) custom-call(bf16[1024,512]{1,0:T(8,128)(2,1)} %collective-permute-done.9.refs_0_.refs_6_, ...), custom_call_target="tpu_custom_call" | custom-call | flops 2000000000 | tf_op jit(solution)/shard_map/wkv/pallas_call | solution.py:119
  164.1 7.2 %collective-permute-done.12 = f32[2,1024]{1,0:T(2,128)S(1)} collective-permute-done((f32[2,1024]{1,0:T(2,128)S(1)}, f32[2,1024]{1,0:T(2,128)S(1)}, u32[]{:S(2)}, u32[]{:S(2)}) %collective-permute-start.12) | collective-permute-done | bytes 8224 | tf_op jit(solution)/shard_map/ppermute | solution.py:676
  174.7 15.1 %hidden.1 = (bf16[1024,4096]{1,0:T(8,128)(2,1)S(1)}, bf16[1024,1024]{1,0:T(8,128)(2,1)S(1)}) custom-call(s32[5]{0:T(128)S(1)} %stack.23.refs_0_.refs_1_.refs_2_.refs_3_, bf16[1024,5120]{1,0:T(8,128)(2,1)} %all-gather.11.cloned.1.call-done.refs_1_.refs_2_, bf16[1024,2048]{1,0:T(8,128)(2,1)S(1)} %copy-done.10), custom_call_target="tpu_custom_call" | custom-call | flops 2000000000 | tf_op jit(solution)/shard_map/hidden/pallas_call | solution.py:119
  199.1 29.9 %value.1 = (bf16[2,8,64,1024]{3,2,1,0:T(8,128)(2,1)}, bf16[1024,1024]{1,0:T(8,128)(2,1)}, bf16[1024,5120]{1,0:T(8,128)(2,1)}, bf16[1024,1024]{1,0:T(8,128)(2,1)}) custom-call(bf16[1024,2048]{1,0:T(8,128)(2,1)} %collective-permute-done.13.refs_0_.refs_4_.refs_6_, bf16[1024,1024]{1,0:T(8,128)(2,1)} %collective-permute-done.14.refs_1_.refs_13_, ...), custom_call_target="tpu_custom_call" | custom-call | flops 60000002048 | tf_op jit(solution)/shard_map/value/pallas_call | solution.py:119
  230.3 9.1 %edge.1 = (f32[16,1024]{1,0:T(8,128)}, f32[2,1024]{1,0:T(2,128)}) custom-call(s32[5]{0:T(128)} %copy-done.32, bf16[1024,5120]{1,0:T(8,128)(2,1)} %all-gather.11.cloned.1.call-done.refs_1_.refs_2_, s32[19]{0:T(128)} %pad_add_fusion.1.refs_2_.refs_3_, bf16[1024,5120]{1,0:T(8,128)(2,1)} %get-tuple-element.113.refs_3_.refs_0_, f32[11,1024]{1,0:T(8,128)} %refs_12_.1), custom_call_target="tpu_custom_call" | custom-call | flops 14000000000 | tf_op jit(solution)/shard_map/edge/pallas_call | solution.py:119
  245.8 15.1 %grad_value.1 = (bf16[2,512,512]{2,1,0:T(8,128)(2,1)}, bf16[2,512,512]{2,1,0:T(8,128)(2,1)}, bf16[2,512,512]{2,1,0:T(8,128)(2,1)}, bf16[2,512,512]{2,1,0:T(8,128)(2,1)}) custom-call(s32[5]{0:T(128)} %copy-done.32, f32[16,1024]{1,0:T(8,128)} %get-tuple-element.114.refs_1_.refs_2_.refs_8_, f32[2,1024]{1,0:T(2,128)} %copy-done.72, ...), custom_call_target="tpu_custom_call" | custom-call | flops 30000001024 | tf_op jit(solution)/shard_map/grad_value/pallas_call | solution.py:884
  263.0 20.2 %grad_hidden.1 = (bf16[2,128,2560]{2,1,0:T(8,128)(2,1)}, bf16[2,128,2560]{2,1,0:T(8,128)(2,1)}, bf16[2,128,2560]{2,1,0:T(8,128)(2,1)}, bf16[2,128,2560]{2,1,0:T(8,128)(2,1)}) custom-call(bf16[2,512,512]{2,1,0:T(8,128)(2,1)} %get-tuple-element.117.refs_0_.refs_2_.refs_6_, s32[5]{0:T(128)} %copy-done.32, f32[11,1024]{1,0:T(8,128)} %refs_12_.1, ...), custom_call_target="tpu_custom_call" | custom-call | flops 40000000000 | tf_op jit(solution)/shard_map/grad_hidden/pallas_call | solution.py:119
  285.3 32.5 %middle_back.1 = (f32[1024,1024]{1,0:T(8,128)}, bf16[1024,2048]{1,0:T(8,128)(2,1)}, bf16[1024,1024]{1,0:T(8,128)(2,1)}, f32[8,1024]{1,0:T(8,128)}, f32[32,1024]{1,0:T(8,128)}, /*index=5*/f32[8,4,1024]{2,1,0:T(4,128)}) custom-call(bf16[2,128,2560]{2,1,0:T(8,128)(2,1)} %get-tuple-element.118.refs_0_.refs_2_.refs_6_, s32[5]{0:T(128)} %copy-done.32, ...), custom_call_target="tpu_custom_call" | custom-call | flops 2000000000 | tf_op jit(solution)/shard_map/middle_back/pallas_call | solution.py:119
  321.3 4.1 grad_value_add_first.1
  328.9 4.5 grad_hidden_add_first.1
  336.3 20.4 %wkv_back.1 = (bf16[1024,2048]{1,0:T(8,128)(2,1)}, f32[8,1024]{1,0:T(8,128)}, f32[16,1024]{1,0:T(8,128)}, f32[2,1024]{1,0:T(2,128)}, bf16[2,128,1024]{2,1,0:T(8,...) custom-call(bf16[1,128,2560]{2,1,0:T(8,128)(2,1)} %get-tuple-element.130.refs, ...), custom_call_target="tpu_custom_call" | custom-call | flops 24000000000 | tf_op jit(solution)/shard_map/wkv_back/pallas_call | solution.py:119
  373.3 19.9 %input_back_high.1 = (bf16[2,8,64,1024]{3,2,1,0:T(8,128)(2,1)}, f32[8,1024]{1,0:T(8,128)S(1)}, f32[16,1024]{1,0:T(8,128)S(1)}, bf16[2,128,1024]{2,1,0:T(8,128)(2...) custom-call(bf16[2,32,5120]{2,1,0:T(8,128)(2,1)S(1)} %copy-done.45, ...), custom_call_target="tpu_custom_call" | custom-call | flops 24000000000 | tf_op jit(solution)/shard_map/input_back_high/pallas_call | solution.py:119
  404.0 13.2 %input_back_low.1 = (bf16[2,8,64,1024]{3,2,1,0:T(8,128)(2,1)}, f32[8,1024]{1,0:T(8,128)}, f32[16,1024]{1,0:T(8,128)}) custom-call(bf16[1,32,5120]{2,1,0:T(8,128)(2,1)} %copy-done.14, bf16[128,1024]{1,0:T(8,128)(2,1)} %reduce-scatter.2.cloned.1.call-done.refs_1_.refs_0_, s32[5]{0:T(128)} %copy-done.32, ...), custom_call_target="tpu_custom_call", output_to_operand_aliasing={{0}: (13, {})} | custom-call | flops 2000000000 | tf_op jit(solution)/shard_map/input_back_low/pallas_call | solution.py:119
  438.3 4.7 %all-to-all-done.3 = f32[32,1,768]{2,1,0:T(1,128)S(1)} async-done(((f32[32,1,768]{2,1,0:T(1,128)}), f32[32,1,768]{2,1,0:T(1,128)S(1)}, u32[]{:S(2)}, u32[]{:S(2)}) %all-to-all-start.3) | async-done | bytes 98336 | tf_op jit(solution)/shard_map/all_to_all | solution.py:1314
  (362 shorter events, 167.1 us)
Async XLA Ops:
  7.2 80.9 %all-gather.5.cloned.1.call-start = ((), (), s32[]{:S(2)}) async-start(), calls=%async_computation.5 | async-start | bytes 1179648 | tf_op jit(solution)/shard_map/all_gather | solution.py:1060
  9.0 84.9 %all-gather.7.cloned.1.call-start = ((), (), s32[]{:S(2)}) async-start(), calls=%async_computation.6 | async-start | bytes 9437184 | tf_op jit(solution)/shard_map/all_gather | solution.py:1057
  36.2 136.3 %all-gather.11.cloned.1.call-start = ((), (), s32[]{:S(2)}) async-start(), calls=%async_computation.8 | async-start | bytes 11796480 | tf_op jit(solution)/shard_map/all_gather | solution.py:1059
  72.1 46.2 %all-to-all-start = ((f32[8,4,2,128]{3,1,2,0:T(4,128)}), f32[8,4,2,128]{3,1,2,0:T(4,128)S(1)}, u32[]{:S(2)}, u32[]{:S(2)}) async-start(f32[8,4,2,128]{3,1,2,0:T(4,128)} %broadcast_in_dim.113), calls=%async_computation | async-start | bytes 65536 | tf_op jit(solution)/shard_map/all_to_all | solution.py:681
  76.7 122.0 %all-gather.9.cloned.1.call-start = ((), (), s32[]{:S(2)}) async-start(), calls=%async_computation.7 | async-start | bytes 4718592 | tf_op jit(solution)/shard_map/all_gather | solution.py:1062
  88.1 46.5 %collective-permute-start.10 = (bf16[1024,512]{1,0:T(8,128)(2,1)}, bf16[1024,512]{1,0:T(8,128)(2,1)S(1)}, u32[]{:S(2)}, u32[]{:S(2)}) collective-permute-start(bf16[1024,512]{1,0:T(8,128)(2,1)} %hold_value.1.refs_0_.refs_5_), channel_id=1, source_target_pairs={{0,1},{1,0},{2,3},{3,2},{4,5},{5,4},{6,7},{7,6},{8,9},{9,8},{10,11... | collective-permute-start | bytes 3145736 | tf_op jit(solution)/shard_map/ppermute | solution.py:696
  88.4 48.7 %collective-permute-start.9 = (bf16[1024,512]{1,0:T(8,128)(2,1)}, bf16[1024,512]{1,0:T(8,128)(2,1)}, u32[]{:S(2)}, u32[]{:S(2)}) collective-permute-start(bf16[1024,512]{1,0:T(8,128)(2,1)} %hold_value.1.refs_0_.refs_5_), channel_id=1, source_target_pairs={{0,2},{1,3},{2,0},{3,1},{4,6},{5,7},{6,4},{7,5},{8,10},{9,11},{10,... | collective-permute-start | bytes 3145736 | tf_op jit(solution)/shard_map/ppermute | solution.py:696
  161.4 37.3 %collective-permute-start.15 = (bf16[1024,3072]{1,0:T(8,128)(2,1)}, bf16[1024,3072]{1,0:T(8,128)(2,1)}, u32[]{:S(2)}, u32[]{:S(2)}) collective-permute-start(bf16[1024,3072]{1,0:T(8,128)(2,1)} %hold_mix.1.refs_14_.refs_12_), channel_id=1, source_target_pairs={{0,4},{4,0},{8,12},{12,8},{16,20},{20,16},{24,28},{28,24},{1,5},{5... | collective-permute-start | bytes 18874376 | tf_op jit(solution)/shard_map/ppermute | solution.py:696
  172.0 26.8 %collective-permute-start.13 = (bf16[1024,2048]{1,0:T(8,128)(2,1)}, bf16[1024,2048]{1,0:T(8,128)(2,1)}, u32[]{:S(2)}, u32[]{:S(2)}) collective-permute-start(bf16[1024,2048]{1,0:T(8,128)(2,1)} %maximum_dynamic-update-slice_fusion.refs_2_.refs_3_.refs_5_), channel_id=1, source_target_pairs={{0,4},{4,0},{8,12},{12,8},{16,20},{20,16},{24,28},{28,24},{1,5},{5... | collective-permute-start | bytes 12582920 | tf_op jit(solution)/shard_map/ppermute | solution.py:696
  172.4 26.4 %collective-permute-start.14 = (bf16[1024,1024]{1,0:T(8,128)(2,1)}, bf16[1024,1024]{1,0:T(8,128)(2,1)}, u32[]{:S(2)}, u32[]{:S(2)}) collective-permute-start(bf16[1024,1024]{1,0:T(8,128)(2,1)} %copy-done.37), channel_id=1, source_target_pairs={{0,4},{4,0},{8,12},{12,8},{16,20},{20,16},{24,28},{28,24},{1,5},{5... | collective-permute-start | bytes 6291464 | tf_op jit(solution)/shard_map/ppermute | solution.py:696
  172.5 25.6 %collective-permute-start.16 = (bf16[1024,512]{1,0:T(8,128)(2,1)}, bf16[1024,512]{1,0:T(8,128)(2,1)S(1)}, u32[]{:S(2)}, u32[]{:S(2)}) collective-permute-start(bf16[1024,512]{1,0:T(8,128)(2,1)} %collective-permute-done.9.refs_0_.refs_6_), channel_id=1, source_target_pairs={{0,1},{1,0},{2,3},{3,2},{4,5},{5,4},{6,7},{7,6},{8,9},{9,8},{10,11... | collective-permute-start | bytes 3145736 | tf_op jit(solution)/shard_map/ppermute | solution.py:696
  261.0 60.3 %collective-permute-start.21 = (bf16[2,512,512]{2,1,0:T(8,128)(2,1)}, bf16[2,512,512]{2,1,0:T(8,128)(2,1)}, u32[]{:S(2)}, u32[]{:S(2)}) collective-permute-start(bf16[2,512,512]{2,1,0:T(8,128)(2,1)} %get-tuple-element.123), channel_id=1, source_target_pairs={{0,8},{4,12},{8,0},{12,4},{16,24},{20,28},{24,16},{28,20},{1,9},{5... | collective-permute-start | bytes 3145736 | tf_op jit(solution)/shard_map/ppermute | solution.py:696
  262.1 59.1 %collective-permute-start.22 = (bf16[2,512,512]{2,1,0:T(8,128)(2,1)}, bf16[2,512,512]{2,1,0:T(8,128)(2,1)}, u32[]{:S(2)}, u32[]{:S(2)}) collective-permute-start(bf16[2,512,512]{2,1,0:T(8,128)(2,1)} %get-tuple-element.125), channel_id=1, source_target_pairs={{0,16},{4,20},{8,24},{12,28},{16,0},{20,4},{24,8},{28,12},{1,17},{... | collective-permute-start | bytes 3145736 | tf_op jit(solution)/shard_map/ppermute | solution.py:696
  283.3 45.6 %collective-permute-start.23 = (bf16[2,128,2560]{2,1,0:T(8,128)(2,1)}, bf16[2,128,2560]{2,1,0:T(8,128)(2,1)}, u32[]{:S(2)}, u32[]{:S(2)}) collective-permute-start(bf16[2,128,2560]{2,1,0:T(8,128)(2,1)} %get-tuple-element.127), channel_id=1, source_target_pairs={{0,8},{4,12},{8,0},{12,4},{16,24},{20,28},{24,16},{28,20},{1,9},{5... | collective-permute-start | bytes 3932168 | tf_op jit(solution)/shard_map/ppermute | solution.py:696
  284.3 44.5 %collective-permute-start.24 = (bf16[2,128,2560]{2,1,0:T(8,128)(2,1)}, bf16[2,128,2560]{2,1,0:T(8,128)(2,1)}, u32[]{:S(2)}, u32[]{:S(2)}) collective-permute-start(bf16[2,128,2560]{2,1,0:T(8,128)(2,1)} %get-tuple-element.129), channel_id=1, source_target_pairs={{0,16},{4,20},{8,24},{12,28},{16,0},{20,4},{24,8},{28,12},{1,17},{... | collective-permute-start | bytes 3932168 | tf_op jit(solution)/shard_map/ppermute | solution.py:696
  321.2 82.8 %reduce-scatter.2.cloned.1.call-start = ((), (), s32[]{:S(2)}) async-start(), calls=%async_computation.9 | async-start | bytes 1310720 | tf_op jit(solution)/shard_map/reduce_scatter | solution.py:995
  325.4 31.6 %collective-permute-start.26 = (bf16[1,512,512]{2,1,0:T(8,128)(2,1)}, bf16[1,512,512]{2,1,0:T(8,128)(2,1)}, u32[]{:S(2)}, u32[]{:S(2)}) collective-permute-start(bf16[1,512,512]{2,1,0:T(8,128)(2,1)} %get-tuple-element.135), channel_id=1, source_target_pairs={{0,16},{4,20},{8,24},{12,28},{16,0},{20,4},{24,8},{28,12},{1,17},{... | collective-permute-start | bytes 1572872 | tf_op jit(solution)/shard_map/ppermute | solution.py:696
  327.4 29.6 %collective-permute-start.27 = (bf16[1,512,512]{2,1,0:T(8,128)(2,1)}, bf16[1,512,512]{2,1,0:T(8,128)(2,1)}, u32[]{:S(2)}, u32[]{:S(2)}) collective-permute-start(bf16[1,512,512]{2,1,0:T(8,128)(2,1)} %get-tuple-element.137), channel_id=1, source_target_pairs={{0,8},{4,12},{8,0},{12,4},{16,24},{20,28},{24,16},{28,20},{1,9},{5... | collective-permute-start | bytes 1572872 | tf_op jit(solution)/shard_map/ppermute | solution.py:696
  333.3 31.0 %collective-permute-start.28 = (bf16[1,128,2560]{2,1,0:T(8,128)(2,1)}, bf16[1,128,2560]{2,1,0:T(8,128)(2,1)S(1)}, u32[]{:S(2)}, u32[]{:S(2)}) collective-permute-start(bf16[1,128,2560]{2,1,0:T(8,128)(2,1)} %get-tuple-element.138), channel_id=1, source_target_pairs={{0,16},{4,20},{8,24},{12,28},{16,0},{20,4},{24,8},{28,12},{1,17},{... | collective-permute-start | bytes 1966088 | tf_op jit(solution)/shard_map/ppermute | solution.py:696
  333.9 30.9 %collective-permute-start.29 = (bf16[1,128,2560]{2,1,0:T(8,128)(2,1)}, bf16[1,128,2560]{2,1,0:T(8,128)(2,1)}, u32[]{:S(2)}, u32[]{:S(2)}) collective-permute-start(bf16[1,128,2560]{2,1,0:T(8,128)(2,1)} %get-tuple-element.140), channel_id=1, source_target_pairs={{0,8},{4,12},{8,0},{12,4},{16,24},{20,28},{24,16},{28,20},{1,9},{5... | collective-permute-start | bytes 1966088 | tf_op jit(solution)/shard_map/ppermute | solution.py:696
  361.6 33.8 %collective-permute-start.32 = (bf16[2,128,1024]{2,1,0:T(8,128)(2,1)}, bf16[2,128,1024]{2,1,0:T(8,128)(2,1)}, u32[]{:S(2)}, u32[]{:S(2)}) collective-permute-start(bf16[2,128,1024]{2,1,0:T(8,128)(2,1)} %get-tuple-element.147), channel_id=1, source_target_pairs={{0,8},{4,12},{8,0},{12,4},{16,24},{20,28},{24,16},{28,20},{1,9},{5... | collective-permute-start | bytes 1572872 | tf_op jit(solution)/shard_map/ppermute | solution.py:696
  364.3 31.1 %collective-permute-start.33 = (bf16[2,128,1024]{2,1,0:T(8,128)(2,1)}, bf16[2,128,1024]{2,1,0:T(8,128)(2,1)}, u32[]{:S(2)}, u32[]{:S(2)}) collective-permute-start(bf16[2,128,1024]{2,1,0:T(8,128)(2,1)} %get-tuple-element.149), channel_id=1, source_target_pairs={{0,16},{4,20},{8,24},{12,28},{16,0},{20,4},{24,8},{28,12},{1,17},{... | collective-permute-start | bytes 1572872 | tf_op jit(solution)/shard_map/ppermute | solution.py:696
  368.7 31.5 %collective-permute-start.34 = (bf16[2,32,5120]{2,1,0:T(8,128)(2,1)}, bf16[2,32,5120]{2,1,0:T(8,128)(2,1)S(1)}, u32[]{:S(2)}, u32[]{:S(2)}) collective-permute-start(bf16[2,32,5120]{2,1,0:T(8,128)(2,1)} %get-tuple-element.151), channel_id=1, source_target_pairs={{0,1},{1,0},{2,3},{3,2},{4,5},{5,4},{6,7},{7,6},{8,9},{9,8},{10,11... | collective-permute-start | bytes 1966088 | tf_op jit(solution)/shard_map/ppermute | solution.py:696
  398.2 24.5 %collective-permute-start.37 = (bf16[1,128,1024]{2,1,0:T(8,128)(2,1)S(1)}, bf16[1,128,1024]{2,1,0:T(8,128)(2,1)S(1)}, u32[]{:S(2)}, u32[]{:S(2)}) collective-permute-start(bf16[1,128,1024]{2,1,0:T(8,128)(2,1)S(1)} %get-tuple-element.162), channel_id=1, source_target_pairs={{0,16},{4,20},{8,24},{12,28},{16,0},{20,4},{24,8},{28,12},{1,17},{... | collective-permute-start | bytes 786440 | tf_op jit(solution)/shard_map/ppermute | solution.py:696
  (115 other events, 1665.5 us)
Sparse Core Ops, SparseCore 0:
  10.5 26.1 all-gather.4
  39.2 54.7 all-gather.6
  96.4 63.2 all-gather.10
  162.0 36.7 all-gather.8
  360.4 39.9 reduce-scatter.1

commit v4 on v3

--- a/solution.py
+++ b/solution.py
@@ -515,6 +515,7 @@
     flag_ref, k_ref, v_ref, dwkv_ref, dr_ref, st_ref, vec_ref, every_ref, first_ref = ins
     out_ref, vsum_ref, edge_ref, send_ref = outs
     past_a, past_b, state_p, state_q, sums, w_ref, sems = scratch
+    make_grad = grad
     i = pl.program_id(0)
     count = pl.num_programs(0)
     loads = column_loads((pieces,), w_ref, sems, 0, 0, 3 * EMBED)
@@ -541,8 +542,6 @@
                 target[base + s : base + s + 1, :] = state
                 state = decay * state + first_ref[q * CHUNKS + s : q * CHUNKS + s + 1, :]
 
-    wait_load(copies)
-    grad()
     for cols in col_chunks():
         right = slice(EMBED + cols.start, EMBED + cols.stop)
         retain = jnp.exp(-jnp.exp(vec_ref[9:10, cols]))
@@ -583,6 +582,8 @@
         state_q[:, cols] = q
         sums[0, :, cols] = sum_decay
         sums[1, :, cols] = sum_bonus
+    wait_load(copies)
+    make_grad()
 
     @pl.when(i == count - 1)
     def _():
@@ -617,11 +618,12 @@
             take_rows(carry, later_ref, got_ref)
         sums[...] = jnp.zeros_like(sums)
 
-    wait_load(loads + list(copies))
+    wait_load(loads)
+    for at, grads in enumerate((grad_ref[:, part(0)], grad_ref[:, part(1)], dr_ref[...])):
+        back[at] = dot_nt(grads, w_ref[:, part(at)])
+    wait_load(list(copies))
     if grad is not None:
         grad()
-    for at, grads in enumerate((grad_ref[:, part(0)], grad_ref[:, part(1)], dr_ref[...])):
-        back[at] = dot_nt(grads, w_ref[:, part(at)])
     gain = vec_ref[0:1, :]
     offset = vec_ref[1:2, :]
     n, rstd = normalize(xp_ref[step_rows(STEPS - 1), :].astype(F32))
@@ -1312,14 +1314,14 @@
     grad_vec = held(jnp.concatenate([vsum_one, vsum_two, vsum_wkv], axis=0), (made,), "hold_vec")
     pieces = jnp.moveaxis(grad_vec.reshape(grad_vec.shape[0], tok_count * rep_count, columns), 1, 0)
     vec_terms = lax.all_to_all(pieces, ("tok", "rep"), 0, 0, tiled=True)
+    if not paired:
+        advance(value_sum)
+    sum_fvalue = advance(value_sum, made)
     made = advance(early_sum, made)
+    sum_fkr = advance(hidden_sum, made)
     advance(early_sum)
     made = advance(late_sum, made)
     advance(late_sum)
-    if not paired:
-        advance(value_sum)
-    sum_fvalue = advance(value_sum, made)
-    sum_fkr = advance(hidden_sum, made)
     sum_early = advance(early_sum, made)
     sum_late = advance(late_sum)
     sums = jnp.sum(held(vec_terms, (made,), "hold_terms"), axis=0)

time: 478 us -> 477 us (level)
    ppermute x42, waiting for transfers between devices: 60.5 us -> 66.9 us  [flip(): lax.ppermute(block, axis, [(i, i ^ bit) for i in range(lax.axis_size(axis...]
    unnamed x176 -> x184, local copies, waits for them, and re-layouts: 45.2 us -> 44.1 us
  transfers between devices with their start and end apart: 55 -> 55, of which waited for: 18 -> 19; matrix products, arithmetic and copies ran while one was open for 5% -> 5% of each run, Pallas kernels for 42% -> 42%
where the time goes in v4:
time: 477 us; the launch traced here: 468 us
  Pallas kernels  229 us (48%)
  waiting for transfers between devices  89.6 us (19%)
  starting transfers between devices  65.9 us (14%)
  local copies, waits for them, and re-layouts  50.6 us (11%)
  other arithmetic  18.4 us (4%)
  between operations  15.2 us (3%)
    pallas_call x11, Pallas kernels, call(): return lambda *args: made(*after, *head, *args)  186 us
    ppermute x42, waiting for transfers between devices, flip(): lax.ppermute(block, axis, [(i, i ^ bit) for i in range(lax.axis_size(axis...  66.9 us
    unnamed x184, local copies, waits for them, and re-layouts  44.1 us
    ppermute x42, starting transfers between devices, flip(): lax.ppermute(block, axis, [(i, i ^ bit) for i in range(lax.axis_size(axis...  43.9 us
    pallas_call x1, Pallas kernels, core_grad(): pl.pallas_call(ordered(tall_kernel, 1, len(after)), grid_spec=pltpu.Prefe...  15.1 us
    pallas_call x7, Pallas kernels, add_split(): pl.pallas_call(ordered(functools.partial(add_kernel, len(sums)), 1, len(a...  13.3 us
    ppermute x4, waiting for transfers between devices, neighbour(): lax.ppermute(block, axis, [(i, i + distance) for i in devices if i + dist...  11.1 us
  transfers between devices with their start and end apart: 55, of which 19 were waited for; matrix products, arithmetic and copies ran while one was open for 5% of the time, Pallas kernels for 42%

profile of v4, /device:TPU:0, one launch (start us, length us, event | category | flops | bytes accessed | tf_op | source)
XLA Modules:
  0.0 468.3 jit_solution(8841803540141254514)
XLA Ops:
  16.7 10.5 %collective-permute-done.refs_2_ = bf16[32,4096]{1,0:T(8,128)(2,1)S(1)} collective-permute-done((bf16[32,4096]{1,0:T(8,128)(2,1)S(1)}, bf16[32,4096]{1,0:T(8,128)(2,1)S(1)}, u32[]{:S(2)}, u32[]{:S(2)}) %collective-permute-start) | collective-permute-done | bytes 262176 | tf_op jit(solution)/shard_map/ppermute | solution.py:698
  27.9 6.7 %collective-permute-done.2.refs_4_ = bf16[32,4096]{1,0:T(8,128)(2,1)S(1)} collective-permute-done((bf16[32,4096]{1,0:T(8,128)(2,1)S(1)}, bf16[32,4096]{1,0:T(8,128)(2,1)S(1)}, u32[]{:S(2)}, u32[]{:S(2)}) %collective-permute-start.2) | collective-permute-done | bytes 262176 | tf_op jit(solution)/shard_map/ppermute | solution.py:698
  41.2 12.9 %collective-permute-done.3.refs_2_ = bf16[32,5120]{1,0:T(8,128)(2,1)S(1)} collective-permute-done((bf16[32,5120]{1,0:T(8,128)(2,1)S(1)}, bf16[32,5120]{1,0:T(8,128)(2,1)S(1)}, u32[]{:S(2)}, u32[]{:S(2)}) %collective-permute-start.3) | collective-permute-done | bytes 327712 | tf_op jit(solution)/shard_map/ppermute | solution.py:698
  54.7 8.1 %collective-permute-done.5.refs_4_ = bf16[32,5120]{1,0:T(8,128)(2,1)S(1)} collective-permute-done((bf16[32,5120]{1,0:T(8,128)(2,1)S(1)}, bf16[32,5120]{1,0:T(8,128)(2,1)S(1)}, u32[]{:S(2)}, u32[]{:S(2)}) %collective-permute-start.5) | collective-permute-done | bytes 327712 | tf_op jit(solution)/shard_map/ppermute | solution.py:698
  72.1 4.6 all-to-all-start
  80.9 5.8 %collective-permute-done.8.refs_5_ = bf16[128,512]{1,0:T(8,128)(2,1)S(1)} collective-permute-done((bf16[128,512]{1,0:T(8,128)(2,1)S(1)}, bf16[128,512]{1,0:T(8,128)(2,1)S(1)}, u32[]{:S(2)}, u32[]{:S(2)}) %collective-permute-start.8) | collective-permute-done | bytes 131104 | tf_op jit(solution)/shard_map/ppermute | solution.py:698
  88.6 5.3 %all-gather.7.cloned.1.call-done.refs_2_.refs_3_ = bf16[1024,4096]{1,0:T(8,128)(2,1)} async-done(((bf16[128,4096]{1,0:T(8,128)(2,1)}), bf16[1024,4096]{1,0:T(8,128)(2,1)}) %all-gather.7.cloned.1.call-update) | async-done | bytes 8388624 | tf_op jit(solution)/shard_map/all_gather | solution.py:1059
  96.8 14.9 %mix_one.1 = (bf16[1024,1024]{1,0:T(8,128)(2,1)S(1)}, bf16[1024,3072]{1,0:T(8,128)(2,1)S(1)}, bf16[1024,1024]{1,0:T(8,128)(2,1)S(1)}, bf16[1024,1024]{1,0:T(8,12...) custom-call(bf16[1024,512]{1,0:T(8,128)(2,1)S(1)} %copy-done.18, ...), custom_call_target="tpu_custom_call" | custom-call | flops 2000000000 | tf_op jit(solution)/shard_map/mix_one/pallas_call | solution.py:119
  123.1 5.5 %all-to-all-done.1 = f32[8,4,1024]{2,1,0:T(4,128)} async-done(((f32[8,4,1024]{2,1,0:T(4,128)}), f32[8,4,1024]{2,1,0:T(4,128)}, u32[]{:S(2)}, u32[]{:S(2)}) %all-to-all-start.1) | async-done | bytes 131104 | tf_op jit(solution)/shard_map/all_to_all | solution.py:683
  129.5 5.1 %collective-permute-done.10.refs_1_.refs_7_ = bf16[1024,512]{1,0:T(8,128)(2,1)S(1)} collective-permute-done((bf16[1024,512]{1,0:T(8,128)(2,1)}, bf16[1024,512]{1,0:T(8,128)(2,1)S(1)}, u32[]{:S(2)}, u32[]{:S(2)}) %collective-permute-start.10) | collective-permute-done | bytes 1048608 | tf_op jit(solution)/shard_map/ppermute | solution.py:698
  142.1 11.2 %wkv.1 = (bf16[1024,1024]{1,0:T(8,128)(2,1)S(1)}, bf16[1024,1024]{1,0:T(8,128)(2,1)S(1)}, f32[1024,1024]{1,0:T(8,128)S(1)}, bf16[1024,2048]{1,0:T(8,128)(2,1)S(1...) custom-call(bf16[1024,512]{1,0:T(8,128)(2,1)} %collective-permute-done.9.refs_0_.refs_6_, ...), custom_call_target="tpu_custom_call" | custom-call | flops 2000000000 | tf_op jit(solution)/shard_map/wkv/pallas_call | solution.py:119
  164.0 7.2 %collective-permute-done.12 = f32[2,1024]{1,0:T(2,128)S(1)} collective-permute-done((f32[2,1024]{1,0:T(2,128)S(1)}, f32[2,1024]{1,0:T(2,128)S(1)}, u32[]{:S(2)}, u32[]{:S(2)}) %collective-permute-start.12) | collective-permute-done | bytes 8224 | tf_op jit(solution)/shard_map/ppermute | solution.py:678
  174.7 15.1 %hidden.1 = (bf16[1024,4096]{1,0:T(8,128)(2,1)S(1)}, bf16[1024,1024]{1,0:T(8,128)(2,1)S(1)}) custom-call(s32[5]{0:T(128)S(1)} %stack.23.refs_0_.refs_1_.refs_2_.refs_3_, bf16[1024,5120]{1,0:T(8,128)(2,1)} %all-gather.11.cloned.1.call-done.refs_1_.refs_2_, bf16[1024,2048]{1,0:T(8,128)(2,1)S(1)} %copy-done.10), custom_call_target="tpu_custom_call" | custom-call | flops 2000000000 | tf_op jit(solution)/shard_map/hidden/pallas_call | solution.py:119
  199.1 29.9 %value.1 = (bf16[2,8,64,1024]{3,2,1,0:T(8,128)(2,1)}, bf16[1024,1024]{1,0:T(8,128)(2,1)}, bf16[1024,5120]{1,0:T(8,128)(2,1)}, bf16[1024,1024]{1,0:T(8,128)(2,1)}) custom-call(bf16[1024,2048]{1,0:T(8,128)(2,1)} %collective-permute-done.13.refs_0_.refs_4_.refs_6_, bf16[1024,1024]{1,0:T(8,128)(2,1)} %collective-permute-done.14.refs_1_.refs_13_, ...), custom_call_target="tpu_custom_call" | custom-call | flops 60000002048 | tf_op jit(solution)/shard_map/value/pallas_call | solution.py:119
  230.2 9.1 %edge.1 = (f32[16,1024]{1,0:T(8,128)}, f32[2,1024]{1,0:T(2,128)}) custom-call(s32[5]{0:T(128)} %copy-done.34, bf16[1024,5120]{1,0:T(8,128)(2,1)} %all-gather.11.cloned.1.call-done.refs_1_.refs_2_, s32[19]{0:T(128)} %pad_add_fusion.1.refs_2_.refs_3_, bf16[1024,5120]{1,0:T(8,128)(2,1)} %get-tuple-element.113.refs_3_.refs_0_, f32[11,1024]{1,0:T(8,128)} %refs_12_.1), custom_call_target="tpu_custom_call" | custom-call | flops 14000000000 | tf_op jit(solution)/shard_map/edge/pallas_call | solution.py:119
  245.8 15.1 %grad_value.1 = (bf16[2,512,512]{2,1,0:T(8,128)(2,1)}, bf16[2,512,512]{2,1,0:T(8,128)(2,1)}, bf16[2,512,512]{2,1,0:T(8,128)(2,1)}, bf16[2,512,512]{2,1,0:T(8,128)(2,1)}) custom-call(s32[5]{0:T(128)} %copy-done.34, f32[16,1024]{1,0:T(8,128)} %get-tuple-element.114.refs_1_.refs_2_.refs_8_, f32[2,1024]{1,0:T(2,128)} %copy-done.76, ...), custom_call_target="tpu_custom_call" | custom-call | flops 30000001024 | tf_op jit(solution)/shard_map/grad_value/pallas_call | solution.py:886
  263.0 20.1 %grad_hidden.1 = (bf16[2,128,2560]{2,1,0:T(8,128)(2,1)}, bf16[2,128,2560]{2,1,0:T(8,128)(2,1)}, bf16[2,128,2560]{2,1,0:T(8,128)(2,1)}, bf16[2,128,2560]{2,1,0:T(8,128)(2,1)}) custom-call(bf16[2,512,512]{2,1,0:T(8,128)(2,1)} %get-tuple-element.117.refs_0_.refs_2_.refs_6_, s32[5]{0:T(128)} %copy-done.34, f32[11,1024]{1,0:T(8,128)} %refs_12_.1, ...), custom_call_target="tpu_custom_call" | custom-call | flops 40000000000 | tf_op jit(solution)/shard_map/grad_hidden/pallas_call | solution.py:119
  285.2 32.5 %middle_back.1 = (f32[1024,1024]{1,0:T(8,128)}, bf16[1024,2048]{1,0:T(8,128)(2,1)}, bf16[1024,1024]{1,0:T(8,128)(2,1)}, f32[8,1024]{1,0:T(8,128)}, f32[32,1024]{1,0:T(8,128)}, /*index=5*/f32[8,4,1024]{2,1,0:T(4,128)}) custom-call(bf16[2,128,2560]{2,1,0:T(8,128)(2,1)} %get-tuple-element.118.refs_0_.refs_2_.refs_6_, s32[5]{0:T(128)} %copy-done.34, ...), custom_call_target="tpu_custom_call" | custom-call | flops 2000000000 | tf_op jit(solution)/shard_map/middle_back/pallas_call | solution.py:119
  328.8 4.4 grad_hidden_add_first.1
  336.3 19.6 %wkv_back.1 = (bf16[1024,2048]{1,0:T(8,128)(2,1)}, f32[8,1024]{1,0:T(8,128)}, f32[16,1024]{1,0:T(8,128)}, f32[2,1024]{1,0:T(2,128)}, bf16[2,128,1024]{2,1,0:T(8,...) custom-call(bf16[1,128,2560]{2,1,0:T(8,128)(2,1)} %get-tuple-element.130.refs, ...), custom_call_target="tpu_custom_call" | custom-call | flops 24000000000 | tf_op jit(solution)/shard_map/wkv_back/pallas_call | solution.py:119
  372.4 20.3 %input_back_high.1 = (bf16[2,8,64,1024]{3,2,1,0:T(8,128)(2,1)}, f32[8,1024]{1,0:T(8,128)S(1)}, f32[16,1024]{1,0:T(8,128)S(1)}, bf16[2,128,1024]{2,1,0:T(8,128)(2...) custom-call(bf16[2,32,5120]{2,1,0:T(8,128)(2,1)S(1)} %copy-done.47, ...), custom_call_target="tpu_custom_call" | custom-call | flops 24000000000 | tf_op jit(solution)/shard_map/input_back_high/pallas_call | solution.py:119
  403.0 13.3 %input_back_low.1 = (bf16[2,8,64,1024]{3,2,1,0:T(8,128)(2,1)}, f32[8,1024]{1,0:T(8,128)}, f32[16,1024]{1,0:T(8,128)}) custom-call(bf16[1,32,5120]{2,1,0:T(8,128)(2,1)} %copy-done.14, bf16[128,1024]{1,0:T(8,128)(2,1)} %reduce-scatter.2.cloned.1.call-done.refs_1_.refs_0_, s32[5]{0:T(128)} %copy-done.34, ...), custom_call_target="tpu_custom_call", output_to_operand_aliasing={{0}: (13, {})} | custom-call | flops 2000000000 | tf_op jit(solution)/shard_map/input_back_low/pallas_call | solution.py:119
  427.7 4.9 %collective-permute-done.42.refs_3_.refs_5_ = bf16[2,32,2048]{2,1,0:T(8,128)(2,1)S(1)} collective-permute-done((bf16[2,32,2048]{2,1,0:T(8,128)(2,1)S(1)}, bf16[2,32,2048]{2,1,0:T(8,128)(2,1)S(1)}, u32[]{:S(2)}, u32[]{:S(2)}) %collective-permute-start.42) | collective-permute-done | bytes 262176 | tf_op jit(solution)/shard_map/ppermute | solution.py:698
  435.2 4.2 all-to-all-start.3
  (370 shorter events, 166.6 us)
Async XLA Ops:
  7.2 80.9 %all-gather.5.cloned.1.call-start = ((), (), s32[]{:S(2)}) async-start(), calls=%async_computation.5 | async-start | bytes 1179648 | tf_op jit(solution)/shard_map/all_gather | solution.py:1062
  9.0 84.9 %all-gather.7.cloned.1.call-start = ((), (), s32[]{:S(2)}) async-start(), calls=%async_computation.6 | async-start | bytes 9437184 | tf_op jit(solution)/shard_map/all_gather | solution.py:1059
  36.2 136.3 %all-gather.11.cloned.1.call-start = ((), (), s32[]{:S(2)}) async-start(), calls=%async_computation.8 | async-start | bytes 11796480 | tf_op jit(solution)/shard_map/all_gather | solution.py:1061
  72.1 46.2 %all-to-all-start = ((f32[8,4,2,128]{3,1,2,0:T(4,128)}), f32[8,4,2,128]{3,1,2,0:T(4,128)S(1)}, u32[]{:S(2)}, u32[]{:S(2)}) async-start(f32[8,4,2,128]{3,1,2,0:T(4,128)} %broadcast_in_dim.113), calls=%async_computation | async-start | bytes 65536 | tf_op jit(solution)/shard_map/all_to_all | solution.py:683
  76.7 122.0 %all-gather.9.cloned.1.call-start = ((), (), s32[]{:S(2)}) async-start(), calls=%async_computation.7 | async-start | bytes 4718592 | tf_op jit(solution)/shard_map/all_gather | solution.py:1064
  88.1 46.5 %collective-permute-start.10 = (bf16[1024,512]{1,0:T(8,128)(2,1)}, bf16[1024,512]{1,0:T(8,128)(2,1)S(1)}, u32[]{:S(2)}, u32[]{:S(2)}) collective-permute-start(bf16[1024,512]{1,0:T(8,128)(2,1)} %hold_value.1.refs_0_.refs_5_), channel_id=1, source_target_pairs={{0,1},{1,0},{2,3},{3,2},{4,5},{5,4},{6,7},{7,6},{8,9},{9,8},{10,11... | collective-permute-start | bytes 3145736 | tf_op jit(solution)/shard_map/ppermute | solution.py:698
  88.4 48.7 %collective-permute-start.9 = (bf16[1024,512]{1,0:T(8,128)(2,1)}, bf16[1024,512]{1,0:T(8,128)(2,1)}, u32[]{:S(2)}, u32[]{:S(2)}) collective-permute-start(bf16[1024,512]{1,0:T(8,128)(2,1)} %hold_value.1.refs_0_.refs_5_), channel_id=1, source_target_pairs={{0,2},{1,3},{2,0},{3,1},{4,6},{5,7},{6,4},{7,5},{8,10},{9,11},{10,... | collective-permute-start | bytes 3145736 | tf_op jit(solution)/shard_map/ppermute | solution.py:698
  161.4 37.4 %collective-permute-start.15 = (bf16[1024,3072]{1,0:T(8,128)(2,1)}, bf16[1024,3072]{1,0:T(8,128)(2,1)}, u32[]{:S(2)}, u32[]{:S(2)}) collective-permute-start(bf16[1024,3072]{1,0:T(8,128)(2,1)} %hold_mix.1.refs_14_.refs_12_), channel_id=1, source_target_pairs={{0,4},{4,0},{8,12},{12,8},{16,20},{20,16},{24,28},{28,24},{1,5},{5... | collective-permute-start | bytes 18874376 | tf_op jit(solution)/shard_map/ppermute | solution.py:698
  172.0 26.8 %collective-permute-start.13 = (bf16[1024,2048]{1,0:T(8,128)(2,1)}, bf16[1024,2048]{1,0:T(8,128)(2,1)}, u32[]{:S(2)}, u32[]{:S(2)}) collective-permute-start(bf16[1024,2048]{1,0:T(8,128)(2,1)} %maximum_dynamic-update-slice_fusion.refs_2_.refs_3_.refs_5_), channel_id=1, source_target_pairs={{0,4},{4,0},{8,12},{12,8},{16,20},{20,16},{24,28},{28,24},{1,5},{5... | collective-permute-start | bytes 12582920 | tf_op jit(solution)/shard_map/ppermute | solution.py:698
  172.4 26.4 %collective-permute-start.14 = (bf16[1024,1024]{1,0:T(8,128)(2,1)}, bf16[1024,1024]{1,0:T(8,128)(2,1)}, u32[]{:S(2)}, u32[]{:S(2)}) collective-permute-start(bf16[1024,1024]{1,0:T(8,128)(2,1)} %copy-done.39), channel_id=1, source_target_pairs={{0,4},{4,0},{8,12},{12,8},{16,20},{20,16},{24,28},{28,24},{1,5},{5... | collective-permute-start | bytes 6291464 | tf_op jit(solution)/shard_map/ppermute | solution.py:698
  172.5 25.6 %collective-permute-start.16 = (bf16[1024,512]{1,0:T(8,128)(2,1)}, bf16[1024,512]{1,0:T(8,128)(2,1)S(1)}, u32[]{:S(2)}, u32[]{:S(2)}) collective-permute-start(bf16[1024,512]{1,0:T(8,128)(2,1)} %collective-permute-done.9.refs_0_.refs_6_), channel_id=1, source_target_pairs={{0,1},{1,0},{2,3},{3,2},{4,5},{5,4},{6,7},{7,6},{8,9},{9,8},{10,11... | collective-permute-start | bytes 3145736 | tf_op jit(solution)/shard_map/ppermute | solution.py:698
  261.0 60.2 %collective-permute-start.21 = (bf16[2,512,512]{2,1,0:T(8,128)(2,1)}, bf16[2,512,512]{2,1,0:T(8,128)(2,1)}, u32[]{:S(2)}, u32[]{:S(2)}) collective-permute-start(bf16[2,512,512]{2,1,0:T(8,128)(2,1)} %get-tuple-element.123), channel_id=1, source_target_pairs={{0,8},{4,12},{8,0},{12,4},{16,24},{20,28},{24,16},{28,20},{1,9},{5... | collective-permute-start | bytes 3145736 | tf_op jit(solution)/shard_map/ppermute | solution.py:698
  262.1 59.1 %collective-permute-start.22 = (bf16[2,512,512]{2,1,0:T(8,128)(2,1)}, bf16[2,512,512]{2,1,0:T(8,128)(2,1)}, u32[]{:S(2)}, u32[]{:S(2)}) collective-permute-start(bf16[2,512,512]{2,1,0:T(8,128)(2,1)} %get-tuple-element.125), channel_id=1, source_target_pairs={{0,16},{4,20},{8,24},{12,28},{16,0},{20,4},{24,8},{28,12},{1,17},{... | collective-permute-start | bytes 3145736 | tf_op jit(solution)/shard_map/ppermute | solution.py:698
  283.1 45.6 %collective-permute-start.23 = (bf16[2,128,2560]{2,1,0:T(8,128)(2,1)}, bf16[2,128,2560]{2,1,0:T(8,128)(2,1)}, u32[]{:S(2)}, u32[]{:S(2)}) collective-permute-start(bf16[2,128,2560]{2,1,0:T(8,128)(2,1)} %get-tuple-element.127), channel_id=1, source_target_pairs={{0,8},{4,12},{8,0},{12,4},{16,24},{20,28},{24,16},{28,20},{1,9},{5... | collective-permute-start | bytes 3932168 | tf_op jit(solution)/shard_map/ppermute | solution.py:698
  284.2 44.5 %collective-permute-start.24 = (bf16[2,128,2560]{2,1,0:T(8,128)(2,1)}, bf16[2,128,2560]{2,1,0:T(8,128)(2,1)}, u32[]{:S(2)}, u32[]{:S(2)}) collective-permute-start(bf16[2,128,2560]{2,1,0:T(8,128)(2,1)} %get-tuple-element.129), channel_id=1, source_target_pairs={{0,16},{4,20},{8,24},{12,28},{16,0},{20,4},{24,8},{28,12},{1,17},{... | collective-permute-start | bytes 3932168 | tf_op jit(solution)/shard_map/ppermute | solution.py:698
  321.1 81.8 %reduce-scatter.2.cloned.1.call-start = ((), (), s32[]{:S(2)}) async-start(), calls=%async_computation.9 | async-start | bytes 1310720 | tf_op jit(solution)/shard_map/reduce_scatter | solution.py:997
  325.3 30.8 %collective-permute-start.26 = (bf16[1,512,512]{2,1,0:T(8,128)(2,1)}, bf16[1,512,512]{2,1,0:T(8,128)(2,1)}, u32[]{:S(2)}, u32[]{:S(2)}) collective-permute-start(bf16[1,512,512]{2,1,0:T(8,128)(2,1)} %get-tuple-element.135), channel_id=1, source_target_pairs={{0,16},{4,20},{8,24},{12,28},{16,0},{20,4},{24,8},{28,12},{1,17},{... | collective-permute-start | bytes 1572872 | tf_op jit(solution)/shard_map/ppermute | solution.py:698
  327.3 28.8 %collective-permute-start.27 = (bf16[1,512,512]{2,1,0:T(8,128)(2,1)}, bf16[1,512,512]{2,1,0:T(8,128)(2,1)}, u32[]{:S(2)}, u32[]{:S(2)}) collective-permute-start(bf16[1,512,512]{2,1,0:T(8,128)(2,1)} %get-tuple-element.137), channel_id=1, source_target_pairs={{0,8},{4,12},{8,0},{12,4},{16,24},{20,28},{24,16},{28,20},{1,9},{5... | collective-permute-start | bytes 1572872 | tf_op jit(solution)/shard_map/ppermute | solution.py:698
  333.2 30.2 %collective-permute-start.28 = (bf16[1,128,2560]{2,1,0:T(8,128)(2,1)}, bf16[1,128,2560]{2,1,0:T(8,128)(2,1)S(1)}, u32[]{:S(2)}, u32[]{:S(2)}) collective-permute-start(bf16[1,128,2560]{2,1,0:T(8,128)(2,1)} %get-tuple-element.138), channel_id=1, source_target_pairs={{0,16},{4,20},{8,24},{12,28},{16,0},{20,4},{24,8},{28,12},{1,17},{... | collective-permute-start | bytes 1966088 | tf_op jit(solution)/shard_map/ppermute | solution.py:698
  333.8 30.1 %collective-permute-start.29 = (bf16[1,128,2560]{2,1,0:T(8,128)(2,1)}, bf16[1,128,2560]{2,1,0:T(8,128)(2,1)}, u32[]{:S(2)}, u32[]{:S(2)}) collective-permute-start(bf16[1,128,2560]{2,1,0:T(8,128)(2,1)} %get-tuple-element.140), channel_id=1, source_target_pairs={{0,8},{4,12},{8,0},{12,4},{16,24},{20,28},{24,16},{28,20},{1,9},{5... | collective-permute-start | bytes 1966088 | tf_op jit(solution)/shard_map/ppermute | solution.py:698
  360.7 34.3 %collective-permute-start.32 = (bf16[2,128,1024]{2,1,0:T(8,128)(2,1)}, bf16[2,128,1024]{2,1,0:T(8,128)(2,1)}, u32[]{:S(2)}, u32[]{:S(2)}) collective-permute-start(bf16[2,128,1024]{2,1,0:T(8,128)(2,1)} %get-tuple-element.147), channel_id=1, source_target_pairs={{0,8},{4,12},{8,0},{12,4},{16,24},{20,28},{24,16},{28,20},{1,9},{5... | collective-permute-start | bytes 1572872 | tf_op jit(solution)/shard_map/ppermute | solution.py:698
  363.4 31.6 %collective-permute-start.33 = (bf16[2,128,1024]{2,1,0:T(8,128)(2,1)}, bf16[2,128,1024]{2,1,0:T(8,128)(2,1)}, u32[]{:S(2)}, u32[]{:S(2)}) collective-permute-start(bf16[2,128,1024]{2,1,0:T(8,128)(2,1)} %get-tuple-element.149), channel_id=1, source_target_pairs={{0,16},{4,20},{8,24},{12,28},{16,0},{20,4},{24,8},{28,12},{1,17},{... | collective-permute-start | bytes 1572872 | tf_op jit(solution)/shard_map/ppermute | solution.py:698
  367.8 31.3 %collective-permute-start.34 = (bf16[2,32,5120]{2,1,0:T(8,128)(2,1)}, bf16[2,32,5120]{2,1,0:T(8,128)(2,1)S(1)}, u32[]{:S(2)}, u32[]{:S(2)}) collective-permute-start(bf16[2,32,5120]{2,1,0:T(8,128)(2,1)} %get-tuple-element.151), channel_id=1, source_target_pairs={{0,1},{1,0},{2,3},{3,2},{4,5},{5,4},{6,7},{7,6},{8,9},{9,8},{10,11... | collective-permute-start | bytes 1966088 | tf_op jit(solution)/shard_map/ppermute | solution.py:698
  397.0 23.8 %collective-permute-start.37 = (bf16[1,128,1024]{2,1,0:T(8,128)(2,1)S(1)}, bf16[1,128,1024]{2,1,0:T(8,128)(2,1)S(1)}, u32[]{:S(2)}, u32[]{:S(2)}) collective-permute-start(bf16[1,128,1024]{2,1,0:T(8,128)(2,1)S(1)} %get-tuple-element.162), channel_id=1, source_target_pairs={{0,16},{4,20},{8,24},{12,28},{16,0},{20,4},{24,8},{28,12},{1,17},{... | collective-permute-start | bytes 786440 | tf_op jit(solution)/shard_map/ppermute | solution.py:698
  (119 other events, 1707.1 us)
Sparse Core Ops, SparseCore 0:
  10.5 26.1 all-gather.4
  39.2 54.7 all-gather.6
  96.4 63.2 all-gather.10
  162.0 36.7 all-gather.8
  359.5 39.9 reduce-scatter.1
